TPU v7x, 128 devices: a whole 4x4x4 slice. The times are simulated.
128 devices in a mesh: rack: 8 (over x_lo, y), dp: 16 (over z, x_hi, core).
Axes of the slice: x: 4 (x_hi: 2, x_lo: 2; x = x_hi * 2 + x_lo), y: 4, z: 4, core: 2. Of those that a mesh axis runs over, the one named last changes fastest.
Arguments:
- grad_part: bfloat16 [8, 16, 512, 8192], P('rack', 'dp'), may hold values from -6 to 6
- weight: float32 [8, 512, 8192], P('rack', 'dp'), may hold values from -6 to 6
- moment_one: float32 [8, 512, 8192], P('rack', 'dp'), may hold values from -4 to 4
- moment_two: float32 [8, 512, 8192], P('rack', 'dp'), may hold values from 0.01 to 1
- code: float32 [4, 8], replicated, may hold values from 0.125 to 8, as said below
- owner: int32 [8, 16], P('rack'), may hold values from 0 to 15, each once within a row
- holder: int32 [16, 8], P('dp'), may hold values from 0 to 7, each once within a row
Outputs:
- weight_new: float32 [8, 512, 8192], P('rack', 'dp')
- moment_one_new: float32 [8, 512, 8192], P('rack', 'dp')
- moment_two_new: float32 [8, 512, 8192], P('rack', 'dp')
- parity: float32 [4, 3, 512, 8192], P(None, None, 'dp', 'rack')
Inputs may be any that keep to these rules, and one draw needn't show every extreme that they name: code[j, r] = t_r ** j for distinct positive nodes t_r.
All inputs are finite; a program needn't handle non-finite values.
Results may differ from a plain program's by a relative error of at most 0.0003.
Values sent between devices are 32-bit elements; how exact they have to be, the bound alone decides.
No kernel may reach another device: no remote copies, remote signals or barrier semaphores. Data moves between devices by JAX's collectives and lax.ppermute only.
A program may use at most 128 MiB of HBM per device.

v0:
```python
import jax
import jax.numpy as jnp
from jax import lax
from jax.sharding import PartitionSpec as P


def inverse_of(perm_row):
    count = perm_row.shape[0]
    marks = (perm_row[None, :] == jnp.arange(count, dtype=jnp.int32)[:, None]).astype(jnp.int32)
    return jnp.sum(marks * jnp.arange(count, dtype=jnp.int32)[None, :], axis=1)


def local(grad_part, weight, moment_one, moment_two, code, owner, holder):
    n_data = lax.axis_size("dp")
    n_racks = lax.axis_size("rack")
    rows_total = grad_part.shape[2]
    width = grad_part.shape[3]
    block_rows = rows_total // n_data
    blocks = grad_part.reshape(n_data, block_rows, width)
    ordered = jnp.take(blocks, inverse_of(owner[0]), axis=0).reshape(rows_total, width)
    owned = lax.psum_scatter(ordered.astype(jnp.float32), "dp", scatter_dimension=0, tiled=True)
    moment_one_new = 0.9 * moment_one[0] + 0.1 * owned
    moment_two_new = 0.95 * moment_two[0] + 0.05 * owned * owned
    step_size = (
        moment_one_new / (1.0 - 0.9**10) / (jnp.sqrt(moment_two_new / (1.0 - 0.95**10)) + 1e-08)
    )
    weight_new = weight[0] - 0.01 * (step_size + 0.1 * weight[0])
    states = jnp.stack([weight_new, moment_one_new, moment_two_new])
    column_width = width // n_racks
    placing = inverse_of(holder[0])
    member = lax.axis_index("rack")
    picker = (jnp.arange(n_racks, dtype=jnp.int32) == member).astype(jnp.float32)
    column = jnp.sum(code * picker[None, :], axis=1)
    partial_code = column[:, None, None, None] * states[None]
    partial_code = partial_code.reshape(code.shape[0], 3, block_rows, n_racks, column_width)
    partial_code = jnp.take(partial_code, placing, axis=3).reshape(
        code.shape[0], 3, block_rows, width
    )
    parity = lax.psum_scatter(partial_code, "rack", scatter_dimension=3, tiled=True)
    return (weight_new[None], moment_one_new[None], moment_two_new[None], parity)


def solution(mesh):
    in_specs = (
        P("rack", "dp", None, None),
        P("rack", "dp", None),
        P("rack", "dp", None),
        P("rack", "dp", None),
        P(),
        P("rack", None),
        P("dp", None),
    )
    out_specs = (
        P("rack", "dp", None),
        P("rack", "dp", None),
        P("rack", "dp", None),
        P(None, None, "dp", "rack"),
    )
    return jax.shard_map(local, mesh=mesh, in_specs=in_specs, out_specs=out_specs, check_vma=False)
```

profile of v0, /device:TPU:0, one launch (start us, length us, event | category | flops | bytes accessed | tf_op | source)
XLA Modules:
  0.0 359.9 jit_solution(16318922817797326889)
XLA Ops:
  7.2 0.0 reduce-scatter.3.cloned.1.call-start
  7.2 0.8 select_reduce_fusion
  8.0 0.1 broadcast_in_dim.44
  8.1 0.1 broadcast_in_dim.45
  8.2 8.1 %gather_fusion = bf16[16,32,8192]{2,1,0:T(8,128)(2,1)} fusion(bf16[16,32,8192]{2,1,0:T(8,128)(2,1)} %bitcast.52, s32[1024]{0:T(1024)S(1)} %pad_clamp_fusion.1), kind=kCustom, calls=%fused_computation | custom fusion | bytes 16777280 | tf_op jit(solution)/shard_map/jit(_take)/gather | solution.py:20
  16.3 10.2 %fusion = f32[512,8192]{1,0:T(8,128)} fusion(bf16[16,32,8192]{2,1,0:T(8,128)(2,1)} %gather_fusion, pred[512]{0:T(512)(128)(4,1)S(1)} %broadcast_in_dim.45), kind=kLoop, calls=%fused_computation.3 | loop fusion | flops 8388608 | bytes 25166336 | tf_op jit(solution)/shard_map/convert_element_type | solution.py:21
  26.6 0.0 reduce-scatter.3.cloned.1.call-update
  26.6 0.0 reduce-scatter.5.cloned.1.call-start
  26.7 0.6 copy-done.4
  27.2 0.1 select_reduce_fusion.1
  27.4 0.1 broadcast_bitcast_fusion
  27.5 0.1 multiply_reduce_fusion
  27.6 148.9 %reduce-scatter.3.cloned.1.call-done = f32[32,8192]{1,0:T(8,128)} async-done(((f32[512,8192]{1,0:T(8,128)}), f32[32,8192]{1,0:T(8,128)}) %reduce-scatter.3.cloned.1.call-update) | async-done | bytes 1048592 | tf_op jit(solution)/shard_map/reduce_scatter | solution.py:21
  176.5 3.0 bitcast_subtract_fusion
  179.5 0.0 copy-start
  179.5 0.0 copy-start.1
  179.5 0.0 copy-start.2
  179.5 0.6 copy.24
  180.2 0.6 copy.18
  180.8 0.6 copy.25
  181.4 0.6 copy.19
  182.0 0.6 copy.26
  182.6 0.6 copy.20
  183.3 0.4 pad_maximum_fusion
  183.7 0.0 copy-done
  183.7 0.0 copy-done.1
  183.7 6.1 %broadcast_multiply_fusion = f32[4,3,32,8,1024]{4,2,3,1,0:T(8,128)} fusion(f32[3,32,8,1024]{3,1,2,0:T(8,128)S(1)} %pad_maximum_fusion, f32[4]{0:T(128)S(1)} %multiply_reduce_fusion), kind=kLoop, calls=%fused_computation.5 | loop fusion | flops 3145728 | bytes 15728656 | tf_op jit(solution)/shard_map/mul | solution.py:34
  189.8 10.5 %gather_fusion.1 = f32[8,4,3,32,1024]{4,3,2,1,0:T(8,128)} fusion(f32[4,3,32,8,1024]{4,2,3,1,0:T(8,128)} %broadcast_multiply_fusion, s32[1024]{0:T(1024)S(1)} %pad_clamp_fusion), kind=kCustom, calls=%fused_computation.1 | custom fusion | bytes 25165856 | tf_op jit(solution)/shard_map/jit(_take)/gather | solution.py:36
  200.3 11.8 %copy.22 = f32[8,4,3,4,8,1024]{5,4,0,3,2,1:T(8,128)} copy(f32[8,4,3,4,8,1024]{5,4,3,2,1,0:T(8,128)} %bitcast.51) | data formatting | bytes 25165824 | tf_op jit(solution)/shard_map/jit(_take)/gather | solution.py:36
  212.1 10.7 %broadcast_select_fusion = f32[4,3,32,8192]{3,2,1,0:T(8,128)} fusion(f32[4,3,32,8192]{3,2,1,0:T(8,128)} %bitcast.50, pred[8192]{0:T(1024)(128)(4,1)S(1)} %bitcast.62), kind=kLoop, calls=%fused_computation.4 | loop fusion | flops 3145728 | bytes 25174016 | tf_op jit(solution)/shard_map/jit(_take)/select_n | solution.py:36
  222.8 0.0 reduce-scatter.5.cloned.1.call-update
  222.8 130.2 %reduce-scatter.5.cloned.1.call-done = f32[4,3,32,1024]{3,2,1,0:T(8,128)} async-done(((f32[4,3,32,8192]{3,2,1,0:T(8,128)}), f32[4,3,32,1024]{3,2,1,0:T(8,128)}) %reduce-scatter.5.cloned.1.call-update) | async-done | bytes 1572880 | tf_op jit(solution)/shard_map/reduce_scatter | solution.py:39
  (12 shorter events, 0.1 us)
Async XLA Ops:
  7.2 169.4 %reduce-scatter.3.cloned.1.call-start = ((), (), s32[]{:S(2)}) async-start(), calls=%async_computation.2 | async-start | bytes 17825792 | tf_op jit(solution)/shard_map/reduce_scatter | solution.py:21
  26.6 0.7 copy-start.4
  26.6 0.9 copy-start.3
  26.6 326.4 %reduce-scatter.5.cloned.1.call-start = ((), (), s32[]{:S(2)}) async-start(), calls=%async_computation.3 | async-start | bytes 14155776 | tf_op jit(solution)/shard_map/reduce_scatter | solution.py:39
  179.5 4.2 %copy-start = (f32[32,8192]{1,0:T(8,128)}, f32[32,8192]{1,0:T(8,128)S(1)}, u32[]{:S(2)}) copy-start(f32[32,8192]{1,0:T(8,128)S(1)} %get-tuple-element.4) | copy-start | bytes 3145732
  179.5 4.2 %copy-start.1 = (f32[32,8192]{1,0:T(8,128)}, f32[32,8192]{1,0:T(8,128)S(1)}, u32[]{:S(2)}) copy-start(f32[32,8192]{1,0:T(8,128)S(1)} %get-tuple-element.5) | copy-start | bytes 3145732
  179.5 4.2 %copy-start.2 = (f32[32,8192]{1,0:T(8,128)}, f32[32,8192]{1,0:T(8,128)S(1)}, u32[]{:S(2)}) copy-start(f32[32,8192]{1,0:T(8,128)S(1)} %get-tuple-element.6) | copy-start | bytes 3145732
Sparse Core Ops, SparseCore 0:
  26.7 149.7 reduce-scatter.2
  223.0 130.0 reduce-scatter.4
where the time goes:
time: 361 us; the launch traced here: 360 us
  waiting for transfers between devices  279 us (77%)
  local copies, waits for them, and re-layouts  35 us (10%)
  other arithmetic  31.5 us (9%)
  between operations  14.2 us (4%)
    reduce_scatter x1, waiting for transfers between devices, local(): lax.psum_scatter(ordered.astype(jnp.float32), 'dp', scatter_dimension=0,...  149 us
    reduce_scatter x1, waiting for transfers between devices, local(): lax.psum_scatter(partial_code, 'rack', scatter_dimension=3, tiled=True)  130 us
    gather x2, local copies, waits for them, and re-layouts, local(): jnp.take(partial_code, placing, axis=3)  22.3 us
    select_n x2, other arithmetic, local(): jnp.take(partial_code, placing, axis=3)  10.7 us
    convert_element_type x1, other arithmetic, local(): ordered.astype(jnp.float32)  10.2 us
    gather x1, local copies, waits for them, and re-layouts, local(): jnp.take(blocks, inverse_of(owner[0]), axis=0).reshape(rows_total, width)  8.15 us
  transfers between devices with their start and end apart: 2, of which 2 were waited for; matrix products, arithmetic and copies ran while one was open for 0% of the time, Pallas kernels for 0%

commit v1 on v0

v1 whole, which is shorter than its diff:
```python
import functools

import jax
import jax.numpy as jnp
from jax import lax
from jax.experimental import pallas as pl
from jax.experimental.pallas import tpu as pltpu
from jax.sharding import PartitionSpec as P

AXES = ("rack", "dp")
F32 = jnp.float32
MIB = 1 << 20


def links(move):
    pairs = []
    for rack in range(8):
        for data in range(16):
            x, y, z, core = (data // 2 % 2) * 2 + rack // 4, rack % 4, data // 4, data % 2
            nx, ny, nz, ncore = move(x, y, z, core)
            nx, ny, nz = nx % 4, ny % 4, nz % 4
            pairs.append((rack * 16 + data, ((nx % 2) * 4 + ny) * 16 + nz * 4 + (nx // 2) * 2 + ncore))
    return pairs


TO_CORE = links(lambda x, y, z, core: (x, y, z, 1 - core))
UP_Z = links(lambda x, y, z, core: (x, y, z + 1, core))
DOWN_Z = links(lambda x, y, z, core: (x, y, z - 1, core))
ACROSS = links(lambda x, y, z, core: (x ^ 2, y, z, core))
BESIDE = links(lambda x, y, z, core: (x ^ 1, y, z, core))
CORNER = links(lambda x, y, z, core: (3 - x, y, z, core))
ALONG_Y = [None] + [links(lambda x, y, z, core, step=step: (x, y + step, z, core)) for step in (1, 2, 3)]


def send(array, pairs):
    return lax.ppermute(array, AXES, pairs)


def call(body, scalars, grid, ins, outs, after=(), aliases=None, flops=0, moved=0, limit=32):
    n_in, n_after = len(ins), len(after)

    def kernel(*refs):
        marks = refs[: len(scalars)]
        rest = refs[len(scalars) :]
        body(marks, rest[:n_in], rest[n_in + n_after :])

    return pl.pallas_call(
        kernel,
        out_shape=[jax.ShapeDtypeStruct(shape, F32) for shape, _, _ in outs],
        grid_spec=pltpu.PrefetchScalarGridSpec(
            num_scalar_prefetch=len(scalars),
            grid=grid,
            in_specs=[
                pl.BlockSpec(memory_space=pl.ANY) if block is None else pl.BlockSpec(block, where)
                for _, block, where in ins
            ]
            + [pl.BlockSpec(memory_space=pl.ANY)] * n_after,
            out_specs=[pl.BlockSpec(block, where) for _, block, where in outs],
        ),
        input_output_aliases=aliases or {},
        compiler_params=pltpu.CompilerParams(vmem_limit_bytes=limit * MIB),
        cost_estimate=pl.CostEstimate(flops=flops, bytes_accessed=moved, transcendentals=0),
    )(*scalars, *[array for array, _, _ in ins], *after)


SEND, KEEP, PLACE, RANK = 0, 8, 16, 24
FAR, UP, DOWN, HERE = 0, 2, 4, 6


def index_vector(owner, holder):
    data, rack = lax.axis_index("dp"), lax.axis_index("rack")
    z, half, core = data // 4, data // 2 % 2, data % 2
    side, y = rack // 4, rack % 4
    k = jnp.arange(32, dtype=jnp.int32)
    kind, low = k // 8, k % 8
    far = low // 2
    relative = jnp.where(far == 0, 2, jnp.where(far == 1, 1, jnp.where(far == 2, 3, 0)))
    whose = jnp.where(kind == 0, 1 - core, core)
    target = (z + relative) % 4 * 4 + (half + low % 2) % 2 * 2 + whose
    rank = (side + low // 4) % 2 * 4 + (y + low % 4) % 4
    source = (side + low // 4) % 2 * 4 + (y - low % 4 + 4) % 4
    blocks = jnp.arange(16, dtype=jnp.int32)
    in_owner = jnp.sum(jnp.where(owner[None, :] == target[:, None], blocks[None, :], 0), axis=1)
    columns = jnp.arange(8, dtype=jnp.int32)
    in_holder = jnp.sum(jnp.where(holder[None, :] == rank[:, None], columns[None, :], 0), axis=1)
    return jnp.where(kind < 2, in_owner, jnp.where(kind == 2, in_holder, source))


def other_places(holder):
    rack = lax.axis_index("rack")
    side, y = rack // 4, rack % 4
    rank = (1 - side) * 4 + (y + jnp.arange(4, dtype=jnp.int32)) % 4
    columns = jnp.arange(8, dtype=jnp.int32)
    return jnp.sum(jnp.where(holder[None, :] == rank[:, None], columns[None, :], 0), axis=1)


def widen(marks, blocks, first, count, after=()):
    def body(marks, ins, outs):
        outs[0][...] = ins[0][...].astype(F32)

    return call(
        body,
        [marks],
        (count, 2),
        [(blocks, (1, 16, 8192), lambda i, c, m: (m[SEND + first + i], c, 0))],
        [((count, 32, 8192), (1, 16, 8192), lambda i, c, m: (i, c, 0))],
        after,
        moved=count * 3 * MIB // 2,
    )[0]


def pair_far(marks, blocks, given):
    def body(marks, ins, outs):
        total = ins[0][0].astype(F32) + ins[1][0]
        outs[0][0, 0] = total[:, :4096]
        outs[1][0, 0] = total[:, 4096:]

    half = ((2, 2, 16, 4096), (1, 1, 16, 4096), lambda i, c, m: (i, c, 0, 0))
    return call(
        body,
        [marks],
        (2, 2),
        [
            (blocks, (1, 16, 8192), lambda i, c, m: (m[KEEP + FAR + i], c, 0)),
            (given, (1, 16, 8192), lambda i, c, m: (i, c, 0)),
        ],
        [half, half],
        moved=5 * MIB,
    )


def pair_near(marks, blocks, given, after=()):
    def body(marks, ins, outs):
        outs[0][0, 0] = ins[0][0].astype(F32) + ins[1][0]
        outs[1][0, 0] = ins[2][0].astype(F32) + ins[3][0]

    half = ((2, 2, 16, 4096), (1, 1, 16, 4096), lambda i, c, m: (i, c, 0, 0))
    return call(
        body,
        [marks],
        (2, 2),
        [
            (blocks, (1, 16, 4096), lambda i, c, m: (m[KEEP + UP + i], c, 1)),
            (given, (1, 16, 4096), lambda i, c, m: (i, c, 1)),
            (blocks, (1, 16, 4096), lambda i, c, m: (m[KEEP + DOWN + i], c, 0)),
            (given, (1, 16, 4096), lambda i, c, m: (2 + i, c, 0)),
        ],
        [half, half],
        after,
        moved=5 * MIB,
    )


def onward(marks, blocks, given, from_below, from_above, c, after=()):
    def body(marks, ins, outs):
        outs[0][0] = ins[0][0].astype(F32) + ins[1][0] + ins[2][0, 0]
        outs[1][0] = ins[3][0].astype(F32) + ins[4][0] + ins[5][0, 0]

    half = ((2, 16, 4096), (1, 16, 4096), lambda i, m: (i, 0, 0))
    return call(
        body,
        [marks],
        (2,),
        [
            (blocks, (1, 16, 4096), lambda i, m: (m[KEEP + UP + i], c, 0)),
            (given, (1, 16, 4096), lambda i, m: (i, c, 0)),
            (from_below, (1, 1, 16, 4096), lambda i, m: (i, c, 0, 0)),
            (blocks, (1, 16, 4096), lambda i, m: (m[KEEP + DOWN + i], c, 1)),
            (given, (1, 16, 4096), lambda i, m: (2 + i, c, 1)),
            (from_above, (1, 1, 16, 4096), lambda i, m: (i, c, 0, 0)),
        ],
        [half, half],
        after,
        moved=4 * MIB,
    )


def gathered_z(marks, places, blocks, given, fwd_below, near_above, near_below, fwd_above, c):
    def body(marks, ins, outs):
        index, other = marks
        for j in range(2):
            mine = ins[j][0].astype(F32) + ins[2][j]
            outs[j][:, :4096] = mine[:, :4096] + ins[3][j] + ins[4][j, 0]
            outs[j][:, 4096:] = mine[:, 4096:] + ins[5][j, 0] + ins[6][j]
        for s in range(4):
            at = pl.multiple_of(index[PLACE + 4 + s] * 1024, 1024)
            outs[2][s] = outs[0][:, pl.ds(at, 1024)]
            at = pl.multiple_of(other[s] * 1024, 1024)
            outs[3][s] = outs[1][:, pl.ds(at, 1024)]

    rows = ((16, 8192), (16, 8192), lambda i, m, o: (0, 0))
    parts = ((4, 16, 1024), (4, 16, 1024), lambda i, m, o: (0, 0, 0))
    return call(
        body,
        [marks, places],
        (1,),
        [
            (blocks, (1, 16, 8192), lambda i, m, o: (m[KEEP + HERE], c, 0)),
            (blocks, (1, 16, 8192), lambda i, m, o: (m[KEEP + HERE + 1], c, 0)),
            (given, (2, 16, 8192), lambda i, m, o: (0, c, 0)),
            (fwd_below, (2, 16, 4096), lambda i, m, o: (0, 0, 0)),
            (near_above, (2, 1, 16, 4096), lambda i, m, o: (0, c, 0, 0)),
            (near_below, (2, 1, 16, 4096), lambda i, m, o: (0, c, 0, 0)),
            (fwd_above, (2, 16, 4096), lambda i, m, o: (0, 0, 0)),
        ],
        [rows, rows, parts, parts],
        moved=5 * MIB,
    )


def for_holders(marks, own, across, beside, corner):
    def body(marks, ins, outs):
        index = marks[0]
        for s in range(4):
            at = pl.multiple_of(index[PLACE + s] * 1024, 1024)
            outs[s][0] = ins[0][:, pl.ds(at, 1024)] + ins[1][:, pl.ds(at, 1024)]
            outs[s][1] = ins[2][s] + ins[3][s]

    rows = ((16, 8192), lambda i, m: (0, 0))
    parts = ((4, 16, 1024), lambda i, m: (0, 0, 0))
    return call(
        body,
        [marks],
        (1,),
        [(own, *rows), (across, *rows), (beside, *parts), (corner, *parts)],
        [((2, 16, 1024), (2, 16, 1024), lambda i, m: (0, 0, 0))] * 4,
        moved=2 * MIB,
    )


def old_beside(marks, weight, first, second, after=()):
    def body(marks, ins, outs):
        for k in range(3):
            outs[0][0, k] = ins[k][0]

    spec = ((1, 32, 1024), lambda s, m: (0, 0, m[PLACE + 4 + s]))
    return call(
        body,
        [marks],
        (4,),
        [(weight, *spec), (first, *spec), (second, *spec)],
        [((4, 3, 32, 1024), (1, 3, 32, 1024), lambda s, m: (s, 0, 0, 0))],
        after,
        moved=3 * MIB,
    )[0]


def old_for_holders(marks, weight, first, second, beside, after=()):
    def body(marks, ins, outs):
        s = pl.program_id(0)
        for at in range(4):

            @pl.when(s == at)
            def _():
                for k in range(3):
                    outs[at][0, k] = ins[k][0]
                    outs[at][1, k] = ins[3][0, k]

    spec = ((1, 32, 1024), lambda s, m: (0, 0, m[PLACE + s]))
    return call(
        body,
        [marks],
        (4,),
        [
            (weight, *spec),
            (first, *spec),
            (second, *spec),
            (beside, (1, 3, 32, 1024), lambda s, m: (s, 0, 0, 0)),
        ],
        [((2, 3, 32, 1024), (2, 3, 32, 1024), lambda s, m: (0, 0, 0, 0))] * 4,
        after,
        moved=6 * MIB,
    )


def advance(weight, first, second, grad):
    first_new = 0.9 * first + 0.1 * grad
    second_new = 0.95 * second + 0.05 * grad * grad
    step = first_new / (1.0 - 0.9**10) / (jnp.sqrt(second_new / (1.0 - 0.95**10)) + 1e-08)
    return weight - 0.01 * (step + 0.1 * weight), first_new, second_new


def update(weight, first, second, own, across, after=()):
    def body(marks, ins, outs):
        c = pl.program_id(0)
        for at in range(2):

            @pl.when(c == at)
            def _():
                grad = ins[3 + at][...] + ins[5 + at][...]
                new = advance(ins[0][0], ins[1][0], ins[2][0], grad)
                for k in range(3):
                    outs[k][0] = new[k]

    spec = ((1, 16, 2048), lambda c, i: (0, c, i))
    chunk = [
        ((16, 2048), lambda c, i: (0, jnp.where(c == 0, i, 3))),
        ((16, 2048), lambda c, i: (0, jnp.where(c == 1, i, 0))),
    ]
    return call(
        body,
        [],
        (2, 4),
        [(weight, *spec), (first, *spec), (second, *spec)]
        + [(own[at], *chunk[at]) for at in range(2)]
        + [(across[at], *chunk[at]) for at in range(2)],
        [((1, 32, 8192), *spec)] * 3,
        after,
        moved=8 * MIB,
    )


def encode(marks, code, old, grads, c, into=None):
    def body(marks, ins, outs):
        index, weights = marks
        for lane in range(0, 1024, 256):
            columns = pl.ds(lane, 256)
            for row in range(0, 16, 8):
                rows = pl.ds(row, 8)
                sums = [[None] * 3 for _ in range(4)]
                for s in range(4):
                    for a in range(2):
                        states = advance(
                            *(ins[s][a, k, rows, columns] for k in range(3)), ins[4 + s][a, rows, columns]
                        )
                        rank = index[RANK + a * 4 + s]
                        for j in range(4):
                            scale = weights[j, rank]
                            for k in range(3):
                                term = scale * states[k]
                                sums[j][k] = term if sums[j][k] is None else sums[j][k] + term
                for j in range(4):
                    for k in range(3):
                        outs[0][j, k, rows, columns] = sums[j][k]

    return call(
        body,
        [marks, code],
        (1,),
        [(array, (2, 3, 16, 1024), lambda i, m, w: (0, 0, c, 0)) for array in old]
        + [(array, (2, 16, 1024), lambda i, m, w: (0, 0, 0)) for array in grads]
        + ([] if into is None else [(into, None, None)]),
        [((4, 3, 32, 1024), (4, 3, 16, 1024), lambda i, m, w: (0, 0, c, 0))],
        aliases=None if into is None else {10: 0},
        moved=3 * MIB,
    )[0]


def local(grad_part, weight, moment_one, moment_two, code, owner, holder):
    marks = index_vector(owner[0], holder[0])
    blocks = grad_part.reshape(16, 32, 8192)

    far = send(widen(marks, blocks, FAR, 2), TO_CORE)
    near = send(widen(marks, blocks, UP, 4), TO_CORE)
    here = send(widen(marks, blocks, HERE, 2), TO_CORE)

    go_up, go_down = pair_far(marks, blocks, far)
    far_below, far_above = send(go_up, UP_Z), send(go_down, DOWN_Z)

    beside = send(old_beside(marks, weight, moment_one, moment_two, (go_up,)), BESIDE)

    go_up, go_down = pair_near(marks, blocks, near, (go_up,))
    near_below, near_above = send(go_up, UP_Z), send(go_down, DOWN_Z)

    places = other_places(send(holder[0], ACROSS))

    fwd = []
    for c in range(2):
        go_up, go_down = onward(marks, blocks, near, far_below, far_above, c)
        fwd.append((send(go_up, UP_Z), send(go_down, DOWN_Z)))

    old = old_for_holders(marks, weight, moment_one, moment_two, beside)
    old = [old[0]] + [send(old[s], ALONG_Y[s]) for s in (1, 2, 3)]

    own, across, grads = [], [], []
    for c in range(2):
        mine, theirs, to_beside, to_corner = gathered_z(
            marks, places, blocks, here, fwd[c][0], near_above, near_below, fwd[c][1], c
        )
        own.append(mine)
        across.append(send(theirs, ACROSS))
        from_beside, from_corner = send(to_beside, BESIDE), send(to_corner, CORNER)
        parts = for_holders(marks, mine, across[c], from_beside, from_corner)
        grads.append([parts[0]] + [send(parts[s], ALONG_Y[s]) for s in (1, 2, 3)])

    new = update(weight, moment_one, moment_two, own, across)
    parity = encode(marks, code, old, grads[0], 0)
    parity = encode(marks, code, old, grads[1], 1, parity)
    return (*new, parity)


def solution(mesh):
    in_specs = (
        P("rack", "dp", None, None),
        P("rack", "dp", None),
        P("rack", "dp", None),
        P("rack", "dp", None),
        P(),
        P("rack", None),
        P("dp", None),
    )
    out_specs = (
        P("rack", "dp", None),
        P("rack", "dp", None),
        P("rack", "dp", None),
        P(None, None, "dp", "rack"),
    )
    return jax.shard_map(local, mesh=mesh, in_specs=in_specs, out_specs=out_specs, check_vma=False)
```

time: 361 us -> 168 us (0.47)
  waiting for transfers between devices: 279 us -> 80.1 us
  starting transfers between devices: 0.08 us -> 41 us
  Pallas kernels: 0 us -> 33.8 us
  other arithmetic: 31.5 us -> 1.74 us
  local copies, waits for them, and re-layouts: 35 us -> 10.4 us
  between operations: 14.2 us -> 0.84 us
    reduce_scatter x2 -> x0, waiting for transfers between devices: 279 us -> none  [the longest x1 149 us: local(): lax.psum_scatter(ordered.astype(jnp.float32), 'dp', scatter_dimension=0,...]
    ppermute x0 -> x28, waiting for transfers between devices: none -> 80.1 us  [send(): return lax.ppermute(array, AXES, pairs)]
    ppermute x0 -> x28, starting transfers between devices: none -> 41 us  [send(): return lax.ppermute(array, AXES, pairs)]
    pallas_call x0 -> x16, Pallas kernels: none -> 33.8 us  [call(): pl.pallas_call(kernel, out_shape=[jax.ShapeDtypeStruct(shape, F32) for sh...]
    gather x3 -> x0, local copies, waits for them, and re-layouts: 30.4 us -> none  [the longest x2 22.3 us: local(): jnp.take(partial_code, placing, axis=3)]
    select_n x3 -> x1, other arithmetic: 10.7 us -> 0.02 us  [index_vector(): jnp.where(kind < 2, in_owner, jnp.where(kind == 2, in_holder, source))]
    convert_element_type x2 -> x0, other arithmetic: 10.3 us -> none  [the longest x1 10.2 us: local(): ordered.astype(jnp.float32)]
    unnamed x15 -> x26, local copies, waits for them, and re-layouts: 2.52 us -> 10.4 us
  transfers between devices with their start and end apart: 2 -> 28, of which waited for: 2 -> 6; matrix products, arithmetic and copies ran while one was open for 0% -> 0% of each run, Pallas kernels for 0% -> 16%
where the time goes in v1:
time: 168 us
  waiting for transfers between devices  80.1 us (48%)
  starting transfers between devices  41 us (24%)
  Pallas kernels  33.8 us (20%)
  local copies, waits for them, and re-layouts  10.4 us (6%)
  other arithmetic  1.74 us (1%)
    ppermute x28, waiting for transfers between devices, send(): return lax.ppermute(array, AXES, pairs)  80.1 us
    ppermute x28, starting transfers between devices, send(): return lax.ppermute(array, AXES, pairs)  41 us
    pallas_call x16, Pallas kernels, call(): pl.pallas_call(kernel, out_shape=[jax.ShapeDtypeStruct(shape, F32) for sh...  33.8 us
    unnamed x26, local copies, waits for them, and re-layouts  10.4 us
  transfers between devices with their start and end apart: 28, of which 6 were waited for; matrix products, arithmetic and copies ran while one was open for 0% of the time, Pallas kernels for 16%

profile of v1, /device:TPU:0, one launch (start us, length us, event | category | flops | bytes accessed | tf_op | source)
XLA Modules:
  0.0 167.9 jit_solution(5060212691432402718)
XLA Ops:
  2.3 3.4 %copy-done = bf16[1,1,512,8192]{3,2,1,0:T(8,128)(2,1)S(1)} copy-done((bf16[1,1,512,8192]{3,2,1,0:T(8,128)(2,1)S(1)}, bf16[1,1,512,8192]{3,2,1,0:T(8,128)(2,1)}, u32[]{:S(2)}) %copy-start) | copy-done | bytes 8388632
  5.6 4.1 %shard_map.103 = f32[4,32,8192]{2,1,0:T(8,128)} custom-call(s32[32]{0:T(128)S(1)} %compare_select_fusion.17.refs_0_, bf16[16,32,8192]{2,1,0:T(8,128)(2,1)S(1)} %bitcast.3), custom_call_target="tpu_custom_call" | custom-call | bytes 6291456 | tf_op jit(solution)/shard_map/pallas_call | solution.py:47
  11.1 2.5 %shard_map.102 = f32[2,32,8192]{2,1,0:T(8,128)} custom-call(s32[32]{0:T(128)S(1)} %compare_select_fusion.17.refs_0_, bf16[16,32,8192]{2,1,0:T(8,128)(2,1)S(1)} %bitcast.5), custom_call_target="tpu_custom_call" | custom-call | bytes 3145728 | tf_op jit(solution)/shard_map/pallas_call | solution.py:47
  13.7 9.2 %collective-permute-done.3.refs_2_ = f32[2,32,8192]{2,1,0:T(8,128)S(1)} collective-permute-done((f32[2,32,8192]{2,1,0:T(8,128)S(1)}, f32[2,32,8192]{2,1,0:T(8,128)S(1)}, u32[]{:S(2)}, u32[]{:S(2)}) %collective-permute-start.3) | collective-permute-done | bytes 2097184 | tf_op jit(solution)/shard_map/ppermute | solution.py:36
  23.7 2.1 %collective-permute-start.4 = (f32[2,2,16,4096]{3,2,1,0:T(8,128)S(1)}, f32[2,2,16,4096]{3,2,1,0:T(8,128)S(1)}, u32[]{:S(2)}, u32[]{:S(2)}) collective-permute-start(f32[2,2,16,4096]{3,2,1,0:T(8,128)S(1)} %get-tuple-element.35.refs_5_.refs_4_), channel_id=1, source_target_pairs={{0,4},{1,5},{2,6},{3,7},{4,8},{5,9},{6,10},{7,11},{8,12},{9,13},{1... | collective-permute-start | bytes 3145736 | tf_op jit(solution)/shard_map/ppermute | solution.py:36
  25.8 2.2 %collective-permute-start.5 = (f32[2,2,16,4096]{3,2,1,0:T(8,128)S(1)}, f32[2,2,16,4096]{3,2,1,0:T(8,128)S(1)}, u32[]{:S(2)}, u32[]{:S(2)}) collective-permute-start(f32[2,2,16,4096]{3,2,1,0:T(8,128)S(1)} %get-tuple-element.36), channel_id=1, source_target_pairs={{0,12},{1,13},{2,14},{3,15},{4,0},{5,1},{6,2},{7,3},{8,4},{9,5},{1... | collective-permute-start | bytes 3145736 | tf_op jit(solution)/shard_map/ppermute | solution.py:36
  28.0 2.4 %shard_map.112 = f32[4,3,32,1024]{3,2,1,0:T(8,128)} custom-call(s32[32]{0:T(128)S(1)} %compare_select_fusion.17.refs_0_, f32[1,32,8192]{2,1,0:T(8,128)S(1)} %copy-done.2, f32[1,32,8192]{2,1,0:T(8,128)S(1)} %copy-done.3, f32[1,32,8192]{2,1,0:T(8,128)S(1)} %copy-done.4, f32[2,2,16,4096]{3,2,1,0:T(8,128)S(1)} %get-tuple-element.35.refs_5_.refs_4_), custom_call_target="tpu_custom_call" | custom-call | bytes 3145728 | tf_op jit(solution)/shard_map/pallas_call | solution.py:47
  31.9 2.7 %collective-permute-start = (s32[8]{0:T(128)S(1)}, s32[8]{0:T(128)S(1)}, u32[]{:S(2)}, u32[]{:S(2)}) collective-permute-start(s32[8]{0:T(128)S(1)} %bitcast.21), channel_id=1, source_target_pairs={{0,2},{1,3},{2,0},{3,1},{4,6},{5,7},{6,4},{7,5},{8,10},{9,11},{10,... | collective-permute-start | bytes 104 | tf_op jit(solution)/shard_map/ppermute | solution.py:36
  34.6 2.6 %shard_map.107 = (f32[2,2,16,4096]{3,2,1,0:T(8,128)}, f32[2,2,16,4096]{3,2,1,0:T(8,128)}) custom-call(s32[32]{0:T(128)S(1)} %compare_select_fusion.17.refs_0_, bf16[16,32,8192]{2,1,0:T(8,128)(2,1)S(1)} %bitcast.9, f32[4,32,8192]{2,1,0:T(8,128)S(1)} %collective-permute-done.2.refs_2_.refs_5_.refs_4_, bf16[16,32,8192]{2,1,0:T(8,128)(2,1)S(1)} %bitcast.10, ...), custom_call_target="tpu_custom_call" | custom-call | bytes 5242880 | tf_op jit(solution)/shard_map/pallas_call | solution.py:47
  37.3 14.1 %collective-permute-done.4.refs_3_ = f32[2,2,16,4096]{3,2,1,0:T(8,128)S(1)} collective-permute-done((f32[2,2,16,4096]{3,2,1,0:T(8,128)S(1)}, f32[2,2,16,4096]{3,2,1,0:T(8,128)S(1)}, u32[]{:S(2)}, u32[]{:S(2)}) %collective-permute-start.4) | collective-permute-done | bytes 1048608 | tf_op jit(solution)/shard_map/ppermute | solution.py:36
  51.4 1.7 %collective-permute-start.7 = (f32[2,2,16,4096]{3,2,1,0:T(8,128)}, f32[2,2,16,4096]{3,2,1,0:T(8,128)}, u32[]{:S(2)}, u32[]{:S(2)}) collective-permute-start(f32[2,2,16,4096]{3,2,1,0:T(8,128)} %get-tuple-element.38), channel_id=1, source_target_pairs={{0,12},{1,13},{2,14},{3,15},{4,0},{5,1},{6,2},{7,3},{8,4},{9,5},{1... | collective-permute-start | bytes 3145736 | tf_op jit(solution)/shard_map/ppermute | solution.py:36
  54.4 14.6 %collective-permute-done = s32[8]{0:T(128)S(1)} collective-permute-done((s32[8]{0:T(128)S(1)}, s32[8]{0:T(128)S(1)}, u32[]{:S(2)}, u32[]{:S(2)}) %collective-permute-start) | collective-permute-done | bytes 64 | tf_op jit(solution)/shard_map/ppermute | solution.py:36
  68.9 3.2 %collective-permute-start.11 = (f32[2,16,4096]{2,1,0:T(8,128)S(1)}, f32[2,16,4096]{2,1,0:T(8,128)S(1)}, u32[]{:S(2)}, u32[]{:S(2)}) collective-permute-start(f32[2,16,4096]{2,1,0:T(8,128)S(1)} %get-tuple-element.43), channel_id=1, source_target_pairs={{0,12},{1,13},{2,14},{3,15},{4,0},{5,1},{6,2},{7,3},{8,4},{9,5},{1... | collective-permute-start | bytes 1572872 | tf_op jit(solution)/shard_map/ppermute | solution.py:36
  72.2 1.8 %shard_map.106 = (f32[2,16,4096]{2,1,0:T(8,128)}, f32[2,16,4096]{2,1,0:T(8,128)}) custom-call(s32[32]{0:T(128)S(1)} %compare_select_fusion.17.refs_0_, bf16[16,32,8192]{2,1,0:T(8,128)(2,1)S(1)} %bitcast.13, f32[4,32,8192]{2,1,0:T(8,128)S(1)} %collective-permute-done.2.refs_2_.refs_5_.refs_4_, f32[2,2,16,4096]{3,2,1,0:T(8,128)S(1)} %collective-permute-done.4.refs_3_, ...), custom_call_target="tpu_custom_call" | custom-call | bytes 4194304 | tf_op jit(solution)/shard_map/pallas_call | solution.py:47
  73.9 16.0 %collective-permute-done.10.refs_5_ = f32[2,16,4096]{2,1,0:T(8,128)S(1)} collective-permute-done((f32[2,16,4096]{2,1,0:T(8,128)S(1)}, f32[2,16,4096]{2,1,0:T(8,128)S(1)}, u32[]{:S(2)}, u32[]{:S(2)}) %collective-permute-start.10) | collective-permute-done | bytes 524320 | tf_op jit(solution)/shard_map/ppermute | solution.py:36
  91.6 3.2 %collective-permute-start.9 = (f32[2,16,4096]{2,1,0:T(8,128)}, f32[2,16,4096]{2,1,0:T(8,128)}, u32[]{:S(2)}, u32[]{:S(2)}) collective-permute-start(f32[2,16,4096]{2,1,0:T(8,128)} %get-tuple-element.40), channel_id=1, source_target_pairs={{0,12},{1,13},{2,14},{3,15},{4,0},{5,1},{6,2},{7,3},{8,4},{9,5},{1... | collective-permute-start | bytes 1572872 | tf_op jit(solution)/shard_map/ppermute | solution.py:36
  95.0 3.4 %copy-done.1 = bf16[1,1,512,8192]{3,2,1,0:T(8,128)(2,1)S(1)} copy-done((bf16[1,1,512,8192]{3,2,1,0:T(8,128)(2,1)S(1)}, bf16[1,1,512,8192]{3,2,1,0:T(8,128)(2,1)}, u32[]{:S(2)}) %copy-start.1) | copy-done | bytes 8388632
  100.5 2.4 %shard_map.110 = (f32[16,8192]{1,0:T(8,128)S(1)}, f32[16,8192]{1,0:T(8,128)S(1)}, f32[4,16,1024]{2,1,0:T(8,128)S(1)}, f32[4,16,1024]{2,1,0:T(8,128)S(1)}) custom-call(s32[32]{0:T(128)S(1)} %compare_select_fusion.17.refs_0_, s32[4]{0:T(128)S(1)} %select_reduce_fusion.2.refs_1_, bf16[16,32,8192]{2,1,0:T(8,128)(2,1)S(1)} %bitcast.15, ...), custom_call_target="tpu_custom_call" | custom-call | bytes 5242880 | tf_op jit(solution)/shard_map/pallas_call | solution.py:47
  104.4 2.7 %shard_map.108 = (f32[16,8192]{1,0:T(8,128)S(1)}, f32[16,8192]{1,0:T(8,128)S(1)}, f32[4,16,1024]{2,1,0:T(8,128)S(1)}, f32[4,16,1024]{2,1,0:T(8,128)S(1)}) custom-call(s32[32]{0:T(128)S(1)} %compare_select_fusion.17.refs_0_, s32[4]{0:T(128)S(1)} %select_reduce_fusion.2.refs_1_, bf16[16,32,8192]{2,1,0:T(8,128)(2,1)S(1)} %bitcast.17, ...), custom_call_target="tpu_custom_call" | custom-call | bytes 5242880 | tf_op jit(solution)/shard_map/pallas_call | solution.py:47
  108.6 2.7 %collective-permute-start.12 = (f32[16,8192]{1,0:T(8,128)S(1)}, f32[16,8192]{1,0:T(8,128)S(1)}, u32[]{:S(2)}, u32[]{:S(2)}) collective-permute-start(f32[16,8192]{1,0:T(8,128)S(1)} %get-tuple-element.45), channel_id=1, source_target_pairs={{0,2},{1,3},{2,0},{3,1},{4,6},{5,7},{6,4},{7,5},{8,10},{9,11},{10,... | collective-permute-start | bytes 1572872 | tf_op jit(solution)/shard_map/ppermute | solution.py:36
  111.9 3.0 %shard_map.113 = (f32[2,3,32,1024]{3,2,1,0:T(8,128)S(1)}, f32[2,3,32,1024]{3,2,1,0:T(8,128)S(1)}, f32[2,3,32,1024]{3,2,1,0:T(8,128)S(1)}, f32[2,3,32,1024]{3,2,1,0:T(8,128)S(1)}) custom-call(s32[32]{0:T(128)S(1)} %compare_select_fusion.17.refs_0_, f32[1,32,8192]{2,1,0:T(8,128)S(1)} %copy-done.2, f32[1,32,8192]{2,1,0:T(8,128)S(1)} %copy-done.3, ...), custom_call_target="tpu_custom_call" | custom-call | bytes 6291456 | tf_op jit(solution)/shard_map/pallas_call | solution.py:47
  114.9 1.6 collective-permute-start.15
  116.5 2.9 %collective-permute-start.16 = (f32[2,3,32,1024]{3,2,1,0:T(8,128)S(1)}, f32[2,3,32,1024]{3,2,1,0:T(8,128)S(1)}, u32[]{:S(2)}, u32[]{:S(2)}) collective-permute-start(f32[2,3,32,1024]{3,2,1,0:T(8,128)S(1)} %get-tuple-element.52), channel_id=1, source_target_pairs={{0,32},{1,33},{2,34},{3,35},{4,36},{5,37},{6,38},{7,39},{8,40},{9,... | collective-permute-start | bytes 2359304 | tf_op jit(solution)/shard_map/ppermute | solution.py:36
  120.8 15.3 %collective-permute-done.24.refs_4_ = f32[4,16,1024]{2,1,0:T(8,128)S(1)} collective-permute-done((f32[4,16,1024]{2,1,0:T(8,128)S(1)}, f32[4,16,1024]{2,1,0:T(8,128)S(1)}, u32[]{:S(2)}, u32[]{:S(2)}) %collective-permute-start.24) | collective-permute-done | bytes 262176 | tf_op jit(solution)/shard_map/ppermute | solution.py:36
  136.0 1.7 %collective-permute-start.19 = (f32[4,16,1024]{2,1,0:T(8,128)S(1)}, f32[4,16,1024]{2,1,0:T(8,128)S(1)}, u32[]{:S(2)}, u32[]{:S(2)}) collective-permute-start(f32[4,16,1024]{2,1,0:T(8,128)S(1)} %get-tuple-element.55), channel_id=1, source_target_pairs={{0,66},{1,67},{2,64},{3,65},{4,70},{5,71},{6,68},{7,69},{8,74},{9,... | collective-permute-start | bytes 786440 | tf_op jit(solution)/shard_map/ppermute | solution.py:36
  138.3 10.9 %collective-permute-done.19.refs_4_ = f32[4,16,1024]{2,1,0:T(8,128)S(1)} collective-permute-done((f32[4,16,1024]{2,1,0:T(8,128)S(1)}, f32[4,16,1024]{2,1,0:T(8,128)S(1)}, u32[]{:S(2)}, u32[]{:S(2)}) %collective-permute-start.19) | collective-permute-done | bytes 262176 | tf_op jit(solution)/shard_map/ppermute | solution.py:36
  149.2 1.6 collective-permute-start.25
  150.8 2.9 %collective-permute-start.26 = (f32[2,16,1024]{2,1,0:T(8,128)S(1)}, f32[2,16,1024]{2,1,0:T(8,128)S(1)}, u32[]{:S(2)}, u32[]{:S(2)}) collective-permute-start(f32[2,16,1024]{2,1,0:T(8,128)S(1)} %get-tuple-element.64), channel_id=1, source_target_pairs={{0,32},{1,33},{2,34},{3,35},{4,36},{5,37},{6,38},{7,39},{8,40},{9,... | collective-permute-start | bytes 393224 | tf_op jit(solution)/shard_map/ppermute | solution.py:36
  157.3 1.9 %collective-permute-start.22 = (f32[2,16,1024]{2,1,0:T(8,128)S(1)}, f32[2,16,1024]{2,1,0:T(8,128)S(1)}, u32[]{:S(2)}, u32[]{:S(2)}) collective-permute-start(f32[2,16,1024]{2,1,0:T(8,128)S(1)} %get-tuple-element.59), channel_id=1, source_target_pairs={{0,48},{1,49},{2,50},{3,51},{4,52},{5,53},{6,54},{7,55},{8,56},{9,... | collective-permute-start | bytes 393224 | tf_op jit(solution)/shard_map/ppermute | solution.py:36
  159.2 4.1 %shard_map.111 = (f32[1,32,8192]{2,1,0:T(8,128)}, f32[1,32,8192]{2,1,0:T(8,128)}, f32[1,32,8192]{2,1,0:T(8,128)}) custom-call(f32[1,32,8192]{2,1,0:T(8,128)S(1)} %copy-done.2, f32[1,32,8192]{2,1,0:T(8,128)S(1)} %copy-done.3, f32[1,32,8192]{2,1,0:T(8,128)S(1)} %copy-done.4, f32[16,8192]{1,0:T(8,128)S(1)} %get-tuple-element.41.refs_3_.refs_1_, ...), custom_call_target="tpu_custom_call" | custom-call | bytes 8388608 | tf_op jit(solution)/shard_map/pallas_call | solution.py:47
  163.3 2.3 %shard_map.116.refs_10_ = f32[4,3,32,1024]{3,2,1,0:T(8,128)} custom-call(s32[32]{0:T(128)S(1)} %compare_select_fusion.17.refs_0_, f32[4,8]{1,0:T(4,128)S(1)} %copy-done.9, f32[2,3,32,1024]{3,2,1,0:T(8,128)S(1)} %get-tuple-element.50.refs_2_, f32[2,3,32,1024]{3,2,1,0:T(8,128)S(1)} %collective-permute-done.15.refs_3_, ...), custom_call_target="tpu_custom_call" | custom-call | bytes 3145728 | tf_op jit(solution)/shard_map/pallas_call | solution.py:47
  165.6 2.3 %shard_map.117 = f32[4,3,32,1024]{3,2,1,0:T(8,128)} custom-call(s32[32]{0:T(128)S(1)} %compare_select_fusion.17.refs_0_, f32[4,8]{1,0:T(4,128)S(1)} %copy-done.9, f32[2,3,32,1024]{3,2,1,0:T(8,128)S(1)} %get-tuple-element.50.refs_2_, f32[2,3,32,1024]{3,2,1,0:T(8,128)S(1)} %collective-permute-done.15.refs_3_, ...), custom_call_target="tpu_custom_call", output_to_operand_aliasing={{}: (10, {})} | custom-call | bytes 3145728 | tf_op jit(solution)/shard_map/pallas_call | solution.py:47
  (74 shorter events, 19.6 us)
Async XLA Ops:
  9.8 22.1 %collective-permute-start.2 = (f32[4,32,8192]{2,1,0:T(8,128)}, f32[4,32,8192]{2,1,0:T(8,128)S(1)}, u32[]{:S(2)}, u32[]{:S(2)}) collective-permute-start(f32[4,32,8192]{2,1,0:T(8,128)} %shard_map.103), channel_id=1, source_target_pairs={{0,1},{1,0},{2,3},{3,2},{4,5},{5,4},{6,7},{7,6},{8,9},{9,8},{10,11... | collective-permute-start | bytes 12582920 | tf_op jit(solution)/shard_map/ppermute | solution.py:36
  10.5 12.4 %collective-permute-start.3 = (f32[2,32,8192]{2,1,0:T(8,128)S(1)}, f32[2,32,8192]{2,1,0:T(8,128)S(1)}, u32[]{:S(2)}, u32[]{:S(2)}) collective-permute-start(f32[2,32,8192]{2,1,0:T(8,128)S(1)} %shard_map.104), channel_id=1, source_target_pairs={{0,1},{1,0},{2,3},{3,2},{4,5},{5,4},{6,7},{7,6},{8,9},{9,8},{10,11... | collective-permute-start | bytes 6291464 | tf_op jit(solution)/shard_map/ppermute | solution.py:36
  11.1 23.5 %slice-start = ((s8[8388608]{0:T(1024)(128)(4,1)}), s8[4194304]{0:T(1024)(128)(4,1)S(1)}, s32[]{:S(2)}) async-start(s8[8388608]{0:T(1024)(128)(4,1)} %bitcast.7), calls=%async_computation | async-start | bytes 8388608
  13.6 14.4 %copy-start.3 = (f32[1,32,8192]{2,1,0:T(8,128)S(1)}, f32[1,32,8192]{2,1,0:T(8,128)}, u32[]{:S(2)}) copy-start(f32[1,32,8192]{2,1,0:T(8,128)} %refs_2_.5) | copy-start | bytes 3145732
  13.6 14.4 %copy-start.4 = (f32[1,32,8192]{2,1,0:T(8,128)S(1)}, f32[1,32,8192]{2,1,0:T(8,128)}, u32[]{:S(2)}) copy-start(f32[1,32,8192]{2,1,0:T(8,128)} %refs_3_.3) | copy-start | bytes 3145732
  13.6 21.0 %slice-start.1 = ((s8[8388608]{0:T(1024)(128)(4,1)}), s8[4194304]{0:T(1024)(128)(4,1)S(1)}, s32[]{:S(2)}) async-start(s8[8388608]{0:T(1024)(128)(4,1)} %bitcast.7), calls=%async_computation.1 | async-start | bytes 8388608
  13.6 55.3 %collective-permute-start.1 = (f32[2,32,8192]{2,1,0:T(8,128)}, f32[2,32,8192]{2,1,0:T(8,128)}, u32[]{:S(2)}, u32[]{:S(2)}) collective-permute-start(f32[2,32,8192]{2,1,0:T(8,128)} %shard_map.102), channel_id=1, source_target_pairs={{0,1},{1,0},{2,3},{3,2},{4,5},{5,4},{6,7},{7,6},{8,9},{9,8},{10,11... | collective-permute-start | bytes 6291464 | tf_op jit(solution)/shard_map/ppermute | solution.py:36
  23.7 27.6 %collective-permute-start.4 = (f32[2,2,16,4096]{3,2,1,0:T(8,128)S(1)}, f32[2,2,16,4096]{3,2,1,0:T(8,128)S(1)}, u32[]{:S(2)}, u32[]{:S(2)}) collective-permute-start(f32[2,2,16,4096]{3,2,1,0:T(8,128)S(1)} %get-tuple-element.35.refs_5_.refs_4_), channel_id=1, source_target_pairs={{0,4},{1,5},{2,6},{3,7},{4,8},{5,9},{6,10},{7,11},{8,12},{9,13},{1... | collective-permute-start | bytes 3145736 | tf_op jit(solution)/shard_map/ppermute | solution.py:36
  25.8 27.3 %collective-permute-start.5 = (f32[2,2,16,4096]{3,2,1,0:T(8,128)S(1)}, f32[2,2,16,4096]{3,2,1,0:T(8,128)S(1)}, u32[]{:S(2)}, u32[]{:S(2)}) collective-permute-start(f32[2,2,16,4096]{3,2,1,0:T(8,128)S(1)} %get-tuple-element.36), channel_id=1, source_target_pairs={{0,12},{1,13},{2,14},{3,15},{4,0},{5,1},{6,2},{7,3},{8,4},{9,5},{1... | collective-permute-start | bytes 3145736 | tf_op jit(solution)/shard_map/ppermute | solution.py:36
  30.4 81.5 %collective-permute-start.14 = (f32[4,3,32,1024]{3,2,1,0:T(8,128)}, f32[4,3,32,1024]{3,2,1,0:T(8,128)}, u32[]{:S(2)}, u32[]{:S(2)}) collective-permute-start(f32[4,3,32,1024]{3,2,1,0:T(8,128)} %shard_map.112), channel_id=1, source_target_pairs={{0,64},{1,65},{2,66},{3,67},{4,68},{5,69},{6,70},{7,71},{8,72},{9,... | collective-permute-start | bytes 4718600 | tf_op jit(solution)/shard_map/ppermute | solution.py:36
  31.9 37.0 %collective-permute-start = (s32[8]{0:T(128)S(1)}, s32[8]{0:T(128)S(1)}, u32[]{:S(2)}, u32[]{:S(2)}) collective-permute-start(s32[8]{0:T(128)S(1)} %bitcast.21), channel_id=1, source_target_pairs={{0,2},{1,3},{2,0},{3,1},{4,6},{5,7},{6,4},{7,5},{8,10},{9,11},{10,... | collective-permute-start | bytes 104 | tf_op jit(solution)/shard_map/ppermute | solution.py:36
  51.4 43.6 %collective-permute-start.7 = (f32[2,2,16,4096]{3,2,1,0:T(8,128)}, f32[2,2,16,4096]{3,2,1,0:T(8,128)}, u32[]{:S(2)}, u32[]{:S(2)}) collective-permute-start(f32[2,2,16,4096]{3,2,1,0:T(8,128)} %get-tuple-element.38), channel_id=1, source_target_pairs={{0,12},{1,13},{2,14},{3,15},{4,0},{5,1},{6,2},{7,3},{8,4},{9,5},{1... | collective-permute-start | bytes 3145736 | tf_op jit(solution)/shard_map/ppermute | solution.py:36
  53.1 41.9 %collective-permute-start.8 = (f32[2,2,16,4096]{3,2,1,0:T(8,128)}, f32[2,2,16,4096]{3,2,1,0:T(8,128)}, u32[]{:S(2)}, u32[]{:S(2)}) collective-permute-start(f32[2,2,16,4096]{3,2,1,0:T(8,128)} %get-tuple-element.39), channel_id=1, source_target_pairs={{0,4},{1,5},{2,6},{3,7},{4,8},{5,9},{6,10},{7,11},{8,12},{9,13},{1... | collective-permute-start | bytes 3145736 | tf_op jit(solution)/shard_map/ppermute | solution.py:36
  68.9 21.0 %collective-permute-start.10 = (f32[2,16,4096]{2,1,0:T(8,128)S(1)}, f32[2,16,4096]{2,1,0:T(8,128)S(1)}, u32[]{:S(2)}, u32[]{:S(2)}) collective-permute-start(f32[2,16,4096]{2,1,0:T(8,128)S(1)} %get-tuple-element.42), channel_id=1, source_target_pairs={{0,4},{1,5},{2,6},{3,7},{4,8},{5,9},{6,10},{7,11},{8,12},{9,13},{1... | collective-permute-start | bytes 1572872 | tf_op jit(solution)/shard_map/ppermute | solution.py:36
  68.9 21.8 %collective-permute-start.11 = (f32[2,16,4096]{2,1,0:T(8,128)S(1)}, f32[2,16,4096]{2,1,0:T(8,128)S(1)}, u32[]{:S(2)}, u32[]{:S(2)}) collective-permute-start(f32[2,16,4096]{2,1,0:T(8,128)S(1)} %get-tuple-element.43), channel_id=1, source_target_pairs={{0,12},{1,13},{2,14},{3,15},{4,0},{5,1},{6,2},{7,3},{8,4},{9,5},{1... | collective-permute-start | bytes 1572872 | tf_op jit(solution)/shard_map/ppermute | solution.py:36
  90.8 13.7 %collective-permute-start.6 = (f32[2,16,4096]{2,1,0:T(8,128)}, f32[2,16,4096]{2,1,0:T(8,128)}, u32[]{:S(2)}, u32[]{:S(2)}) collective-permute-start(f32[2,16,4096]{2,1,0:T(8,128)} %get-tuple-element.37), channel_id=1, source_target_pairs={{0,4},{1,5},{2,6},{3,7},{4,8},{5,9},{6,10},{7,11},{8,12},{9,13},{1... | collective-permute-start | bytes 1572872 | tf_op jit(solution)/shard_map/ppermute | solution.py:36
  91.6 12.9 %collective-permute-start.9 = (f32[2,16,4096]{2,1,0:T(8,128)}, f32[2,16,4096]{2,1,0:T(8,128)}, u32[]{:S(2)}, u32[]{:S(2)}) collective-permute-start(f32[2,16,4096]{2,1,0:T(8,128)} %get-tuple-element.40), channel_id=1, source_target_pairs={{0,12},{1,13},{2,14},{3,15},{4,0},{5,1},{6,2},{7,3},{8,4},{9,5},{1... | collective-permute-start | bytes 1572872 | tf_op jit(solution)/shard_map/ppermute | solution.py:36
  102.8 13.7 %collective-permute-start.18 = (f32[4,16,1024]{2,1,0:T(8,128)S(1)}, f32[4,16,1024]{2,1,0:T(8,128)S(1)}, u32[]{:S(2)}, u32[]{:S(2)}) collective-permute-start(f32[4,16,1024]{2,1,0:T(8,128)S(1)} %get-tuple-element.54), channel_id=1, source_target_pairs={{0,64},{1,65},{2,66},{3,67},{4,68},{5,69},{6,70},{7,71},{8,72},{9,... | collective-permute-start | bytes 786440 | tf_op jit(solution)/shard_map/ppermute | solution.py:36
  107.1 12.3 %collective-permute-start.23 = (f32[4,16,1024]{2,1,0:T(8,128)S(1)}, f32[4,16,1024]{2,1,0:T(8,128)S(1)}, u32[]{:S(2)}, u32[]{:S(2)}) collective-permute-start(f32[4,16,1024]{2,1,0:T(8,128)S(1)} %get-tuple-element.60), channel_id=1, source_target_pairs={{0,64},{1,65},{2,66},{3,67},{4,68},{5,69},{6,70},{7,71},{8,72},{9,... | collective-permute-start | bytes 786440 | tf_op jit(solution)/shard_map/ppermute | solution.py:36
  108.6 27.4 %collective-permute-start.12 = (f32[16,8192]{1,0:T(8,128)S(1)}, f32[16,8192]{1,0:T(8,128)S(1)}, u32[]{:S(2)}, u32[]{:S(2)}) collective-permute-start(f32[16,8192]{1,0:T(8,128)S(1)} %get-tuple-element.45), channel_id=1, source_target_pairs={{0,2},{1,3},{2,0},{3,1},{4,6},{5,7},{6,4},{7,5},{8,10},{9,11},{10,... | collective-permute-start | bytes 1572872 | tf_op jit(solution)/shard_map/ppermute | solution.py:36
  111.4 24.7 %collective-permute-start.24 = (f32[4,16,1024]{2,1,0:T(8,128)S(1)}, f32[4,16,1024]{2,1,0:T(8,128)S(1)}, u32[]{:S(2)}, u32[]{:S(2)}) collective-permute-start(f32[4,16,1024]{2,1,0:T(8,128)S(1)} %get-tuple-element.61), channel_id=1, source_target_pairs={{0,66},{1,67},{2,64},{3,65},{4,70},{5,71},{6,68},{7,69},{8,74},{9,... | collective-permute-start | bytes 786440 | tf_op jit(solution)/shard_map/ppermute | solution.py:36
  114.9 39.5 %collective-permute-start.15 = (f32[2,3,32,1024]{3,2,1,0:T(8,128)S(1)}, f32[2,3,32,1024]{3,2,1,0:T(8,128)S(1)}, u32[]{:S(2)}, u32[]{:S(2)}) collective-permute-start(f32[2,3,32,1024]{3,2,1,0:T(8,128)S(1)} %get-tuple-element.51), channel_id=1, source_target_pairs={{0,16},{1,17},{2,18},{3,19},{4,20},{5,21},{6,22},{7,23},{8,24},{9,... | collective-permute-start | bytes 2359304 | tf_op jit(solution)/shard_map/ppermute | solution.py:36
  116.5 39.2 %collective-permute-start.16 = (f32[2,3,32,1024]{3,2,1,0:T(8,128)S(1)}, f32[2,3,32,1024]{3,2,1,0:T(8,128)S(1)}, u32[]{:S(2)}, u32[]{:S(2)}) collective-permute-start(f32[2,3,32,1024]{3,2,1,0:T(8,128)S(1)} %get-tuple-element.52), channel_id=1, source_target_pairs={{0,32},{1,33},{2,34},{3,35},{4,36},{5,37},{6,38},{7,39},{8,40},{9,... | collective-permute-start | bytes 2359304 | tf_op jit(solution)/shard_map/ppermute | solution.py:36
  119.4 37.0 %collective-permute-start.17 = (f32[2,3,32,1024]{3,2,1,0:T(8,128)S(1)}, f32[2,3,32,1024]{3,2,1,0:T(8,128)S(1)}, u32[]{:S(2)}, u32[]{:S(2)}) collective-permute-start(f32[2,3,32,1024]{3,2,1,0:T(8,128)S(1)} %get-tuple-element.53), channel_id=1, source_target_pairs={{0,48},{1,49},{2,50},{3,51},{4,52},{5,53},{6,54},{7,55},{8,56},{9,... | collective-permute-start | bytes 2359304 | tf_op jit(solution)/shard_map/ppermute | solution.py:36
  136.0 14.8 %collective-permute-start.13 = (f32[16,8192]{1,0:T(8,128)S(1)}, f32[16,8192]{1,0:T(8,128)S(1)}, u32[]{:S(2)}, u32[]{:S(2)}) collective-permute-start(f32[16,8192]{1,0:T(8,128)S(1)} %get-tuple-element.46), channel_id=1, source_target_pairs={{0,2},{1,3},{2,0},{3,1},{4,6},{5,7},{6,4},{7,5},{8,10},{9,11},{10,... | collective-permute-start | bytes 1572872 | tf_op jit(solution)/shard_map/ppermute | solution.py:36
  136.0 13.2 %collective-permute-start.19 = (f32[4,16,1024]{2,1,0:T(8,128)S(1)}, f32[4,16,1024]{2,1,0:T(8,128)S(1)}, u32[]{:S(2)}, u32[]{:S(2)}) collective-permute-start(f32[4,16,1024]{2,1,0:T(8,128)S(1)} %get-tuple-element.55), channel_id=1, source_target_pairs={{0,66},{1,67},{2,64},{3,65},{4,70},{5,71},{6,68},{7,69},{8,74},{9,... | collective-permute-start | bytes 786440 | tf_op jit(solution)/shard_map/ppermute | solution.py:36
  149.2 8.1 %collective-permute-start.25 = (f32[2,16,1024]{2,1,0:T(8,128)S(1)}, f32[2,16,1024]{2,1,0:T(8,128)S(1)}, u32[]{:S(2)}, u32[]{:S(2)}) collective-permute-start(f32[2,16,1024]{2,1,0:T(8,128)S(1)} %get-tuple-element.63), channel_id=1, source_target_pairs={{0,16},{1,17},{2,18},{3,19},{4,20},{5,21},{6,22},{7,23},{8,24},{9,... | collective-permute-start | bytes 393224 | tf_op jit(solution)/shard_map/ppermute | solution.py:36
  150.8 12.4 %collective-permute-start.26 = (f32[2,16,1024]{2,1,0:T(8,128)S(1)}, f32[2,16,1024]{2,1,0:T(8,128)S(1)}, u32[]{:S(2)}, u32[]{:S(2)}) collective-permute-start(f32[2,16,1024]{2,1,0:T(8,128)S(1)} %get-tuple-element.64), channel_id=1, source_target_pairs={{0,32},{1,33},{2,34},{3,35},{4,36},{5,37},{6,38},{7,39},{8,40},{9,... | collective-permute-start | bytes 393224 | tf_op jit(solution)/shard_map/ppermute | solution.py:36
  154.3 8.9 %collective-permute-start.27 = (f32[2,16,1024]{2,1,0:T(8,128)S(1)}, f32[2,16,1024]{2,1,0:T(8,128)S(1)}, u32[]{:S(2)}, u32[]{:S(2)}) collective-permute-start(f32[2,16,1024]{2,1,0:T(8,128)S(1)} %get-tuple-element.65), channel_id=1, source_target_pairs={{0,48},{1,49},{2,50},{3,51},{4,52},{5,53},{6,54},{7,55},{8,56},{9,... | collective-permute-start | bytes 393224 | tf_op jit(solution)/shard_map/ppermute | solution.py:36
  155.7 9.8 %collective-permute-start.20 = (f32[2,16,1024]{2,1,0:T(8,128)S(1)}, f32[2,16,1024]{2,1,0:T(8,128)S(1)}, u32[]{:S(2)}, u32[]{:S(2)}) collective-permute-start(f32[2,16,1024]{2,1,0:T(8,128)S(1)} %get-tuple-element.57), channel_id=1, source_target_pairs={{0,16},{1,17},{2,18},{3,19},{4,20},{5,21},{6,22},{7,23},{8,24},{9,... | collective-permute-start | bytes 393224 | tf_op jit(solution)/shard_map/ppermute | solution.py:36
  156.4 9.1 %collective-permute-start.21 = (f32[2,16,1024]{2,1,0:T(8,128)S(1)}, f32[2,16,1024]{2,1,0:T(8,128)S(1)}, u32[]{:S(2)}, u32[]{:S(2)}) collective-permute-start(f32[2,16,1024]{2,1,0:T(8,128)S(1)} %get-tuple-element.58), channel_id=1, source_target_pairs={{0,32},{1,33},{2,34},{3,35},{4,36},{5,37},{6,38},{7,39},{8,40},{9,... | collective-permute-start | bytes 393224 | tf_op jit(solution)/shard_map/ppermute | solution.py:36
  157.3 8.3 %collective-permute-start.22 = (f32[2,16,1024]{2,1,0:T(8,128)S(1)}, f32[2,16,1024]{2,1,0:T(8,128)S(1)}, u32[]{:S(2)}, u32[]{:S(2)}) collective-permute-start(f32[2,16,1024]{2,1,0:T(8,128)S(1)} %get-tuple-element.59), channel_id=1, source_target_pairs={{0,48},{1,49},{2,50},{3,51},{4,52},{5,53},{6,54},{7,55},{8,56},{9,... | collective-permute-start | bytes 393224 | tf_op jit(solution)/shard_map/ppermute | solution.py:36
  (9 other events, 36.9 us)

commit v2 on v0

v2 whole, which is shorter than its diff:
```python
import jax
import jax.numpy as jnp
from jax import lax
from jax.experimental import pallas as pl
from jax.experimental.pallas import tpu as pltpu
from jax.sharding import PartitionSpec as P

AXES = ("rack", "dp")
F32, BF16 = jnp.float32, jnp.bfloat16
MIB = 1 << 20
VMEM = pl.BlockSpec(memory_space=pltpu.VMEM)
SMEM = pl.BlockSpec(memory_space=pltpu.SMEM)
HBM = pl.BlockSpec(memory_space=pltpu.HBM)


def links(move):
    pairs = []
    for rack in range(8):
        for data in range(16):
            x, y, z, core = (data // 2 % 2) * 2 + rack // 4, rack % 4, data // 4, data % 2
            nx, ny, nz, ncore = move(x, y, z, core)
            nx, ny, nz = nx % 4, ny % 4, nz % 4
            pairs.append((rack * 16 + data, ((nx % 2) * 4 + ny) * 16 + nz * 4 + (nx // 2) * 2 + ncore))
    return pairs


TO_CORE = links(lambda x, y, z, core: (x, y, z, 1 - core))
UP_Z = links(lambda x, y, z, core: (x, y, z + 1, core))
DOWN_Z = links(lambda x, y, z, core: (x, y, z - 1, core))
ACROSS = links(lambda x, y, z, core: (x ^ 2, y, z, core))
BESIDE = links(lambda x, y, z, core: (x ^ 1, y, z, core))
CORNER = links(lambda x, y, z, core: (3 - x, y, z, core))
ALONG_Y = [None] + [links(lambda x, y, z, core, step=step: (x, y + step, z, core)) for step in (1, 2, 3)]

RELATIVE_Z = (2, 1, 3, 0)
FAR, UP, DOWN, HERE = 0, 2, 4, 6


def send(array, pairs):
    return lax.ppermute(array, AXES, pairs)


def call(name, body, ins, outs, scratch=(), aliases=None, limit=16):
    return pl.pallas_call(
        body,
        out_shape=[jax.ShapeDtypeStruct(shape, kind) for shape, kind, _ in outs],
        in_specs=[spec for _, spec in ins],
        out_specs=[spec for _, _, spec in outs],
        scratch_shapes=list(scratch),
        input_output_aliases=aliases or {},
        compiler_params=pltpu.CompilerParams(vmem_limit_bytes=limit * MIB),
        name=name,
    )(*[array for array, _ in ins])


def position():
    data, rack = lax.axis_index("dp"), lax.axis_index("rack")
    return lax.div(data, 4), lax.rem(lax.div(data, 2), 2), lax.rem(data, 2), lax.div(rack, 4), lax.rem(rack, 4)


def found(row, count, value):
    at = jnp.int32(0)
    for i in range(count):
        at = jnp.where(row[0, i] == value, i, at)
    return at


def block_of(owner, slot, keep):
    z, half, core, _, _ = position()
    whose = core if keep else 1 - core
    target = lax.rem(z + RELATIVE_Z[slot // 2], 4) * 4 + lax.rem(half + slot % 2, 2) * 2 + whose
    return found(owner, 16, target)


def column_of(holder, side_step, y_step):
    _, _, _, side, y = position()
    rank = lax.rem(side + side_step, 2) * 4 + lax.rem(y + y_step, 4)
    return pl.multiple_of(found(holder, 8, rank) * 1024, 1024)


def by_tiles(width, step, body):
    def one(i, carry):
        body(pl.ds(pl.multiple_of(i * step, step), step))
        return carry

    lax.fori_loop(0, width // step, one, 0)


def widen_far(blocks, owner):
    def body(blocks, owner, out, read, sems):
        copies = [
            pltpu.make_async_copy(blocks.at[block_of(owner, FAR + i, False)], read.at[i], sems.at[i]) for i in range(2)
        ]
        for copy in copies:
            copy.start()
        for i in range(2):
            copies[i].wait()

            def cast(columns):
                out[i, :, columns] = read[i, :, columns].astype(F32)

            by_tiles(8192, 1024, cast)

    return call(
        "widen_far",
        body,
        [(blocks, HBM), (owner, SMEM)],
        [((2, 32, 8192), F32, VMEM)],
        [pltpu.VMEM((2, 32, 8192), BF16), pltpu.SemaphoreType.DMA((2,))],
        limit=50,
    )[0]


def widen_rest(blocks, owner, far):
    def body(blocks, owner, far, out, own, read, sems):
        copies = [
            pltpu.make_async_copy(blocks.at[block_of(owner, UP + i, False)], read.at[i], sems.at[i]) for i in range(6)
        ] + [pltpu.make_async_copy(blocks.at[block_of(owner, i, True)], own.at[i], sems.at[6 + i]) for i in range(8)]
        for copy in copies:
            copy.start()
        for i in range(6):
            copies[i].wait()

            def cast(columns):
                out[i, :, columns] = read[i, :, columns].astype(F32)

            by_tiles(8192, 1024, cast)
        for copy in copies[6:]:
            copy.wait()

    return call(
        "widen_rest",
        body,
        [(blocks, HBM), (owner, SMEM), (far, VMEM)],
        [((6, 32, 8192), F32, VMEM), ((8, 32, 8192), BF16, VMEM)],
        [pltpu.VMEM((6, 32, 8192), BF16), pltpu.SemaphoreType.DMA((14,))],
        limit=40,
    )


def pair_far(own, far, rest):
    def body(own, far, rest, up, down, same):
        for j in range(2):

            def add(columns):
                later = pl.ds(columns.start + 4096, columns.size)
                up[j, :, columns] = own[FAR + j, :, columns].astype(F32) + far[j, :, columns]
                down[j, :, columns] = own[FAR + j, :, later].astype(F32) + far[j, :, later]

            by_tiles(4096, 512, add)

    half = ((2, 32, 4096), F32, VMEM)
    return call(
        "pair_far",
        body,
        [(own, VMEM), (far, VMEM), (rest, VMEM)],
        [half, half, (rest.shape, F32, VMEM)],
        aliases={2: 2},
    )


def onward(own, rest, below, above, c, after=()):
    def body(own, rest, below, above, *refs):
        up, down = refs[len(after) :]
        rows = pl.ds(16 * c, 16)

        def pair(slot, columns):
            return own[slot, rows, columns].astype(F32) + rest[slot - 2, rows, columns]

        for j in range(2):

            def add(columns):
                later = pl.ds(columns.start + 4096, columns.size)
                up[0, j, :, columns] = pair(UP + j, columns) + below[j, rows, columns]
                up[1, j, :, columns] = pair(UP + j, later)
                down[0, j, :, columns] = pair(DOWN + j, later) + above[j, rows, columns]
                down[1, j, :, columns] = pair(DOWN + j, columns)

            by_tiles(4096, 512, add)

    half = ((2, 2, 16, 4096), F32, VMEM)
    return call(
        f"onward_{c}",
        body,
        [(own, VMEM), (rest, VMEM), (below, VMEM), (above, VMEM)] + [(array, VMEM) for array in after],
        [half, half],
    )


def gathered_z(own, rest, holder, below, above, c, after):
    def body(own, rest, mine_held, other_held, below, above, *refs):
        mine, theirs, beside, corner = refs[len(after) :]
        rows = pl.ds(16 * c, 16)
        for j, out in enumerate((mine, theirs)):

            def add(columns):
                later = pl.ds(columns.start + 4096, columns.size)
                both = own[HERE + j, rows, columns].astype(F32) + rest[HERE - 2 + j, rows, columns]
                out[:, columns] = both + below[0, j, :, columns] + above[1, j, :, columns]
                both = own[HERE + j, rows, later].astype(F32) + rest[HERE - 2 + j, rows, later]
                out[:, later] = both + below[1, j, :, columns] + above[0, j, :, columns]

            by_tiles(4096, 512, add)
        for s in range(4):
            beside[s] = mine[:, pl.ds(column_of(mine_held, 1, s), 1024)]
            corner[s] = theirs[:, pl.ds(column_of(other_held, 1, s), 1024)]

    rows = ((16, 8192), F32, VMEM)
    parts = ((4, 16, 1024), F32, VMEM)
    return call(
        f"gathered_z_{c}",
        body,
        [(own, VMEM), (rest, VMEM), (holder[0], SMEM), (holder[1], SMEM), (below, VMEM), (above, VMEM)]
        + [(array, VMEM) for array in after],
        [rows, rows, parts, parts],
    )


def for_holders(holder, mine, across, beside, corner, after=()):
    def body(holder, mine, across, beside, corner, *refs):
        outs = refs[len(after) :]
        for s in range(4):
            columns = pl.ds(column_of(holder, 0, s), 1024)
            outs[s][0] = mine[:, columns] + across[:, columns]
            outs[s][1] = beside[s] + corner[s]

    return call(
        "for_holders",
        body,
        [(holder, SMEM)] + [(array, VMEM) for array in (mine, across, beside, corner, *after)],
        [((2, 16, 1024), F32, VMEM)] * 4,
    )


def old_parts(name, holder, states, asked, after):
    def body(holder, weight, first, second, *refs):
        outs, same, sems = refs[len(after) : -2], refs[-2], refs[-1]
        copies = []
        for out, steps in zip(outs, asked):
            for i, (a, s) in enumerate(steps):
                columns = pl.ds(column_of(holder, a, s), 1024)
                for k, old in enumerate((weight, first, second)):
                    copies.append(pltpu.make_async_copy(old.at[0, :, columns], out.at[i, k], sems.at[len(copies)]))
        for copy in copies:
            copy.start()
        for i in range(8):
            same[0, i] = holder[0, i]
        for copy in copies:
            copy.wait()

    return call(
        name,
        body,
        [(holder, SMEM)] + [(old, HBM) for old in states] + [(array, VMEM) for array in after],
        [((len(steps), 3, 32, 1024), F32, VMEM) for steps in asked] + [((1, 8), jnp.int32, SMEM)],
        [pltpu.SemaphoreType.DMA((3 * sum(len(steps) for steps in asked),))],
    )


def other_side(olds, after):
    count = len(olds)

    def body(*refs):
        out = refs[count + len(after)]
        for i in range(count):

            def copy(columns):
                for k in range(3):
                    out[i, k, :, columns] = refs[i][1, k, :, columns]

            by_tiles(1024, 256, copy)

    return call(
        "other_side",
        body,
        [(old, VMEM) for old in olds] + after,
        [((count, 3, 32, 1024), F32, VMEM)],
    )[0]


def advance(weight, first, second, grad):
    first_new = 0.9 * first + 0.1 * grad
    second_new = 0.95 * second + 0.05 * grad * grad
    step = first_new / (1.0 - 0.9**10) / (jnp.sqrt(second_new / (1.0 - 0.95**10)) + 1e-08)
    return weight - 0.01 * (step + 0.1 * weight), first_new, second_new


def update(weight, first, second, mine, across):
    def body(weight, first, second, mine_0, mine_1, across_0, across_1, *refs):
        outs, read, sems = refs[:3], refs[3], refs[4]
        reads = [pltpu.make_async_copy(old.at[0], read.at[k], sems.at[k]) for k, old in enumerate((weight, first, second))]
        for copy in reads:
            copy.start()
        for copy in reads:
            copy.wait()
        writes = []
        for c, (mine, across) in enumerate(((mine_0, across_0), (mine_1, across_1))):
            rows = pl.ds(16 * c, 16)

            def step(columns):
                new = advance(*(read[k, rows, columns] for k in range(3)), mine[:, columns] + across[:, columns])
                for k in range(3):
                    read[k, rows, columns] = new[k]

            by_tiles(8192, 512, step)
            for k in range(3):
                copy = pltpu.make_async_copy(read.at[k, rows], outs[k].at[0, rows], sems.at[3 + 3 * c + k])
                copy.start()
                writes.append(copy)
        for copy in writes:
            copy.wait()

    return call(
        "update",
        body,
        [(weight, HBM), (first, HBM), (second, HBM)] + [(array, VMEM) for array in (*mine, *across)],
        [((1, 32, 8192), F32, HBM)] * 3,
        [pltpu.VMEM((3, 32, 8192), F32), pltpu.SemaphoreType.DMA((9,))],
    )


def encode(code, old, grads, c, into=None):
    arrays, places = [], [[None] * 4, [None] * 4]
    for a in range(2):
        for s in range(4):
            array, part = old[a][s]
            known = [i for i, other in enumerate(arrays) if other is array]
            if not known:
                arrays.append(array)
            places[a][s] = (known[0] if known else len(arrays) - 1, part)

    def body(code, *refs):
        olds, ins, (out, total, sem) = refs[: len(arrays)], refs[len(arrays) :], refs[-3:]
        _, _, _, side, y = position()
        ranks = [[lax.rem(side + a, 2) * 4 + lax.rem(y + 4 - s, 4) for s in range(4)] for a in range(2)]
        scales = [[[code[j, ranks[a][s]] for s in range(4)] for a in range(2)] for j in range(4)]

        def state(s, a, k, row, columns):
            array, part = places[a][s]
            return olds[array][part, k, pl.ds(16 * c + row, 8), columns]

        for row in range(0, 16, 8):

            def one(columns):
                rows = pl.ds(row, 8)
                sums = [[None] * 3 for _ in range(4)]
                for s in range(4):
                    for a in range(2):
                        was = [state(s, a, k, row, columns) for k in range(3)]
                        states = advance(*was, ins[s][a, rows, columns])
                        for j in range(4):
                            for k in range(3):
                                term = scales[j][a][s] * states[k]
                                sums[j][k] = term if sums[j][k] is None else sums[j][k] + term
                for j in range(4):
                    for k in range(3):
                        total[j, k, rows, columns] = sums[j][k]

            by_tiles(1024, 256, one)
        copy = pltpu.make_async_copy(total, out.at[:, :, pl.ds(16 * c, 16)], sem)
        copy.start()
        copy.wait()

    return call(
        f"encode_{c}",
        body,
        [(code, SMEM)] + [(array, VMEM) for array in (*arrays, *grads)] + ([] if into is None else [(into, HBM)]),
        [((4, 3, 32, 1024), F32, HBM)],
        [pltpu.VMEM((4, 3, 16, 1024), F32), pltpu.SemaphoreType.DMA],
        aliases=None if into is None else {1 + len(arrays) + len(grads): 0},
    )[0]


def local(grad_part, weight, moment_one, moment_two, code, owner, holder):
    blocks = grad_part.reshape(16, 32, 8192)
    states = (weight, moment_one, moment_two)

    far = widen_far(blocks, owner)
    rest, own = widen_rest(blocks, owner, far)
    go_up, go_down, rest = pair_far(own, send(far, TO_CORE), rest)
    rest = send(rest, TO_CORE)
    far_below, far_above = send(go_up, UP_Z), send(go_down, DOWN_Z)

    one, three, _ = old_parts("old_odd", holder, states, [[(0, 1), (1, 1)], [(0, 3), (1, 3)]], (go_up,))
    one, three = send(one, ALONG_Y[1]), send(three, ALONG_Y[3])
    asked = [[(0, 2), (1, 2)], [(0, 0)], [(1, 0)]]
    two, zero, beside, held = old_parts("old_even", holder, states, asked, (rest,))
    beside = send(beside, BESIDE)
    two = send(two, ALONG_Y[2])
    held = send(held, ACROSS)

    go_up, go_down = onward(own, rest, far_below, far_above, 0)
    along_z = [(send(go_up, UP_Z), send(go_down, DOWN_Z))]
    odd = other_side([one, three], [(go_up, VMEM)])
    even = other_side([two], [(odd, VMEM), (beside, VMEM), (held, SMEM)])
    after = (even,)
    odd, even = send(odd, BESIDE), send(even, BESIDE)
    go_up, go_down = onward(own, rest, far_below, far_above, 1)
    along_z.append((send(go_up, UP_Z), send(go_down, DOWN_Z)))
    old = [[(zero, 0), (one, 0), (two, 0), (three, 0)], [(beside, 0), (odd, 0), (even, 0), (odd, 1)]]

    mine, across, parts = [], [], []
    for c in range(2):
        ours, theirs, to_beside, to_corner = gathered_z(own, rest, (holder, held), *along_z[c], c, after)
        after = (odd, even)
        mine.append(ours)
        across.append(send(theirs, ACROSS))
        parts.append((send(to_beside, BESIDE), send(to_corner, CORNER)))
    grads = []
    for c in range(2):
        sums = for_holders(holder, mine[c], across[c], *parts[c], () if c else (mine[1],))
        grads.append([sums[0]] + [send(sums[s], ALONG_Y[s]) for s in (1, 2, 3)])

    new = update(*states, mine, across)
    parity = encode(code, old, grads[0], 0)
    parity = encode(code, old, grads[1], 1, parity)
    return (*new, parity)


def solution(mesh):
    in_specs = (
        P("rack", "dp", None, None),
        P("rack", "dp", None),
        P("rack", "dp", None),
        P("rack", "dp", None),
        P(),
        P("rack", None),
        P("dp", None),
    )
    out_specs = (
        P("rack", "dp", None),
        P("rack", "dp", None),
        P("rack", "dp", None),
        P(None, None, "dp", "rack"),
    )
    return jax.shard_map(local, mesh=mesh, in_specs=in_specs, out_specs=out_specs, check_vma=False)
```

time: 361 us -> 134 us (0.37)
  waiting for transfers between devices: 279 us -> 56.9 us
  starting transfers between devices: 0.08 us -> 53.9 us
  local copies, waits for them, and re-layouts: 35 us -> 0.67 us
  other arithmetic: 31.5 us -> 0 us
  Pallas kernels: 0 us -> 21.5 us
  between operations: 14.2 us -> 0.84 us
    reduce_scatter x2 -> x0, waiting for transfers between devices: 279 us -> none  [the longest x1 149 us: local(): lax.psum_scatter(ordered.astype(jnp.float32), 'dp', scatter_dimension=0,...]
    ppermute x0 -> x27, waiting for transfers between devices: none -> 56.9 us  [send(): return lax.ppermute(array, AXES, pairs)]
    ppermute x0 -> x27, starting transfers between devices: none -> 53.9 us  [send(): return lax.ppermute(array, AXES, pairs)]
    gather x3 -> x0, local copies, waits for them, and re-layouts: 30.4 us -> none  [the longest x2 22.3 us: local(): jnp.take(partial_code, placing, axis=3)]
    pallas_call x0 -> x16, Pallas kernels: none -> 21.5 us  [call(): pl.pallas_call(body, out_shape=[jax.ShapeDtypeStruct(shape, kind) for sha...]
    select_n x3 -> x0, other arithmetic: 10.7 us -> none  [the longest x2 10.7 us: local(): jnp.take(partial_code, placing, axis=3)]
    convert_element_type x2 -> x0, other arithmetic: 10.3 us -> none  [the longest x1 10.2 us: local(): ordered.astype(jnp.float32)]
    mul x1 -> x0, other arithmetic: 6.14 us -> none  [local(): partial_code = column[:, None, None, None] * states[None]]
  transfers between devices with their start and end apart: 2 -> 27, of which waited for: 2 -> 12; matrix products, arithmetic and copies ran while one was open for 0% -> 0% of each run, Pallas kernels for 0% -> 13%
where the time goes in v2:
time: 134 us
  waiting for transfers between devices  56.9 us (42%)
  starting transfers between devices  53.9 us (40%)
  Pallas kernels  21.5 us (16%)
    ppermute x27, waiting for transfers between devices, send(): return lax.ppermute(array, AXES, pairs)  56.9 us
    ppermute x27, starting transfers between devices, send(): return lax.ppermute(array, AXES, pairs)  53.9 us
    pallas_call x16, Pallas kernels, call(): pl.pallas_call(body, out_shape=[jax.ShapeDtypeStruct(shape, kind) for sha...  21.5 us
  transfers between devices with their start and end apart: 27, of which 12 were waited for; matrix products, arithmetic and copies ran while one was open for 0% of the time, Pallas kernels for 13%

profile of v2, /device:TPU:0, one launch (start us, length us, event | category | flops | bytes accessed | tf_op | source)
XLA Modules:
  0.0 133.7 jit_solution(17246164512011622210)
XLA Ops:
  1.3 1.9 %widen_far.1.far = f32[2,32,8192]{2,1,0:T(8,128)S(1)} custom-call(bf16[16,32,8192]{2,1,0:T(8,128)(2,1)} %bitcast.1, s32[1,16]{1,0:T(1,128)S(1)} %copy-done.5), custom_call_target="tpu_custom_call" | custom-call | tf_op jit(solution)/shard_map/widen_far/pallas_call | solution.py:44
  3.3 3.8 %widen_rest.1 = (f32[6,32,8192]{2,1,0:T(8,128)S(1)}, bf16[8,32,8192]{2,1,0:T(8,128)(2,1)S(1)}) custom-call(bf16[16,32,8192]{2,1,0:T(8,128)(2,1)} %bitcast.2, s32[1,16]{1,0:T(1,128)S(1)} %copy-done.6, f32[2,32,8192]{2,1,0:T(8,128)S(1)} %widen_far.1.far), custom_call_target="tpu_custom_call" | custom-call | tf_op jit(solution)/shard_map/widen_rest/pallas_call | solution.py:44
  8.0 2.0 %collective-permute-start.3 = (f32[2,32,4096]{2,1,0:T(8,128)S(1)}, f32[2,32,4096]{2,1,0:T(8,128)S(1)}, u32[]{:S(2)}, u32[]{:S(2)}) collective-permute-start(f32[2,32,4096]{2,1,0:T(8,128)S(1)} %get-tuple-element.42.refs_0_), channel_id=1, source_target_pairs={{0,4},{1,5},{2,6},{3,7},{4,8},{5,9},{6,10},{7,11},{8,12},{9,13},{1... | collective-permute-start | bytes 3145736 | tf_op jit(solution)/shard_map/ppermute | solution.py:40
  10.0 2.1 %collective-permute-start.4 = (f32[2,32,4096]{2,1,0:T(8,128)S(1)}, f32[2,32,4096]{2,1,0:T(8,128)S(1)}, u32[]{:S(2)}, u32[]{:S(2)}) collective-permute-start(f32[2,32,4096]{2,1,0:T(8,128)S(1)} %get-tuple-element.43), channel_id=1, source_target_pairs={{0,12},{1,13},{2,14},{3,15},{4,0},{5,1},{6,2},{7,3},{8,4},{9,5},{1... | collective-permute-start | bytes 3145736 | tf_op jit(solution)/shard_map/ppermute | solution.py:40
  12.1 1.7 %old_odd.1 = (f32[2,3,32,1024]{3,2,1,0:T(8,128)S(1)}, f32[2,3,32,1024]{3,2,1,0:T(8,128)S(1)}, s32[1,8]{1,0:T(1,128)}) custom-call(s32[1,8]{1,0:T(1,128)S(1)} %copy-done.3, f32[1,32,8192]{2,1,0:T(8,128)S(1)} %copy-done, f32[1,32,8192]{2,1,0:T(8,128)S(1)} %copy-done.1, f32[1,32,8192]{2,1,0:T(8,128)S(1)} %copy-done.2, f32[2,32,4096]{2,1,0:T(8,128)S(1)} %get-tuple-element.42.refs_0_), custom_call_target="tpu_custom_call" | custom-call | tf_op jit(solution)/shard_map/old_odd/pallas_call | solution.py:44
  13.9 1.6 %collective-permute-start.8 = (f32[2,3,32,1024]{3,2,1,0:T(8,128)S(1)}, f32[2,3,32,1024]{3,2,1,0:T(8,128)S(1)}, u32[]{:S(2)}, u32[]{:S(2)}) collective-permute-start(f32[2,3,32,1024]{3,2,1,0:T(8,128)S(1)} %get-tuple-element.47), channel_id=1, source_target_pairs={{0,16},{1,17},{2,18},{3,19},{4,20},{5,21},{6,22},{7,23},{8,24},{9,... | collective-permute-start | bytes 2359304 | tf_op jit(solution)/shard_map/ppermute | solution.py:40
  15.5 1.7 %collective-permute-start.9 = (f32[2,3,32,1024]{3,2,1,0:T(8,128)S(1)}, f32[2,3,32,1024]{3,2,1,0:T(8,128)S(1)}, u32[]{:S(2)}, u32[]{:S(2)}) collective-permute-start(f32[2,3,32,1024]{3,2,1,0:T(8,128)S(1)} %get-tuple-element.48), channel_id=1, source_target_pairs={{0,48},{1,49},{2,50},{3,51},{4,52},{5,53},{6,54},{7,55},{8,56},{9,... | collective-permute-start | bytes 2359304 | tf_op jit(solution)/shard_map/ppermute | solution.py:40
  17.9 1.8 %old_even.1 = (f32[2,3,32,1024]{3,2,1,0:T(8,128)S(1)}, f32[1,3,32,1024]{3,2,1,0:T(8,128)S(1)}, f32[1,3,32,1024]{3,2,1,0:T(8,128)S(1)}, s32[1,8]{1,0:T(1,128)S(1)}) custom-call(s32[1,8]{1,0:T(1,128)S(1)} %copy-done.3, f32[1,32,8192]{2,1,0:T(8,128)S(1)} %copy-done, f32[1,32,8192]{2,1,0:T(8,128)S(1)} %copy-done.1, f32[1,32,8192]{2,1,0:T(8,128)S(1)} %copy-done.2, ...), custom_call_target="tpu_custom_call" | custom-call | tf_op jit(solution)/shard_map/old_even/pallas_call | solution.py:44
  19.7 3.4 %collective-permute-start.7 = (f32[2,3,32,1024]{3,2,1,0:T(8,128)S(1)}, f32[2,3,32,1024]{3,2,1,0:T(8,128)S(1)}, u32[]{:S(2)}, u32[]{:S(2)}) collective-permute-start(f32[2,3,32,1024]{3,2,1,0:T(8,128)S(1)} %get-tuple-element.46), channel_id=1, source_target_pairs={{0,32},{1,33},{2,34},{3,35},{4,36},{5,37},{6,38},{7,39},{8,40},{9,... | collective-permute-start | bytes 2359304 | tf_op jit(solution)/shard_map/ppermute | solution.py:40
  23.1 12.6 %collective-permute-done.3.below = f32[2,32,4096]{2,1,0:T(8,128)S(1)} collective-permute-done((f32[2,32,4096]{2,1,0:T(8,128)S(1)}, f32[2,32,4096]{2,1,0:T(8,128)S(1)}, u32[]{:S(2)}, u32[]{:S(2)}) %collective-permute-start.3) | collective-permute-done | bytes 1048608 | tf_op jit(solution)/shard_map/ppermute | solution.py:40
  37.6 3.2 %collective-permute-start.6 = (f32[2,2,16,4096]{3,2,1,0:T(8,128)S(1)}, f32[2,2,16,4096]{3,2,1,0:T(8,128)S(1)}, u32[]{:S(2)}, u32[]{:S(2)}) collective-permute-start(f32[2,2,16,4096]{3,2,1,0:T(8,128)S(1)} %get-tuple-element.45), channel_id=1, source_target_pairs={{0,12},{1,13},{2,14},{3,15},{4,0},{5,1},{6,2},{7,3},{8,4},{9,5},{1... | collective-permute-start | bytes 3145736 | tf_op jit(solution)/shard_map/ppermute | solution.py:40
  41.2 9.7 %collective-permute-done.9.refs_1_.refs_3_ = f32[2,3,32,1024]{3,2,1,0:T(8,128)S(1)} collective-permute-done((f32[2,3,32,1024]{3,2,1,0:T(8,128)S(1)}, f32[2,3,32,1024]{3,2,1,0:T(8,128)S(1)}, u32[]{:S(2)}, u32[]{:S(2)}) %collective-permute-start.9) | collective-permute-done | bytes 786464 | tf_op jit(solution)/shard_map/ppermute | solution.py:40
  50.9 3.0 %collective-permute-start.2 = (s32[1,8]{1,0:T(1,128)S(1)}, s32[1,8]{1,0:T(1,128)S(1)}, u32[]{:S(2)}, u32[]{:S(2)}) collective-permute-start(s32[1,8]{1,0:T(1,128)S(1)} %get-tuple-element.41), channel_id=1, source_target_pairs={{0,2},{1,3},{2,0},{3,1},{4,6},{5,7},{6,4},{7,5},{8,10},{9,11},{10,... | collective-permute-start | bytes 104 | tf_op jit(solution)/shard_map/ppermute | solution.py:40
  53.9 2.0 %collective-permute-done.2.refs_3_.other_held = s32[1,8]{1,0:T(1,128)S(1)} collective-permute-done((s32[1,8]{1,0:T(1,128)S(1)}, s32[1,8]{1,0:T(1,128)S(1)}, u32[]{:S(2)}, u32[]{:S(2)}) %collective-permute-start.2) | collective-permute-done | bytes 64 | tf_op jit(solution)/shard_map/ppermute | solution.py:40
  55.9 3.2 %collective-permute-start.12 = (f32[2,2,16,4096]{3,2,1,0:T(8,128)S(1)}, f32[2,2,16,4096]{3,2,1,0:T(8,128)S(1)}, u32[]{:S(2)}, u32[]{:S(2)}) collective-permute-start(f32[2,2,16,4096]{3,2,1,0:T(8,128)S(1)} %get-tuple-element.52), channel_id=1, source_target_pairs={{0,12},{1,13},{2,14},{3,15},{4,0},{5,1},{6,2},{7,3},{8,4},{9,5},{1... | collective-permute-start | bytes 3145736 | tf_op jit(solution)/shard_map/ppermute | solution.py:40
  59.3 1.6 %collective-permute-start.13 = (f32[2,3,32,1024]{3,2,1,0:T(8,128)S(1)}, f32[2,3,32,1024]{3,2,1,0:T(8,128)S(1)}, u32[]{:S(2)}, u32[]{:S(2)}) collective-permute-start(f32[2,3,32,1024]{3,2,1,0:T(8,128)S(1)} %other_side.2.refs_1_), channel_id=1, source_target_pairs={{0,64},{1,65},{2,66},{3,67},{4,68},{5,69},{6,70},{7,71},{8,72},{9,... | collective-permute-start | bytes 2359304 | tf_op jit(solution)/shard_map/ppermute | solution.py:40
  61.4 3.5 %collective-permute-done.5.below = f32[2,2,16,4096]{3,2,1,0:T(8,128)S(1)} collective-permute-done((f32[2,2,16,4096]{3,2,1,0:T(8,128)S(1)}, f32[2,2,16,4096]{3,2,1,0:T(8,128)S(1)}, u32[]{:S(2)}, u32[]{:S(2)}) %collective-permute-start.5) | collective-permute-done | bytes 1048608 | tf_op jit(solution)/shard_map/ppermute | solution.py:40
  66.3 3.1 %collective-permute-start.15 = (f32[16,8192]{1,0:T(8,128)S(1)}, f32[16,8192]{1,0:T(8,128)S(1)}, u32[]{:S(2)}, u32[]{:S(2)}) collective-permute-start(f32[16,8192]{1,0:T(8,128)S(1)} %get-tuple-element.54), channel_id=1, source_target_pairs={{0,2},{1,3},{2,0},{3,1},{4,6},{5,7},{6,4},{7,5},{8,10},{9,11},{10,... | collective-permute-start | bytes 1572872 | tf_op jit(solution)/shard_map/ppermute | solution.py:40
  69.5 8.6 %collective-permute-done.13.refs_0_.refs_5_ = f32[2,3,32,1024]{3,2,1,0:T(8,128)S(1)} collective-permute-done((f32[2,3,32,1024]{3,2,1,0:T(8,128)S(1)}, f32[2,3,32,1024]{3,2,1,0:T(8,128)S(1)}, u32[]{:S(2)}, u32[]{:S(2)}) %collective-permute-start.13) | collective-permute-done | bytes 786464 | tf_op jit(solution)/shard_map/ppermute | solution.py:40
  78.1 2.5 %collective-permute-start.22 = (f32[4,16,1024]{2,1,0:T(8,128)S(1)}, f32[4,16,1024]{2,1,0:T(8,128)S(1)}, u32[]{:S(2)}, u32[]{:S(2)}) collective-permute-start(f32[4,16,1024]{2,1,0:T(8,128)S(1)} %get-tuple-element.66), channel_id=1, source_target_pairs={{0,64},{1,65},{2,66},{3,67},{4,68},{5,69},{6,70},{7,71},{8,72},{9,... | collective-permute-start | bytes 786440 | tf_op jit(solution)/shard_map/ppermute | solution.py:40
  80.5 5.3 %collective-permute-done.11.below = f32[2,2,16,4096]{3,2,1,0:T(8,128)S(1)} collective-permute-done((f32[2,2,16,4096]{3,2,1,0:T(8,128)S(1)}, f32[2,2,16,4096]{3,2,1,0:T(8,128)S(1)}, u32[]{:S(2)}, u32[]{:S(2)}) %collective-permute-start.11) | collective-permute-done | bytes 1048608 | tf_op jit(solution)/shard_map/ppermute | solution.py:40
  87.4 3.5 %collective-permute-start.16 = (f32[16,8192]{1,0:T(8,128)S(1)}, f32[16,8192]{1,0:T(8,128)S(1)}, u32[]{:S(2)}, u32[]{:S(2)}) collective-permute-start(f32[16,8192]{1,0:T(8,128)S(1)} %get-tuple-element.55), channel_id=1, source_target_pairs={{0,2},{1,3},{2,0},{3,1},{4,6},{5,7},{6,4},{7,5},{8,10},{9,11},{10,... | collective-permute-start | bytes 1572872 | tf_op jit(solution)/shard_map/ppermute | solution.py:40
  90.9 1.8 %collective-permute-start.23 = (f32[4,16,1024]{2,1,0:T(8,128)S(1)}, f32[4,16,1024]{2,1,0:T(8,128)S(1)}, u32[]{:S(2)}, u32[]{:S(2)}) collective-permute-start(f32[4,16,1024]{2,1,0:T(8,128)S(1)} %get-tuple-element.67), channel_id=1, source_target_pairs={{0,66},{1,67},{2,64},{3,65},{4,70},{5,71},{6,68},{7,69},{8,74},{9,... | collective-permute-start | bytes 786440 | tf_op jit(solution)/shard_map/ppermute | solution.py:40
  92.6 10.7 %collective-permute-done.22.beside = f32[4,16,1024]{2,1,0:T(8,128)S(1)} collective-permute-done((f32[4,16,1024]{2,1,0:T(8,128)S(1)}, f32[4,16,1024]{2,1,0:T(8,128)S(1)}, u32[]{:S(2)}, u32[]{:S(2)}) %collective-permute-start.22) | collective-permute-done | bytes 262176 | tf_op jit(solution)/shard_map/ppermute | solution.py:40
  103.3 3.6 %collective-permute-start.18 = (f32[4,16,1024]{2,1,0:T(8,128)S(1)}, f32[4,16,1024]{2,1,0:T(8,128)S(1)}, u32[]{:S(2)}, u32[]{:S(2)}) collective-permute-start(f32[4,16,1024]{2,1,0:T(8,128)S(1)} %get-tuple-element.61), channel_id=1, source_target_pairs={{0,66},{1,67},{2,64},{3,65},{4,70},{5,71},{6,68},{7,69},{8,74},{9,... | collective-permute-start | bytes 786440 | tf_op jit(solution)/shard_map/ppermute | solution.py:40
  109.0 4.6 %collective-permute-start.24 = (f32[2,16,1024]{2,1,0:T(8,128)S(1)}, f32[2,16,1024]{2,1,0:T(8,128)S(1)}, u32[]{:S(2)}, u32[]{:S(2)}) collective-permute-start(f32[2,16,1024]{2,1,0:T(8,128)S(1)} %get-tuple-element.69), channel_id=1, source_target_pairs={{0,16},{1,17},{2,18},{3,19},{4,20},{5,21},{6,22},{7,23},{8,24},{9,... | collective-permute-start | bytes 393224 | tf_op jit(solution)/shard_map/ppermute | solution.py:40
  113.6 3.7 %collective-permute-start.26 = (f32[2,16,1024]{2,1,0:T(8,128)S(1)}, f32[2,16,1024]{2,1,0:T(8,128)S(1)}, u32[]{:S(2)}, u32[]{:S(2)}) collective-permute-start(f32[2,16,1024]{2,1,0:T(8,128)S(1)} %get-tuple-element.71), channel_id=1, source_target_pairs={{0,48},{1,49},{2,50},{3,51},{4,52},{5,53},{6,54},{7,55},{8,56},{9,... | collective-permute-start | bytes 393224 | tf_op jit(solution)/shard_map/ppermute | solution.py:40
  119.2 5.1 %collective-permute-start.20 = (f32[2,16,1024]{2,1,0:T(8,128)S(1)}, f32[2,16,1024]{2,1,0:T(8,128)S(1)}, u32[]{:S(2)}, u32[]{:S(2)}) collective-permute-start(f32[2,16,1024]{2,1,0:T(8,128)S(1)} %get-tuple-element.64), channel_id=1, source_target_pairs={{0,32},{1,33},{2,34},{3,35},{4,36},{5,37},{6,38},{7,39},{8,40},{9,... | collective-permute-start | bytes 393224 | tf_op jit(solution)/shard_map/ppermute | solution.py:40
  124.3 1.6 %collective-permute-start.21 = (f32[2,16,1024]{2,1,0:T(8,128)S(1)}, f32[2,16,1024]{2,1,0:T(8,128)S(1)}, u32[]{:S(2)}, u32[]{:S(2)}) collective-permute-start(f32[2,16,1024]{2,1,0:T(8,128)S(1)} %get-tuple-element.65), channel_id=1, source_target_pairs={{0,48},{1,49},{2,50},{3,51},{4,52},{5,53},{6,54},{7,55},{8,56},{9,... | collective-permute-start | bytes 393224 | tf_op jit(solution)/shard_map/ppermute | solution.py:40
  126.0 2.5 %encode_0.1.refs_11_ = f32[4,3,32,1024]{3,2,1,0:T(8,128)} custom-call(f32[4,8]{1,0:T(4,128)S(1)} %copy-done.4, f32[1,3,32,1024]{3,2,1,0:T(8,128)S(1)} %get-tuple-element.59.refs_0_, f32[2,3,32,1024]{3,2,1,0:T(8,128)S(1)} %collective-permute-done.8.refs_0_.refs_1_, f32[2,3,32,1024]{3,2,1,0:T(8,128)S(1)} %collective-permute-done.7.refs_0_.refs_2_, ...), custom_call_target="tpu_custom_call" | custom-call | tf_op jit(solution)/shard_map/encode_0/pallas_call | solution.py:44
  128.4 2.8 %update.1 = (f32[1,32,8192]{2,1,0:T(8,128)}, f32[1,32,8192]{2,1,0:T(8,128)}, f32[1,32,8192]{2,1,0:T(8,128)}) custom-call(f32[1,32,8192]{2,1,0:T(8,128)S(1)} %copy-done, f32[1,32,8192]{2,1,0:T(8,128)S(1)} %copy-done.1, f32[1,32,8192]{2,1,0:T(8,128)S(1)} %copy-done.2, f32[16,8192]{1,0:T(8,128)S(1)} %get-tuple-element.50.mine_0.mine, ...), custom_call_target="tpu_custom_call" | custom-call | tf_op jit(solution)/shard_map/update/pallas_call | solution.py:44
  131.2 2.5 %encode_1.1 = f32[4,3,32,1024]{3,2,1,0:T(8,128)} custom-call(f32[4,8]{1,0:T(4,128)S(1)} %copy-done.4, f32[1,3,32,1024]{3,2,1,0:T(8,128)S(1)} %get-tuple-element.59.refs_0_, f32[2,3,32,1024]{3,2,1,0:T(8,128)S(1)} %collective-permute-done.8.refs_0_.refs_1_, ...), custom_call_target="tpu_custom_call", output_to_operand_aliasing={{}: (12, {})} | custom-call | tf_op jit(solution)/shard_map/encode_1/pallas_call | solution.py:44
  (52 shorter events, 12.2 us)
Async XLA Ops:
  3.2 4.2 %collective-permute-start = (f32[2,32,8192]{2,1,0:T(8,128)S(1)}, f32[2,32,8192]{2,1,0:T(8,128)S(1)}, u32[]{:S(2)}, u32[]{:S(2)}) collective-permute-start(f32[2,32,8192]{2,1,0:T(8,128)S(1)} %widen_far.1.far), channel_id=1, source_target_pairs={{0,1},{1,0},{2,3},{3,2},{4,5},{5,4},{6,7},{7,6},{8,9},{9,8},{10,11... | collective-permute-start | bytes 6291464 | tf_op jit(solution)/shard_map/ppermute | solution.py:40
  7.4 4.7 %copy-start = (f32[1,32,8192]{2,1,0:T(8,128)S(1)}, f32[1,32,8192]{2,1,0:T(8,128)}, u32[]{:S(2)}) copy-start(f32[1,32,8192]{2,1,0:T(8,128)} %weight.5) | copy-start | bytes 3145732
  7.4 4.7 %copy-start.1 = (f32[1,32,8192]{2,1,0:T(8,128)S(1)}, f32[1,32,8192]{2,1,0:T(8,128)}, u32[]{:S(2)}) copy-start(f32[1,32,8192]{2,1,0:T(8,128)} %first.5) | copy-start | bytes 3145732
  7.4 4.7 %copy-start.2 = (f32[1,32,8192]{2,1,0:T(8,128)S(1)}, f32[1,32,8192]{2,1,0:T(8,128)}, u32[]{:S(2)}) copy-start(f32[1,32,8192]{2,1,0:T(8,128)} %second.5) | copy-start | bytes 3145732
  7.4 4.7 %copy-start.3 = (s32[1,8]{1,0:T(1,128)S(1)}, s32[1,8]{1,0:T(1,128)}, u32[]{:S(2)}) copy-start(s32[1,8]{1,0:T(1,128)} %holder.7) | copy-start | bytes 100
  7.7 10.2 %collective-permute-start.1 = (f32[6,32,8192]{2,1,0:T(8,128)S(1)}, f32[6,32,8192]{2,1,0:T(8,128)S(1)}, u32[]{:S(2)}, u32[]{:S(2)}) collective-permute-start(f32[6,32,8192]{2,1,0:T(8,128)S(1)} %get-tuple-element.40), channel_id=1, source_target_pairs={{0,1},{1,0},{2,3},{3,2},{4,5},{5,4},{6,7},{7,6},{8,9},{9,8},{10,11... | collective-permute-start | bytes 18874376 | tf_op jit(solution)/shard_map/ppermute | solution.py:40
  8.0 27.7 %collective-permute-start.3 = (f32[2,32,4096]{2,1,0:T(8,128)S(1)}, f32[2,32,4096]{2,1,0:T(8,128)S(1)}, u32[]{:S(2)}, u32[]{:S(2)}) collective-permute-start(f32[2,32,4096]{2,1,0:T(8,128)S(1)} %get-tuple-element.42.refs_0_), channel_id=1, source_target_pairs={{0,4},{1,5},{2,6},{3,7},{4,8},{5,9},{6,10},{7,11},{8,12},{9,13},{1... | collective-permute-start | bytes 3145736 | tf_op jit(solution)/shard_map/ppermute | solution.py:40
  10.0 27.2 %collective-permute-start.4 = (f32[2,32,4096]{2,1,0:T(8,128)S(1)}, f32[2,32,4096]{2,1,0:T(8,128)S(1)}, u32[]{:S(2)}, u32[]{:S(2)}) collective-permute-start(f32[2,32,4096]{2,1,0:T(8,128)S(1)} %get-tuple-element.43), channel_id=1, source_target_pairs={{0,12},{1,13},{2,14},{3,15},{4,0},{5,1},{6,2},{7,3},{8,4},{9,5},{1... | collective-permute-start | bytes 3145736 | tf_op jit(solution)/shard_map/ppermute | solution.py:40
  13.9 23.8 %collective-permute-start.8 = (f32[2,3,32,1024]{3,2,1,0:T(8,128)S(1)}, f32[2,3,32,1024]{3,2,1,0:T(8,128)S(1)}, u32[]{:S(2)}, u32[]{:S(2)}) collective-permute-start(f32[2,3,32,1024]{3,2,1,0:T(8,128)S(1)} %get-tuple-element.47), channel_id=1, source_target_pairs={{0,16},{1,17},{2,18},{3,19},{4,20},{5,21},{6,22},{7,23},{8,24},{9,... | collective-permute-start | bytes 2359304 | tf_op jit(solution)/shard_map/ppermute | solution.py:40
  15.5 35.4 %collective-permute-start.9 = (f32[2,3,32,1024]{3,2,1,0:T(8,128)S(1)}, f32[2,3,32,1024]{3,2,1,0:T(8,128)S(1)}, u32[]{:S(2)}, u32[]{:S(2)}) collective-permute-start(f32[2,3,32,1024]{3,2,1,0:T(8,128)S(1)} %get-tuple-element.48), channel_id=1, source_target_pairs={{0,48},{1,49},{2,50},{3,51},{4,52},{5,53},{6,54},{7,55},{8,56},{9,... | collective-permute-start | bytes 2359304 | tf_op jit(solution)/shard_map/ppermute | solution.py:40
  19.7 39.5 %collective-permute-start.7 = (f32[2,3,32,1024]{3,2,1,0:T(8,128)S(1)}, f32[2,3,32,1024]{3,2,1,0:T(8,128)S(1)}, u32[]{:S(2)}, u32[]{:S(2)}) collective-permute-start(f32[2,3,32,1024]{3,2,1,0:T(8,128)S(1)} %get-tuple-element.46), channel_id=1, source_target_pairs={{0,32},{1,33},{2,34},{3,35},{4,36},{5,37},{6,38},{7,39},{8,40},{9,... | collective-permute-start | bytes 2359304 | tf_op jit(solution)/shard_map/ppermute | solution.py:40
  35.7 20.2 %collective-permute-start.10 = (f32[1,3,32,1024]{3,2,1,0:T(8,128)S(1)}, f32[1,3,32,1024]{3,2,1,0:T(8,128)S(1)}, u32[]{:S(2)}, u32[]{:S(2)}) collective-permute-start(f32[1,3,32,1024]{3,2,1,0:T(8,128)S(1)} %get-tuple-element.49), channel_id=1, source_target_pairs={{0,64},{1,65},{2,66},{3,67},{4,68},{5,69},{6,70},{7,71},{8,72},{9,... | collective-permute-start | bytes 1179656 | tf_op jit(solution)/shard_map/ppermute | solution.py:40
  37.5 27.4 %collective-permute-start.5 = (f32[2,2,16,4096]{3,2,1,0:T(8,128)S(1)}, f32[2,2,16,4096]{3,2,1,0:T(8,128)S(1)}, u32[]{:S(2)}, u32[]{:S(2)}) collective-permute-start(f32[2,2,16,4096]{3,2,1,0:T(8,128)S(1)} %get-tuple-element.44.refs_2_), channel_id=1, source_target_pairs={{0,4},{1,5},{2,6},{3,7},{4,8},{5,9},{6,10},{7,11},{8,12},{9,13},{1... | collective-permute-start | bytes 3145736 | tf_op jit(solution)/shard_map/ppermute | solution.py:40
  37.6 27.8 %collective-permute-start.6 = (f32[2,2,16,4096]{3,2,1,0:T(8,128)S(1)}, f32[2,2,16,4096]{3,2,1,0:T(8,128)S(1)}, u32[]{:S(2)}, u32[]{:S(2)}) collective-permute-start(f32[2,2,16,4096]{3,2,1,0:T(8,128)S(1)} %get-tuple-element.45), channel_id=1, source_target_pairs={{0,12},{1,13},{2,14},{3,15},{4,0},{5,1},{6,2},{7,3},{8,4},{9,5},{1... | collective-permute-start | bytes 3145736 | tf_op jit(solution)/shard_map/ppermute | solution.py:40
  50.9 5.0 %collective-permute-start.2 = (s32[1,8]{1,0:T(1,128)S(1)}, s32[1,8]{1,0:T(1,128)S(1)}, u32[]{:S(2)}, u32[]{:S(2)}) collective-permute-start(s32[1,8]{1,0:T(1,128)S(1)} %get-tuple-element.41), channel_id=1, source_target_pairs={{0,2},{1,3},{2,0},{3,1},{4,6},{5,7},{6,4},{7,5},{8,10},{9,11},{10,... | collective-permute-start | bytes 104 | tf_op jit(solution)/shard_map/ppermute | solution.py:40
  55.9 29.9 %collective-permute-start.11 = (f32[2,2,16,4096]{3,2,1,0:T(8,128)S(1)}, f32[2,2,16,4096]{3,2,1,0:T(8,128)S(1)}, u32[]{:S(2)}, u32[]{:S(2)}) collective-permute-start(f32[2,2,16,4096]{3,2,1,0:T(8,128)S(1)} %get-tuple-element.51), channel_id=1, source_target_pairs={{0,4},{1,5},{2,6},{3,7},{4,8},{5,9},{6,10},{7,11},{8,12},{9,13},{1... | collective-permute-start | bytes 3145736 | tf_op jit(solution)/shard_map/ppermute | solution.py:40
  55.9 29.9 %collective-permute-start.12 = (f32[2,2,16,4096]{3,2,1,0:T(8,128)S(1)}, f32[2,2,16,4096]{3,2,1,0:T(8,128)S(1)}, u32[]{:S(2)}, u32[]{:S(2)}) collective-permute-start(f32[2,2,16,4096]{3,2,1,0:T(8,128)S(1)} %get-tuple-element.52), channel_id=1, source_target_pairs={{0,12},{1,13},{2,14},{3,15},{4,0},{5,1},{6,2},{7,3},{8,4},{9,5},{1... | collective-permute-start | bytes 3145736 | tf_op jit(solution)/shard_map/ppermute | solution.py:40
  59.3 18.8 %collective-permute-start.13 = (f32[2,3,32,1024]{3,2,1,0:T(8,128)S(1)}, f32[2,3,32,1024]{3,2,1,0:T(8,128)S(1)}, u32[]{:S(2)}, u32[]{:S(2)}) collective-permute-start(f32[2,3,32,1024]{3,2,1,0:T(8,128)S(1)} %other_side.2.refs_1_), channel_id=1, source_target_pairs={{0,64},{1,65},{2,66},{3,67},{4,68},{5,69},{6,70},{7,71},{8,72},{9,... | collective-permute-start | bytes 2359304 | tf_op jit(solution)/shard_map/ppermute | solution.py:40
  64.9 21.6 %collective-permute-start.14 = (f32[1,3,32,1024]{3,2,1,0:T(8,128)S(1)}, f32[1,3,32,1024]{3,2,1,0:T(8,128)S(1)}, u32[]{:S(2)}, u32[]{:S(2)}) collective-permute-start(f32[1,3,32,1024]{3,2,1,0:T(8,128)S(1)} %other_side.3.refs_0_), channel_id=1, source_target_pairs={{0,64},{1,65},{2,66},{3,67},{4,68},{5,69},{6,70},{7,71},{8,72},{9,... | collective-permute-start | bytes 1179656 | tf_op jit(solution)/shard_map/ppermute | solution.py:40
  66.3 42.0 %collective-permute-start.15 = (f32[16,8192]{1,0:T(8,128)S(1)}, f32[16,8192]{1,0:T(8,128)S(1)}, u32[]{:S(2)}, u32[]{:S(2)}) collective-permute-start(f32[16,8192]{1,0:T(8,128)S(1)} %get-tuple-element.54), channel_id=1, source_target_pairs={{0,2},{1,3},{2,0},{3,1},{4,6},{5,7},{6,4},{7,5},{8,10},{9,11},{10,... | collective-permute-start | bytes 1572872 | tf_op jit(solution)/shard_map/ppermute | solution.py:40
  78.1 47.9 %copy-start.4 = (f32[4,8]{1,0:T(4,128)S(1)}, f32[4,8]{1,0:T(4,128)}, u32[]{:S(2)}) copy-start(f32[4,8]{1,0:T(4,128)} %code.3) | copy-start | bytes 388
  78.1 25.2 %collective-permute-start.22 = (f32[4,16,1024]{2,1,0:T(8,128)S(1)}, f32[4,16,1024]{2,1,0:T(8,128)S(1)}, u32[]{:S(2)}, u32[]{:S(2)}) collective-permute-start(f32[4,16,1024]{2,1,0:T(8,128)S(1)} %get-tuple-element.66), channel_id=1, source_target_pairs={{0,64},{1,65},{2,66},{3,67},{4,68},{5,69},{6,70},{7,71},{8,72},{9,... | collective-permute-start | bytes 786440 | tf_op jit(solution)/shard_map/ppermute | solution.py:40
  87.4 31.1 %collective-permute-start.16 = (f32[16,8192]{1,0:T(8,128)S(1)}, f32[16,8192]{1,0:T(8,128)S(1)}, u32[]{:S(2)}, u32[]{:S(2)}) collective-permute-start(f32[16,8192]{1,0:T(8,128)S(1)} %get-tuple-element.55), channel_id=1, source_target_pairs={{0,2},{1,3},{2,0},{3,1},{4,6},{5,7},{6,4},{7,5},{8,10},{9,11},{10,... | collective-permute-start | bytes 1572872 | tf_op jit(solution)/shard_map/ppermute | solution.py:40
  90.9 17.5 %collective-permute-start.23 = (f32[4,16,1024]{2,1,0:T(8,128)S(1)}, f32[4,16,1024]{2,1,0:T(8,128)S(1)}, u32[]{:S(2)}, u32[]{:S(2)}) collective-permute-start(f32[4,16,1024]{2,1,0:T(8,128)S(1)} %get-tuple-element.67), channel_id=1, source_target_pairs={{0,66},{1,67},{2,64},{3,65},{4,70},{5,71},{6,68},{7,69},{8,74},{9,... | collective-permute-start | bytes 786440 | tf_op jit(solution)/shard_map/ppermute | solution.py:40
  92.6 20.9 %collective-permute-start.17 = (f32[4,16,1024]{2,1,0:T(8,128)S(1)}, f32[4,16,1024]{2,1,0:T(8,128)S(1)}, u32[]{:S(2)}, u32[]{:S(2)}) collective-permute-start(f32[4,16,1024]{2,1,0:T(8,128)S(1)} %get-tuple-element.60), channel_id=1, source_target_pairs={{0,64},{1,65},{2,66},{3,67},{4,68},{5,69},{6,70},{7,71},{8,72},{9,... | collective-permute-start | bytes 786440 | tf_op jit(solution)/shard_map/ppermute | solution.py:40
  103.3 15.2 %collective-permute-start.18 = (f32[4,16,1024]{2,1,0:T(8,128)S(1)}, f32[4,16,1024]{2,1,0:T(8,128)S(1)}, u32[]{:S(2)}, u32[]{:S(2)}) collective-permute-start(f32[4,16,1024]{2,1,0:T(8,128)S(1)} %get-tuple-element.61), channel_id=1, source_target_pairs={{0,66},{1,67},{2,64},{3,65},{4,70},{5,71},{6,68},{7,69},{8,74},{9,... | collective-permute-start | bytes 786440 | tf_op jit(solution)/shard_map/ppermute | solution.py:40
  109.0 15.4 %collective-permute-start.24 = (f32[2,16,1024]{2,1,0:T(8,128)S(1)}, f32[2,16,1024]{2,1,0:T(8,128)S(1)}, u32[]{:S(2)}, u32[]{:S(2)}) collective-permute-start(f32[2,16,1024]{2,1,0:T(8,128)S(1)} %get-tuple-element.69), channel_id=1, source_target_pairs={{0,16},{1,17},{2,18},{3,19},{4,20},{5,21},{6,22},{7,23},{8,24},{9,... | collective-permute-start | bytes 393224 | tf_op jit(solution)/shard_map/ppermute | solution.py:40
  113.6 12.4 %collective-permute-start.25 = (f32[2,16,1024]{2,1,0:T(8,128)S(1)}, f32[2,16,1024]{2,1,0:T(8,128)S(1)}, u32[]{:S(2)}, u32[]{:S(2)}) collective-permute-start(f32[2,16,1024]{2,1,0:T(8,128)S(1)} %get-tuple-element.70), channel_id=1, source_target_pairs={{0,32},{1,33},{2,34},{3,35},{4,36},{5,37},{6,38},{7,39},{8,40},{9,... | collective-permute-start | bytes 393224 | tf_op jit(solution)/shard_map/ppermute | solution.py:40
  113.6 12.4 %collective-permute-start.26 = (f32[2,16,1024]{2,1,0:T(8,128)S(1)}, f32[2,16,1024]{2,1,0:T(8,128)S(1)}, u32[]{:S(2)}, u32[]{:S(2)}) collective-permute-start(f32[2,16,1024]{2,1,0:T(8,128)S(1)} %get-tuple-element.71), channel_id=1, source_target_pairs={{0,48},{1,49},{2,50},{3,51},{4,52},{5,53},{6,54},{7,55},{8,56},{9,... | collective-permute-start | bytes 393224 | tf_op jit(solution)/shard_map/ppermute | solution.py:40
  119.1 12.1 %collective-permute-start.19 = (f32[2,16,1024]{2,1,0:T(8,128)S(1)}, f32[2,16,1024]{2,1,0:T(8,128)S(1)}, u32[]{:S(2)}, u32[]{:S(2)}) collective-permute-start(f32[2,16,1024]{2,1,0:T(8,128)S(1)} %get-tuple-element.63), channel_id=1, source_target_pairs={{0,16},{1,17},{2,18},{3,19},{4,20},{5,21},{6,22},{7,23},{8,24},{9,... | collective-permute-start | bytes 393224 | tf_op jit(solution)/shard_map/ppermute | solution.py:40
  119.2 12.0 %collective-permute-start.20 = (f32[2,16,1024]{2,1,0:T(8,128)S(1)}, f32[2,16,1024]{2,1,0:T(8,128)S(1)}, u32[]{:S(2)}, u32[]{:S(2)}) collective-permute-start(f32[2,16,1024]{2,1,0:T(8,128)S(1)} %get-tuple-element.64), channel_id=1, source_target_pairs={{0,32},{1,33},{2,34},{3,35},{4,36},{5,37},{6,38},{7,39},{8,40},{9,... | collective-permute-start | bytes 393224 | tf_op jit(solution)/shard_map/ppermute | solution.py:40
  124.3 6.9 %collective-permute-start.21 = (f32[2,16,1024]{2,1,0:T(8,128)S(1)}, f32[2,16,1024]{2,1,0:T(8,128)S(1)}, u32[]{:S(2)}, u32[]{:S(2)}) collective-permute-start(f32[2,16,1024]{2,1,0:T(8,128)S(1)} %get-tuple-element.65), channel_id=1, source_target_pairs={{0,48},{1,49},{2,50},{3,51},{4,52},{5,53},{6,54},{7,55},{8,56},{9,... | collective-permute-start | bytes 393224 | tf_op jit(solution)/shard_map/ppermute | solution.py:40
  (2 other events, 2.6 us)

commit v3 on v2

--- a/solution.py
+++ b/solution.py
@@ -188,8 +188,10 @@
 
 
 def gathered_z(own, rest, holder, below, above, c, after):
+    count = 2 - c
+
     def body(own, rest, mine_held, other_held, below, above, *refs):
-        mine, theirs, beside, corner = refs[len(after) :]
+        mine, near, beside, corner, theirs = refs[len(after) :]
         rows = pl.ds(16 * c, 16)
         for j, out in enumerate((mine, theirs)):
 
@@ -203,57 +205,56 @@
             by_tiles(4096, 512, add)
         for s in range(4):
             beside[s] = mine[:, pl.ds(column_of(mine_held, 1, s), 1024)]
-            corner[s] = theirs[:, pl.ds(column_of(other_held, 1, s), 1024)]
-
-    rows = ((16, 8192), F32, VMEM)
+            near[s] = theirs[:, pl.ds(column_of(other_held, 0, s), 1024)]
+            others = theirs[:, pl.ds(column_of(other_held, 1, s), 1024)]
+            corner[s] = others
+            if count == 2:
+                near[4 + s] = others
+
     parts = ((4, 16, 1024), F32, VMEM)
     return call(
         f"gathered_z_{c}",
         body,
         [(own, VMEM), (rest, VMEM), (holder[0], SMEM), (holder[1], SMEM), (below, VMEM), (above, VMEM)]
         + [(array, VMEM) for array in after],
-        [rows, rows, parts, parts],
-    )
-
-
-def for_holders(holder, mine, across, beside, corner, after=()):
-    def body(holder, mine, across, beside, corner, *refs):
-        outs = refs[len(after) :]
+        [((16, 8192), F32, VMEM), ((4 * count, 16, 1024), F32, VMEM), parts, parts],
+        [pltpu.VMEM((16, 8192), F32)],
+    )
+
+
+def for_holders(holder, mine, near, beside, corner, after):
+    def body(holder, mine, near, beside, corner, after, *outs):
         for s in range(4):
-            columns = pl.ds(column_of(holder, 0, s), 1024)
-            outs[s][0] = mine[:, columns] + across[:, columns]
+            outs[s][0] = mine[:, pl.ds(column_of(holder, 0, s), 1024)] + near[s]
             outs[s][1] = beside[s] + corner[s]
 
     return call(
         "for_holders",
         body,
-        [(holder, SMEM)] + [(array, VMEM) for array in (mine, across, beside, corner, *after)],
+        [(holder, SMEM)] + [(array, VMEM) for array in (mine, near, beside, corner, after)],
         [((2, 16, 1024), F32, VMEM)] * 4,
     )
 
 
 def old_parts(name, holder, states, asked, after):
     def body(holder, weight, first, second, *refs):
-        outs, same, sems = refs[len(after) : -2], refs[-2], refs[-1]
-        copies = []
+        outs = refs[len(after) :]
         for out, steps in zip(outs, asked):
             for i, (a, s) in enumerate(steps):
-                columns = pl.ds(column_of(holder, a, s), 1024)
-                for k, old in enumerate((weight, first, second)):
-                    copies.append(pltpu.make_async_copy(old.at[0, :, columns], out.at[i, k], sems.at[len(copies)]))
-        for copy in copies:
-            copy.start()
-        for i in range(8):
-            same[0, i] = holder[0, i]
-        for copy in copies:
-            copy.wait()
+                start = column_of(holder, a, s)
+
+                def copy(columns):
+                    source = pl.ds(pl.multiple_of(start + columns.start, 128), columns.size)
+                    for k, old in enumerate((weight, first, second)):
+                        out[i, k, :, columns] = old[0, :, source]
+
+                by_tiles(1024, 256, copy)
 
     return call(
         name,
         body,
-        [(holder, SMEM)] + [(old, HBM) for old in states] + [(array, VMEM) for array in after],
-        [((len(steps), 3, 32, 1024), F32, VMEM) for steps in asked] + [((1, 8), jnp.int32, SMEM)],
-        [pltpu.SemaphoreType.DMA((3 * sum(len(steps) for steps in asked),))],
+        [(holder, SMEM)] + [(old, VMEM) for old in states] + [(array, VMEM) for array in after],
+        [((len(steps), 3, 32, 1024), F32, VMEM) for steps in asked],
     )
 
 
@@ -285,26 +286,20 @@
     return weight - 0.01 * (step + 0.1 * weight), first_new, second_new
 
 
-def update(weight, first, second, mine, across):
-    def body(weight, first, second, mine_0, mine_1, across_0, across_1, *refs):
-        outs, read, sems = refs[:3], refs[3], refs[4]
-        reads = [pltpu.make_async_copy(old.at[0], read.at[k], sems.at[k]) for k, old in enumerate((weight, first, second))]
-        for copy in reads:
-            copy.start()
-        for copy in reads:
-            copy.wait()
+def update(holder, weight, first, second, mine, across):
+    def body(holder, weight, first, second, mine_0, mine_1, all_0, near_1, far_1, *refs):
+        outs, made, sems = refs[:3], refs[3], refs[4]
         writes = []
-        for c, (mine, across) in enumerate(((mine_0, across_0), (mine_1, across_1))):
+        for c, mine in enumerate((mine_0, mine_1)):
             rows = pl.ds(16 * c, 16)
-
-            def step(columns):
-                new = advance(*(read[k, rows, columns] for k in range(3)), mine[:, columns] + across[:, columns])
+            for i in range(8):
+                columns = pl.ds(column_of(holder, i // 4, i % 4), 1024)
+                more = all_0[i] if c == 0 else (near_1, far_1)[i // 4][i % 4]
+                new = advance(*(old[0, rows, columns] for old in (weight, first, second)), mine[:, columns] + more)
                 for k in range(3):
-                    read[k, rows, columns] = new[k]
-
-            by_tiles(8192, 512, step)
+                    made[k, rows, columns] = new[k]
             for k in range(3):
-                copy = pltpu.make_async_copy(read.at[k, rows], outs[k].at[0, rows], sems.at[3 + 3 * c + k])
+                copy = pltpu.make_async_copy(made.at[k, rows], outs[k].at[0, rows], sems.at[3 * c + k])
                 copy.start()
                 writes.append(copy)
         for copy in writes:
@@ -313,9 +308,9 @@
     return call(
         "update",
         body,
-        [(weight, HBM), (first, HBM), (second, HBM)] + [(array, VMEM) for array in (*mine, *across)],
+        [(holder, SMEM)] + [(array, VMEM) for array in (weight, first, second, *mine, *across)],
         [((1, 32, 8192), F32, HBM)] * 3,
-        [pltpu.VMEM((3, 32, 8192), F32), pltpu.SemaphoreType.DMA((9,))],
+        [pltpu.VMEM((3, 32, 8192), F32), pltpu.SemaphoreType.DMA((6,))],
     )
 
 
@@ -330,7 +325,7 @@
             places[a][s] = (known[0] if known else len(arrays) - 1, part)
 
     def body(code, *refs):
-        olds, ins, (out, total, sem) = refs[: len(arrays)], refs[len(arrays) :], refs[-3:]
+        olds, ins, (out, total, sem) = refs[: len(arrays)], refs[len(arrays) :], (refs[-4], *refs[-2:])
         _, _, _, side, y = position()
         ranks = [[lax.rem(side + a, 2) * 4 + lax.rem(y + 4 - s, 4) for s in range(4)] for a in range(2)]
         scales = [[[code[j, ranks[a][s]] for s in range(4)] for a in range(2)] for j in range(4)]
@@ -360,15 +355,16 @@
         copy = pltpu.make_async_copy(total, out.at[:, :, pl.ds(16 * c, 16)], sem)
         copy.start()
         copy.wait()
+        refs[-3][...] = jnp.zeros((8, 128), F32)
 
     return call(
         f"encode_{c}",
         body,
         [(code, SMEM)] + [(array, VMEM) for array in (*arrays, *grads)] + ([] if into is None else [(into, HBM)]),
-        [((4, 3, 32, 1024), F32, HBM)],
+        [((4, 3, 32, 1024), F32, HBM), ((8, 128), F32, VMEM)],
         [pltpu.VMEM((4, 3, 16, 1024), F32), pltpu.SemaphoreType.DMA],
         aliases=None if into is None else {1 + len(arrays) + len(grads): 0},
-    )[0]
+    )
 
 
 def local(grad_part, weight, moment_one, moment_two, code, owner, holder):
@@ -381,39 +377,39 @@
     rest = send(rest, TO_CORE)
     far_below, far_above = send(go_up, UP_Z), send(go_down, DOWN_Z)
 
-    one, three, _ = old_parts("old_odd", holder, states, [[(0, 1), (1, 1)], [(0, 3), (1, 3)]], (go_up,))
+    one, three = old_parts("old_odd", holder, states, [[(0, 1), (1, 1)], [(0, 3), (1, 3)]], (go_up,))
     one, three = send(one, ALONG_Y[1]), send(three, ALONG_Y[3])
-    asked = [[(0, 2), (1, 2)], [(0, 0)], [(1, 0)]]
-    two, zero, beside, held = old_parts("old_even", holder, states, asked, (rest,))
+    zero, beside = old_parts("old_here", holder, states, [[(0, 0)], [(1, 0)]], (rest,))
     beside = send(beside, BESIDE)
-    two = send(two, ALONG_Y[2])
-    held = send(held, ACROSS)
-
-    go_up, go_down = onward(own, rest, far_below, far_above, 0)
+
+    held = send(holder, ACROSS)
+    odd = other_side([one, three], [(beside, VMEM), (held, SMEM)])
+    (two,) = old_parts("old_two", holder, states, [[(0, 2), (1, 2)]], (odd,))
+    after = (two,)
+    odd, two = send(odd, BESIDE), send(two, ALONG_Y[2])
+
+    go_up, go_down = onward(own, rest, far_below, far_above, 0, after)
     along_z = [(send(go_up, UP_Z), send(go_down, DOWN_Z))]
-    odd = other_side([one, three], [(go_up, VMEM)])
-    even = other_side([two], [(odd, VMEM), (beside, VMEM), (held, SMEM)])
+    even = other_side([two], [(odd, VMEM), (go_up, VMEM)])
     after = (even,)
-    odd, even = send(odd, BESIDE), send(even, BESIDE)
-    go_up, go_down = onward(own, rest, far_below, far_above, 1)
+    even = send(even, BESIDE)
+    go_up, go_down = onward(own, rest, far_below, far_above, 1, after)
     along_z.append((send(go_up, UP_Z), send(go_down, DOWN_Z)))
     old = [[(zero, 0), (one, 0), (two, 0), (three, 0)], [(beside, 0), (odd, 0), (even, 0), (odd, 1)]]
 
-    mine, across, parts = [], [], []
+    mine, across, parity = [], [], None
     for c in range(2):
-        ours, theirs, to_beside, to_corner = gathered_z(own, rest, (holder, held), *along_z[c], c, after)
-        after = (odd, even)
+        ours, near, to_beside, to_corner = gathered_z(own, rest, (holder, held), *along_z[c], c, after)
         mine.append(ours)
-        across.append(send(theirs, ACROSS))
-        parts.append((send(to_beside, BESIDE), send(to_corner, CORNER)))
-    grads = []
-    for c in range(2):
-        sums = for_holders(holder, mine[c], across[c], *parts[c], () if c else (mine[1],))
-        grads.append([sums[0]] + [send(sums[s], ALONG_Y[s]) for s in (1, 2, 3)])
-
-    new = update(*states, mine, across)
-    parity = encode(code, old, grads[0], 0)
-    parity = encode(code, old, grads[1], 1, parity)
+        across.append(send(near, ACROSS))
+        done = even if c == 0 else done
+        sums = for_holders(holder, ours, across[c], send(to_beside, BESIDE), send(to_corner, CORNER), done)
+        after = (sums[1],)
+        grads = [sums[0]] + [send(sums[s], ALONG_Y[s]) for s in (1, 2, 3)]
+        parity, done = encode(code, old, grads, c, parity)
+    across.append(send(to_corner, ACROSS))
+
+    new = update(holder, *states, mine, across)
     return (*new, parity)
 
 

time: 134 us -> 116 us (0.87)
  waiting for transfers between devices: 56.9 us -> 47.8 us
  starting transfers between devices: 53.9 us -> 46.4 us
    ppermute x27 -> x28, waiting for transfers between devices: 56.9 us -> 47.8 us  [send(): return lax.ppermute(array, AXES, pairs)]
    ppermute x27 -> x28, starting transfers between devices: 53.9 us -> 46.4 us  [send(): return lax.ppermute(array, AXES, pairs)]
    pallas_call x16 -> x17, Pallas kernels: 21.5 us -> 20.6 us  [call(): pl.pallas_call(body, out_shape=[jax.ShapeDtypeStruct(shape, kind) for sha...]
  transfers between devices with their start and end apart: 27 -> 28, of which waited for: 12 -> 13; matrix products, arithmetic and copies ran while one was open for 0% -> 0% of each run, Pallas kernels for 13% -> 13%
where the time goes in v3:
time: 116 us
  waiting for transfers between devices  47.8 us (41%)
  starting transfers between devices  46.4 us (40%)
  Pallas kernels  20.6 us (18%)
    ppermute x28, waiting for transfers between devices, send(): return lax.ppermute(array, AXES, pairs)  47.8 us
    ppermute x28, starting transfers between devices, send(): return lax.ppermute(array, AXES, pairs)  46.4 us
    pallas_call x17, Pallas kernels, call(): pl.pallas_call(body, out_shape=[jax.ShapeDtypeStruct(shape, kind) for sha...  20.6 us
  transfers between devices with their start and end apart: 28, of which 13 were waited for; matrix products, arithmetic and copies ran while one was open for 0% of the time, Pallas kernels for 13%

profile of v3, /device:TPU:0, one launch (start us, length us, event | category | flops | bytes accessed | tf_op | source)
XLA Modules:
  0.0 116.2 jit_solution(14505296120829169634)
XLA Ops:
  1.3 1.9 %widen_far.1.far = f32[2,32,8192]{2,1,0:T(8,128)S(1)} custom-call(bf16[16,32,8192]{2,1,0:T(8,128)(2,1)} %bitcast.1, s32[1,16]{1,0:T(1,128)S(1)} %copy-done.5), custom_call_target="tpu_custom_call" | custom-call | tf_op jit(solution)/shard_map/widen_far/pallas_call | solution.py:44
  3.3 3.8 %widen_rest.1 = (f32[6,32,8192]{2,1,0:T(8,128)S(1)}, bf16[8,32,8192]{2,1,0:T(8,128)(2,1)S(1)}) custom-call(bf16[16,32,8192]{2,1,0:T(8,128)(2,1)} %bitcast.2, s32[1,16]{1,0:T(1,128)S(1)} %copy-done.6, f32[2,32,8192]{2,1,0:T(8,128)S(1)} %widen_far.1.far), custom_call_target="tpu_custom_call" | custom-call | tf_op jit(solution)/shard_map/widen_rest/pallas_call | solution.py:44
  8.0 2.0 %collective-permute-start.3 = (f32[2,32,4096]{2,1,0:T(8,128)S(1)}, f32[2,32,4096]{2,1,0:T(8,128)S(1)}, u32[]{:S(2)}, u32[]{:S(2)}) collective-permute-start(f32[2,32,4096]{2,1,0:T(8,128)S(1)} %get-tuple-element.42.refs_0_), channel_id=1, source_target_pairs={{0,4},{1,5},{2,6},{3,7},{4,8},{5,9},{6,10},{7,11},{8,12},{9,13},{1... | collective-permute-start | bytes 3145736 | tf_op jit(solution)/shard_map/ppermute | solution.py:40
  10.0 2.1 %collective-permute-start.4 = (f32[2,32,4096]{2,1,0:T(8,128)S(1)}, f32[2,32,4096]{2,1,0:T(8,128)S(1)}, u32[]{:S(2)}, u32[]{:S(2)}) collective-permute-start(f32[2,32,4096]{2,1,0:T(8,128)S(1)} %get-tuple-element.43), channel_id=1, source_target_pairs={{0,12},{1,13},{2,14},{3,15},{4,0},{5,1},{6,2},{7,3},{8,4},{9,5},{1... | collective-permute-start | bytes 3145736 | tf_op jit(solution)/shard_map/ppermute | solution.py:40
  12.9 1.6 %collective-permute-start.5 = (f32[2,3,32,1024]{3,2,1,0:T(8,128)S(1)}, f32[2,3,32,1024]{3,2,1,0:T(8,128)S(1)}, u32[]{:S(2)}, u32[]{:S(2)}) collective-permute-start(f32[2,3,32,1024]{3,2,1,0:T(8,128)S(1)} %get-tuple-element.44), channel_id=1, source_target_pairs={{0,16},{1,17},{2,18},{3,19},{4,20},{5,21},{6,22},{7,23},{8,24},{9,... | collective-permute-start | bytes 2359304 | tf_op jit(solution)/shard_map/ppermute | solution.py:40
  14.5 1.7 %collective-permute-start.6 = (f32[2,3,32,1024]{3,2,1,0:T(8,128)S(1)}, f32[2,3,32,1024]{3,2,1,0:T(8,128)S(1)}, u32[]{:S(2)}, u32[]{:S(2)}) collective-permute-start(f32[2,3,32,1024]{3,2,1,0:T(8,128)S(1)} %get-tuple-element.45), channel_id=1, source_target_pairs={{0,48},{1,49},{2,50},{3,51},{4,52},{5,53},{6,54},{7,55},{8,56},{9,... | collective-permute-start | bytes 2359304 | tf_op jit(solution)/shard_map/ppermute | solution.py:40
  16.2 1.8 %collective-permute-done.1.refs_0_.rest = f32[6,32,8192]{2,1,0:T(8,128)S(1)} collective-permute-done((f32[6,32,8192]{2,1,0:T(8,128)S(1)}, f32[6,32,8192]{2,1,0:T(8,128)S(1)}, u32[]{:S(2)}, u32[]{:S(2)}) %collective-permute-start.1) | collective-permute-done | bytes 6291488 | tf_op jit(solution)/shard_map/ppermute | solution.py:40
  17.9 3.1 %collective-permute-start.2 = (s32[1,8]{1,0:T(1,128)S(1)}, s32[1,8]{1,0:T(1,128)S(1)}, u32[]{:S(2)}, u32[]{:S(2)}) collective-permute-start(s32[1,8]{1,0:T(1,128)S(1)} %copy-done.3), channel_id=1, source_target_pairs={{0,2},{1,3},{2,0},{3,1},{4,6},{5,7},{6,4},{7,5},{8,10},{9,11},{10,... | collective-permute-start | bytes 104 | tf_op jit(solution)/shard_map/ppermute | solution.py:40
  21.7 1.3 %collective-permute-done.2.refs_3_.other_held = s32[1,8]{1,0:T(1,128)S(1)} collective-permute-done((s32[1,8]{1,0:T(1,128)S(1)}, s32[1,8]{1,0:T(1,128)S(1)}, u32[]{:S(2)}, u32[]{:S(2)}) %collective-permute-start.2) | collective-permute-done | bytes 64 | tf_op jit(solution)/shard_map/ppermute | solution.py:40
  23.0 1.6 %collective-permute-start.7 = (f32[1,3,32,1024]{3,2,1,0:T(8,128)S(1)}, f32[1,3,32,1024]{3,2,1,0:T(8,128)S(1)}, u32[]{:S(2)}, u32[]{:S(2)}) collective-permute-start(f32[1,3,32,1024]{3,2,1,0:T(8,128)S(1)} %get-tuple-element.46), channel_id=1, source_target_pairs={{0,64},{1,65},{2,66},{3,67},{4,68},{5,69},{6,70},{7,71},{8,72},{9,... | collective-permute-start | bytes 1179656 | tf_op jit(solution)/shard_map/ppermute | solution.py:40
  24.5 9.1 %collective-permute-done.5.refs_0_.refs_1_ = f32[2,3,32,1024]{3,2,1,0:T(8,128)S(1)} collective-permute-done((f32[2,3,32,1024]{3,2,1,0:T(8,128)S(1)}, f32[2,3,32,1024]{3,2,1,0:T(8,128)S(1)}, u32[]{:S(2)}, u32[]{:S(2)}) %collective-permute-start.5) | collective-permute-done | bytes 786464 | tf_op jit(solution)/shard_map/ppermute | solution.py:40
  35.0 3.0 %collective-permute-start.10 = (f32[2,3,32,1024]{3,2,1,0:T(8,128)S(1)}, f32[2,3,32,1024]{3,2,1,0:T(8,128)S(1)}, u32[]{:S(2)}, u32[]{:S(2)}) collective-permute-start(f32[2,3,32,1024]{3,2,1,0:T(8,128)S(1)} %old_two.1.refs_0_), channel_id=1, source_target_pairs={{0,32},{1,33},{2,34},{3,35},{4,36},{5,37},{6,38},{7,39},{8,40},{9,... | collective-permute-start | bytes 2359304 | tf_op jit(solution)/shard_map/ppermute | solution.py:40
  37.9 1.5 %collective-permute-start.11 = (f32[2,3,32,1024]{3,2,1,0:T(8,128)S(1)}, f32[2,3,32,1024]{3,2,1,0:T(8,128)S(1)}, u32[]{:S(2)}, u32[]{:S(2)}) collective-permute-start(f32[2,3,32,1024]{3,2,1,0:T(8,128)S(1)} %other_side.2.refs_0_), channel_id=1, source_target_pairs={{0,64},{1,65},{2,66},{3,67},{4,68},{5,69},{6,70},{7,71},{8,72},{9,... | collective-permute-start | bytes 2359304 | tf_op jit(solution)/shard_map/ppermute | solution.py:40
  39.8 1.7 %collective-permute-start.8 = (f32[2,2,16,4096]{3,2,1,0:T(8,128)S(1)}, f32[2,2,16,4096]{3,2,1,0:T(8,128)S(1)}, u32[]{:S(2)}, u32[]{:S(2)}) collective-permute-start(f32[2,2,16,4096]{3,2,1,0:T(8,128)S(1)} %get-tuple-element.47.refs_2_), channel_id=1, source_target_pairs={{0,4},{1,5},{2,6},{3,7},{4,8},{5,9},{6,10},{7,11},{8,12},{9,13},{1... | collective-permute-start | bytes 3145736 | tf_op jit(solution)/shard_map/ppermute | solution.py:40
  41.5 2.5 %collective-permute-start.9 = (f32[2,2,16,4096]{3,2,1,0:T(8,128)S(1)}, f32[2,2,16,4096]{3,2,1,0:T(8,128)S(1)}, u32[]{:S(2)}, u32[]{:S(2)}) collective-permute-start(f32[2,2,16,4096]{3,2,1,0:T(8,128)S(1)} %get-tuple-element.48), channel_id=1, source_target_pairs={{0,12},{1,13},{2,14},{3,15},{4,0},{5,1},{6,2},{7,3},{8,4},{9,5},{1... | collective-permute-start | bytes 3145736 | tf_op jit(solution)/shard_map/ppermute | solution.py:40
  44.0 11.2 %collective-permute-done.10.refs_0_.refs_2_ = f32[2,3,32,1024]{3,2,1,0:T(8,128)S(1)} collective-permute-done((f32[2,3,32,1024]{3,2,1,0:T(8,128)S(1)}, f32[2,3,32,1024]{3,2,1,0:T(8,128)S(1)}, u32[]{:S(2)}, u32[]{:S(2)}) %collective-permute-start.10) | collective-permute-done | bytes 786464 | tf_op jit(solution)/shard_map/ppermute | solution.py:40
  57.4 2.5 %collective-permute-start.13 = (f32[2,2,16,4096]{3,2,1,0:T(8,128)S(1)}, f32[2,2,16,4096]{3,2,1,0:T(8,128)S(1)}, u32[]{:S(2)}, u32[]{:S(2)}) collective-permute-start(f32[2,2,16,4096]{3,2,1,0:T(8,128)S(1)} %get-tuple-element.51), channel_id=1, source_target_pairs={{0,12},{1,13},{2,14},{3,15},{4,0},{5,1},{6,2},{7,3},{8,4},{9,5},{1... | collective-permute-start | bytes 3145736 | tf_op jit(solution)/shard_map/ppermute | solution.py:40
  59.9 1.7 %collective-permute-start.17 = (f32[1,3,32,1024]{3,2,1,0:T(8,128)S(1)}, f32[1,3,32,1024]{3,2,1,0:T(8,128)S(1)}, u32[]{:S(2)}, u32[]{:S(2)}) collective-permute-start(f32[1,3,32,1024]{3,2,1,0:T(8,128)S(1)} %other_side.3.refs_0_), channel_id=1, source_target_pairs={{0,64},{1,65},{2,66},{3,67},{4,68},{5,69},{6,70},{7,71},{8,72},{9,... | collective-permute-start | bytes 1179656 | tf_op jit(solution)/shard_map/ppermute | solution.py:40
  61.6 6.4 %collective-permute-done.8.below = f32[2,2,16,4096]{3,2,1,0:T(8,128)S(1)} collective-permute-done((f32[2,2,16,4096]{3,2,1,0:T(8,128)S(1)}, f32[2,2,16,4096]{3,2,1,0:T(8,128)S(1)}, u32[]{:S(2)}, u32[]{:S(2)}) %collective-permute-start.8) | collective-permute-done | bytes 1048608 | tf_op jit(solution)/shard_map/ppermute | solution.py:40
  68.9 2.5 %collective-permute-start.14 = (f32[8,16,1024]{2,1,0:T(8,128)S(1)}, f32[8,16,1024]{2,1,0:T(8,128)S(1)}, u32[]{:S(2)}, u32[]{:S(2)}) collective-permute-start(f32[8,16,1024]{2,1,0:T(8,128)S(1)} %get-tuple-element.52), channel_id=1, source_target_pairs={{0,2},{1,3},{2,0},{3,1},{4,6},{5,7},{6,4},{7,5},{8,10},{9,11},{10,... | collective-permute-start | bytes 1572872 | tf_op jit(solution)/shard_map/ppermute | solution.py:40
  73.1 11.6 %collective-permute-done.15.beside = f32[4,16,1024]{2,1,0:T(8,128)S(1)} collective-permute-done((f32[4,16,1024]{2,1,0:T(8,128)S(1)}, f32[4,16,1024]{2,1,0:T(8,128)S(1)}, u32[]{:S(2)}, u32[]{:S(2)}) %collective-permute-start.15) | collective-permute-done | bytes 262176 | tf_op jit(solution)/shard_map/ppermute | solution.py:40
  88.5 2.2 %collective-permute-start.18 = (f32[4,16,1024]{2,1,0:T(8,128)S(1)}, f32[4,16,1024]{2,1,0:T(8,128)S(1)}, u32[]{:S(2)}, u32[]{:S(2)}) collective-permute-start(f32[4,16,1024]{2,1,0:T(8,128)S(1)} %get-tuple-element.57), channel_id=1, source_target_pairs={{0,2},{1,3},{2,0},{3,1},{4,6},{5,7},{6,4},{7,5},{8,10},{9,11},{10,... | collective-permute-start | bytes 786440 | tf_op jit(solution)/shard_map/ppermute | solution.py:40
  92.7 1.8 %collective-permute-start.23 = (f32[2,16,1024]{2,1,0:T(8,128)S(1)}, f32[2,16,1024]{2,1,0:T(8,128)S(1)}, u32[]{:S(2)}, u32[]{:S(2)}) collective-permute-start(f32[2,16,1024]{2,1,0:T(8,128)S(1)} %get-tuple-element.65), channel_id=1, source_target_pairs={{0,32},{1,33},{2,34},{3,35},{4,36},{5,37},{6,38},{7,39},{8,40},{9,... | collective-permute-start | bytes 393224 | tf_op jit(solution)/shard_map/ppermute | solution.py:40
  94.5 1.5 %collective-permute-start.24 = (f32[2,16,1024]{2,1,0:T(8,128)S(1)}, f32[2,16,1024]{2,1,0:T(8,128)S(1)}, u32[]{:S(2)}, u32[]{:S(2)}) collective-permute-start(f32[2,16,1024]{2,1,0:T(8,128)S(1)} %get-tuple-element.66), channel_id=1, source_target_pairs={{0,48},{1,49},{2,50},{3,51},{4,52},{5,53},{6,54},{7,55},{8,56},{9,... | collective-permute-start | bytes 393224 | tf_op jit(solution)/shard_map/ppermute | solution.py:40
  96.0 3.1 %collective-permute-done.23.refs_9_ = f32[2,16,1024]{2,1,0:T(8,128)S(1)} collective-permute-done((f32[2,16,1024]{2,1,0:T(8,128)S(1)}, f32[2,16,1024]{2,1,0:T(8,128)S(1)}, u32[]{:S(2)}, u32[]{:S(2)}) %collective-permute-start.23) | collective-permute-done | bytes 131104 | tf_op jit(solution)/shard_map/ppermute | solution.py:40
  99.2 2.1 %collective-permute-start.19 = (f32[4,16,1024]{2,1,0:T(8,128)S(1)}, f32[4,16,1024]{2,1,0:T(8,128)S(1)}, u32[]{:S(2)}, u32[]{:S(2)}) collective-permute-start(f32[4,16,1024]{2,1,0:T(8,128)S(1)} %get-tuple-element.58), channel_id=1, source_target_pairs={{0,2},{1,3},{2,0},{3,1},{4,6},{5,7},{6,4},{7,5},{8,10},{9,11},{10,... | collective-permute-start | bytes 786440 | tf_op jit(solution)/shard_map/ppermute | solution.py:40
  101.3 2.5 %encode_0.1 = (f32[4,3,32,1024]{3,2,1,0:T(8,128)}, f32[8,128]{1,0:T(8,128)S(1)}) custom-call(f32[4,8]{1,0:T(4,128)S(1)} %copy-done.4, f32[1,3,32,1024]{3,2,1,0:T(8,128)S(1)} %get-tuple-element.62.refs_0_, f32[2,3,32,1024]{3,2,1,0:T(8,128)S(1)} %collective-permute-done.5.refs_0_.refs_1_, f32[2,3,32,1024]{3,2,1,0:T(8,128)S(1)} %collective-permute-done.10.refs_0_.refs_2_, ...), custom_call_target="tpu_custom_call" | custom-call | tf_op jit(solution)/shard_map/encode_0/pallas_call | solution.py:44
  104.4 1.2 %collective-permute-start.25 = (f32[2,16,1024]{2,1,0:T(8,128)S(1)}, f32[2,16,1024]{2,1,0:T(8,128)S(1)}, u32[]{:S(2)}, u32[]{:S(2)}) collective-permute-start(f32[2,16,1024]{2,1,0:T(8,128)S(1)} %get-tuple-element.69), channel_id=1, source_target_pairs={{0,16},{1,17},{2,18},{3,19},{4,20},{5,21},{6,22},{7,23},{8,24},{9,... | collective-permute-start | bytes 393224 | tf_op jit(solution)/shard_map/ppermute | solution.py:40
  105.6 2.6 %collective-permute-start.26 = (f32[2,16,1024]{2,1,0:T(8,128)S(1)}, f32[2,16,1024]{2,1,0:T(8,128)S(1)}, u32[]{:S(2)}, u32[]{:S(2)}) collective-permute-start(f32[2,16,1024]{2,1,0:T(8,128)S(1)} %get-tuple-element.70), channel_id=1, source_target_pairs={{0,32},{1,33},{2,34},{3,35},{4,36},{5,37},{6,38},{7,39},{8,40},{9,... | collective-permute-start | bytes 393224 | tf_op jit(solution)/shard_map/ppermute | solution.py:40
  108.2 1.5 %collective-permute-start.27 = (f32[2,16,1024]{2,1,0:T(8,128)S(1)}, f32[2,16,1024]{2,1,0:T(8,128)S(1)}, u32[]{:S(2)}, u32[]{:S(2)}) collective-permute-start(f32[2,16,1024]{2,1,0:T(8,128)S(1)} %get-tuple-element.71), channel_id=1, source_target_pairs={{0,48},{1,49},{2,50},{3,51},{4,52},{5,53},{6,54},{7,55},{8,56},{9,... | collective-permute-start | bytes 393224 | tf_op jit(solution)/shard_map/ppermute | solution.py:40
  109.7 2.7 %update.1 = (f32[1,32,8192]{2,1,0:T(8,128)}, f32[1,32,8192]{2,1,0:T(8,128)}, f32[1,32,8192]{2,1,0:T(8,128)}) custom-call(s32[1,8]{1,0:T(1,128)S(1)} %copy-done.3, f32[1,32,8192]{2,1,0:T(8,128)S(1)} %copy-done, f32[1,32,8192]{2,1,0:T(8,128)S(1)} %copy-done.1, f32[1,32,8192]{2,1,0:T(8,128)S(1)} %copy-done.2, f32[16,8192]{1,0:T(8,128)S(1)} %get-tuple-element.49.mine.mine_0, ...), custom_call_target="tpu_custom_call" | custom-call | tf_op jit(solution)/shard_map/update/pallas_call | solution.py:44
  113.2 3.0 %encode_1.1 = (f32[4,3,32,1024]{3,2,1,0:T(8,128)}, f32[8,128]{1,0:T(8,128)}) custom-call(f32[4,8]{1,0:T(4,128)S(1)} %copy-done.4, f32[1,3,32,1024]{3,2,1,0:T(8,128)S(1)} %get-tuple-element.62.refs_0_, f32[2,3,32,1024]{3,2,1,0:T(8,128)S(1)} %collective-permute-done.5.refs_0_.refs_1_, ...), custom_call_target="tpu_custom_call", output_to_operand_aliasing={{0}: (12, {})} | custom-call | tf_op jit(solution)/shard_map/encode_1/pallas_call | solution.py:44
  (55 shorter events, 16.4 us)
Async XLA Ops:
  3.2 4.2 %collective-permute-start = (f32[2,32,8192]{2,1,0:T(8,128)S(1)}, f32[2,32,8192]{2,1,0:T(8,128)S(1)}, u32[]{:S(2)}, u32[]{:S(2)}) collective-permute-start(f32[2,32,8192]{2,1,0:T(8,128)S(1)} %widen_far.1.far), channel_id=1, source_target_pairs={{0,1},{1,0},{2,3},{3,2},{4,5},{5,4},{6,7},{7,6},{8,9},{9,8},{10,11... | collective-permute-start | bytes 6291464 | tf_op jit(solution)/shard_map/ppermute | solution.py:40
  7.4 4.7 %copy-start.1 = (f32[1,32,8192]{2,1,0:T(8,128)S(1)}, f32[1,32,8192]{2,1,0:T(8,128)}, u32[]{:S(2)}) copy-start(f32[1,32,8192]{2,1,0:T(8,128)} %first.7) | copy-start | bytes 3145732
  7.4 4.7 %copy-start.2 = (f32[1,32,8192]{2,1,0:T(8,128)S(1)}, f32[1,32,8192]{2,1,0:T(8,128)}, u32[]{:S(2)}) copy-start(f32[1,32,8192]{2,1,0:T(8,128)} %second.7) | copy-start | bytes 3145732
  7.4 4.7 %copy-start.3 = (s32[1,8]{1,0:T(1,128)S(1)}, s32[1,8]{1,0:T(1,128)}, u32[]{:S(2)}) copy-start(s32[1,8]{1,0:T(1,128)} %holder.11) | copy-start | bytes 100
  7.7 10.2 %collective-permute-start.1 = (f32[6,32,8192]{2,1,0:T(8,128)S(1)}, f32[6,32,8192]{2,1,0:T(8,128)S(1)}, u32[]{:S(2)}, u32[]{:S(2)}) collective-permute-start(f32[6,32,8192]{2,1,0:T(8,128)S(1)} %get-tuple-element.41), channel_id=1, source_target_pairs={{0,1},{1,0},{2,3},{3,2},{4,5},{5,4},{6,7},{7,6},{8,9},{9,8},{10,11... | collective-permute-start | bytes 18874376 | tf_op jit(solution)/shard_map/ppermute | solution.py:40
  8.0 31.5 %collective-permute-start.3 = (f32[2,32,4096]{2,1,0:T(8,128)S(1)}, f32[2,32,4096]{2,1,0:T(8,128)S(1)}, u32[]{:S(2)}, u32[]{:S(2)}) collective-permute-start(f32[2,32,4096]{2,1,0:T(8,128)S(1)} %get-tuple-element.42.refs_0_), channel_id=1, source_target_pairs={{0,4},{1,5},{2,6},{3,7},{4,8},{5,9},{6,10},{7,11},{8,12},{9,13},{1... | collective-permute-start | bytes 3145736 | tf_op jit(solution)/shard_map/ppermute | solution.py:40
  10.0 29.5 %collective-permute-start.4 = (f32[2,32,4096]{2,1,0:T(8,128)S(1)}, f32[2,32,4096]{2,1,0:T(8,128)S(1)}, u32[]{:S(2)}, u32[]{:S(2)}) collective-permute-start(f32[2,32,4096]{2,1,0:T(8,128)S(1)} %get-tuple-element.43), channel_id=1, source_target_pairs={{0,12},{1,13},{2,14},{3,15},{4,0},{5,1},{6,2},{7,3},{8,4},{9,5},{1... | collective-permute-start | bytes 3145736 | tf_op jit(solution)/shard_map/ppermute | solution.py:40
  12.9 20.8 %collective-permute-start.5 = (f32[2,3,32,1024]{3,2,1,0:T(8,128)S(1)}, f32[2,3,32,1024]{3,2,1,0:T(8,128)S(1)}, u32[]{:S(2)}, u32[]{:S(2)}) collective-permute-start(f32[2,3,32,1024]{3,2,1,0:T(8,128)S(1)} %get-tuple-element.44), channel_id=1, source_target_pairs={{0,16},{1,17},{2,18},{3,19},{4,20},{5,21},{6,22},{7,23},{8,24},{9,... | collective-permute-start | bytes 2359304 | tf_op jit(solution)/shard_map/ppermute | solution.py:40
  14.5 19.2 %collective-permute-start.6 = (f32[2,3,32,1024]{3,2,1,0:T(8,128)S(1)}, f32[2,3,32,1024]{3,2,1,0:T(8,128)S(1)}, u32[]{:S(2)}, u32[]{:S(2)}) collective-permute-start(f32[2,3,32,1024]{3,2,1,0:T(8,128)S(1)} %get-tuple-element.45), channel_id=1, source_target_pairs={{0,48},{1,49},{2,50},{3,51},{4,52},{5,53},{6,54},{7,55},{8,56},{9,... | collective-permute-start | bytes 2359304 | tf_op jit(solution)/shard_map/ppermute | solution.py:40
  17.9 5.0 %collective-permute-start.2 = (s32[1,8]{1,0:T(1,128)S(1)}, s32[1,8]{1,0:T(1,128)S(1)}, u32[]{:S(2)}, u32[]{:S(2)}) collective-permute-start(s32[1,8]{1,0:T(1,128)S(1)} %copy-done.3), channel_id=1, source_target_pairs={{0,2},{1,3},{2,0},{3,1},{4,6},{5,7},{6,4},{7,5},{8,10},{9,11},{10,... | collective-permute-start | bytes 104 | tf_op jit(solution)/shard_map/ppermute | solution.py:40
  23.0 10.7 %collective-permute-start.7 = (f32[1,3,32,1024]{3,2,1,0:T(8,128)S(1)}, f32[1,3,32,1024]{3,2,1,0:T(8,128)S(1)}, u32[]{:S(2)}, u32[]{:S(2)}) collective-permute-start(f32[1,3,32,1024]{3,2,1,0:T(8,128)S(1)} %get-tuple-element.46), channel_id=1, source_target_pairs={{0,64},{1,65},{2,66},{3,67},{4,68},{5,69},{6,70},{7,71},{8,72},{9,... | collective-permute-start | bytes 1179656 | tf_op jit(solution)/shard_map/ppermute | solution.py:40
  35.0 20.3 %collective-permute-start.10 = (f32[2,3,32,1024]{3,2,1,0:T(8,128)S(1)}, f32[2,3,32,1024]{3,2,1,0:T(8,128)S(1)}, u32[]{:S(2)}, u32[]{:S(2)}) collective-permute-start(f32[2,3,32,1024]{3,2,1,0:T(8,128)S(1)} %old_two.1.refs_0_), channel_id=1, source_target_pairs={{0,32},{1,33},{2,34},{3,35},{4,36},{5,37},{6,38},{7,39},{8,40},{9,... | collective-permute-start | bytes 2359304 | tf_op jit(solution)/shard_map/ppermute | solution.py:40
  37.9 18.0 %collective-permute-start.11 = (f32[2,3,32,1024]{3,2,1,0:T(8,128)S(1)}, f32[2,3,32,1024]{3,2,1,0:T(8,128)S(1)}, u32[]{:S(2)}, u32[]{:S(2)}) collective-permute-start(f32[2,3,32,1024]{3,2,1,0:T(8,128)S(1)} %other_side.2.refs_0_), channel_id=1, source_target_pairs={{0,64},{1,65},{2,66},{3,67},{4,68},{5,69},{6,70},{7,71},{8,72},{9,... | collective-permute-start | bytes 2359304 | tf_op jit(solution)/shard_map/ppermute | solution.py:40
  39.8 28.2 %collective-permute-start.8 = (f32[2,2,16,4096]{3,2,1,0:T(8,128)S(1)}, f32[2,2,16,4096]{3,2,1,0:T(8,128)S(1)}, u32[]{:S(2)}, u32[]{:S(2)}) collective-permute-start(f32[2,2,16,4096]{3,2,1,0:T(8,128)S(1)} %get-tuple-element.47.refs_2_), channel_id=1, source_target_pairs={{0,4},{1,5},{2,6},{3,7},{4,8},{5,9},{6,10},{7,11},{8,12},{9,13},{1... | collective-permute-start | bytes 3145736 | tf_op jit(solution)/shard_map/ppermute | solution.py:40
  41.5 26.5 %collective-permute-start.9 = (f32[2,2,16,4096]{3,2,1,0:T(8,128)S(1)}, f32[2,2,16,4096]{3,2,1,0:T(8,128)S(1)}, u32[]{:S(2)}, u32[]{:S(2)}) collective-permute-start(f32[2,2,16,4096]{3,2,1,0:T(8,128)S(1)} %get-tuple-element.48), channel_id=1, source_target_pairs={{0,12},{1,13},{2,14},{3,15},{4,0},{5,1},{6,2},{7,3},{8,4},{9,5},{1... | collective-permute-start | bytes 3145736 | tf_op jit(solution)/shard_map/ppermute | solution.py:40
  56.4 31.2 %collective-permute-start.12 = (f32[2,2,16,4096]{3,2,1,0:T(8,128)S(1)}, f32[2,2,16,4096]{3,2,1,0:T(8,128)S(1)}, u32[]{:S(2)}, u32[]{:S(2)}) collective-permute-start(f32[2,2,16,4096]{3,2,1,0:T(8,128)S(1)} %get-tuple-element.50), channel_id=1, source_target_pairs={{0,4},{1,5},{2,6},{3,7},{4,8},{5,9},{6,10},{7,11},{8,12},{9,13},{1... | collective-permute-start | bytes 3145736 | tf_op jit(solution)/shard_map/ppermute | solution.py:40
  57.4 30.2 %collective-permute-start.13 = (f32[2,2,16,4096]{3,2,1,0:T(8,128)S(1)}, f32[2,2,16,4096]{3,2,1,0:T(8,128)S(1)}, u32[]{:S(2)}, u32[]{:S(2)}) collective-permute-start(f32[2,2,16,4096]{3,2,1,0:T(8,128)S(1)} %get-tuple-element.51), channel_id=1, source_target_pairs={{0,12},{1,13},{2,14},{3,15},{4,0},{5,1},{6,2},{7,3},{8,4},{9,5},{1... | collective-permute-start | bytes 3145736 | tf_op jit(solution)/shard_map/ppermute | solution.py:40
  59.9 12.1 %collective-permute-start.17 = (f32[1,3,32,1024]{3,2,1,0:T(8,128)S(1)}, f32[1,3,32,1024]{3,2,1,0:T(8,128)S(1)}, u32[]{:S(2)}, u32[]{:S(2)}) collective-permute-start(f32[1,3,32,1024]{3,2,1,0:T(8,128)S(1)} %other_side.3.refs_0_), channel_id=1, source_target_pairs={{0,64},{1,65},{2,66},{3,67},{4,68},{5,69},{6,70},{7,71},{8,72},{9,... | collective-permute-start | bytes 1179656 | tf_op jit(solution)/shard_map/ppermute | solution.py:40
  68.9 16.5 %collective-permute-start.14 = (f32[8,16,1024]{2,1,0:T(8,128)S(1)}, f32[8,16,1024]{2,1,0:T(8,128)S(1)}, u32[]{:S(2)}, u32[]{:S(2)}) collective-permute-start(f32[8,16,1024]{2,1,0:T(8,128)S(1)} %get-tuple-element.52), channel_id=1, source_target_pairs={{0,2},{1,3},{2,0},{3,1},{4,6},{5,7},{6,4},{7,5},{8,10},{9,11},{10,... | collective-permute-start | bytes 1572872 | tf_op jit(solution)/shard_map/ppermute | solution.py:40
  71.5 13.3 %collective-permute-start.15 = (f32[4,16,1024]{2,1,0:T(8,128)S(1)}, f32[4,16,1024]{2,1,0:T(8,128)S(1)}, u32[]{:S(2)}, u32[]{:S(2)}) collective-permute-start(f32[4,16,1024]{2,1,0:T(8,128)S(1)} %get-tuple-element.53), channel_id=1, source_target_pairs={{0,64},{1,65},{2,66},{3,67},{4,68},{5,69},{6,70},{7,71},{8,72},{9,... | collective-permute-start | bytes 786440 | tf_op jit(solution)/shard_map/ppermute | solution.py:40
  72.0 13.4 %collective-permute-start.16 = (f32[4,16,1024]{2,1,0:T(8,128)S(1)}, f32[4,16,1024]{2,1,0:T(8,128)S(1)}, u32[]{:S(2)}, u32[]{:S(2)}) collective-permute-start(f32[4,16,1024]{2,1,0:T(8,128)S(1)} %get-tuple-element.54), channel_id=1, source_target_pairs={{0,66},{1,67},{2,64},{3,65},{4,70},{5,71},{6,68},{7,69},{8,74},{9,... | collective-permute-start | bytes 786440 | tf_op jit(solution)/shard_map/ppermute | solution.py:40
  86.0 15.3 %copy-start.4 = (f32[4,8]{1,0:T(4,128)S(1)}, f32[4,8]{1,0:T(4,128)}, u32[]{:S(2)}) copy-start(f32[4,8]{1,0:T(4,128)} %code.3) | copy-start | bytes 388
  86.0 8.5 %collective-permute-start.22 = (f32[2,16,1024]{2,1,0:T(8,128)S(1)}, f32[2,16,1024]{2,1,0:T(8,128)S(1)}, u32[]{:S(2)}, u32[]{:S(2)}) collective-permute-start(f32[2,16,1024]{2,1,0:T(8,128)S(1)} %get-tuple-element.55.refs_0_), channel_id=1, source_target_pairs={{0,16},{1,17},{2,18},{3,19},{4,20},{5,21},{6,22},{7,23},{8,24},{9,... | collective-permute-start | bytes 393224 | tf_op jit(solution)/shard_map/ppermute | solution.py:40
  88.5 15.3 %collective-permute-start.18 = (f32[4,16,1024]{2,1,0:T(8,128)S(1)}, f32[4,16,1024]{2,1,0:T(8,128)S(1)}, u32[]{:S(2)}, u32[]{:S(2)}) collective-permute-start(f32[4,16,1024]{2,1,0:T(8,128)S(1)} %get-tuple-element.57), channel_id=1, source_target_pairs={{0,2},{1,3},{2,0},{3,1},{4,6},{5,7},{6,4},{7,5},{8,10},{9,11},{10,... | collective-permute-start | bytes 786440 | tf_op jit(solution)/shard_map/ppermute | solution.py:40
  90.7 13.0 %collective-permute-start.20 = (f32[4,16,1024]{2,1,0:T(8,128)S(1)}, f32[4,16,1024]{2,1,0:T(8,128)S(1)}, u32[]{:S(2)}, u32[]{:S(2)}) collective-permute-start(f32[4,16,1024]{2,1,0:T(8,128)S(1)} %get-tuple-element.63), channel_id=1, source_target_pairs={{0,64},{1,65},{2,66},{3,67},{4,68},{5,69},{6,70},{7,71},{8,72},{9,... | collective-permute-start | bytes 786440 | tf_op jit(solution)/shard_map/ppermute | solution.py:40
  91.6 12.2 %collective-permute-start.21 = (f32[4,16,1024]{2,1,0:T(8,128)S(1)}, f32[4,16,1024]{2,1,0:T(8,128)S(1)}, u32[]{:S(2)}, u32[]{:S(2)}) collective-permute-start(f32[4,16,1024]{2,1,0:T(8,128)S(1)} %get-tuple-element.58), channel_id=1, source_target_pairs={{0,66},{1,67},{2,64},{3,65},{4,70},{5,71},{6,68},{7,69},{8,74},{9,... | collective-permute-start | bytes 786440 | tf_op jit(solution)/shard_map/ppermute | solution.py:40
  92.7 6.5 %collective-permute-start.23 = (f32[2,16,1024]{2,1,0:T(8,128)S(1)}, f32[2,16,1024]{2,1,0:T(8,128)S(1)}, u32[]{:S(2)}, u32[]{:S(2)}) collective-permute-start(f32[2,16,1024]{2,1,0:T(8,128)S(1)} %get-tuple-element.65), channel_id=1, source_target_pairs={{0,32},{1,33},{2,34},{3,35},{4,36},{5,37},{6,38},{7,39},{8,40},{9,... | collective-permute-start | bytes 393224 | tf_op jit(solution)/shard_map/ppermute | solution.py:40
  94.5 6.8 %collective-permute-start.24 = (f32[2,16,1024]{2,1,0:T(8,128)S(1)}, f32[2,16,1024]{2,1,0:T(8,128)S(1)}, u32[]{:S(2)}, u32[]{:S(2)}) collective-permute-start(f32[2,16,1024]{2,1,0:T(8,128)S(1)} %get-tuple-element.66), channel_id=1, source_target_pairs={{0,48},{1,49},{2,50},{3,51},{4,52},{5,53},{6,54},{7,55},{8,56},{9,... | collective-permute-start | bytes 393224 | tf_op jit(solution)/shard_map/ppermute | solution.py:40
  99.2 10.6 %collective-permute-start.19 = (f32[4,16,1024]{2,1,0:T(8,128)S(1)}, f32[4,16,1024]{2,1,0:T(8,128)S(1)}, u32[]{:S(2)}, u32[]{:S(2)}) collective-permute-start(f32[4,16,1024]{2,1,0:T(8,128)S(1)} %get-tuple-element.58), channel_id=1, source_target_pairs={{0,2},{1,3},{2,0},{3,1},{4,6},{5,7},{6,4},{7,5},{8,10},{9,11},{10,... | collective-permute-start | bytes 786440 | tf_op jit(solution)/shard_map/ppermute | solution.py:40
  104.4 8.0 %collective-permute-start.25 = (f32[2,16,1024]{2,1,0:T(8,128)S(1)}, f32[2,16,1024]{2,1,0:T(8,128)S(1)}, u32[]{:S(2)}, u32[]{:S(2)}) collective-permute-start(f32[2,16,1024]{2,1,0:T(8,128)S(1)} %get-tuple-element.69), channel_id=1, source_target_pairs={{0,16},{1,17},{2,18},{3,19},{4,20},{5,21},{6,22},{7,23},{8,24},{9,... | collective-permute-start | bytes 393224 | tf_op jit(solution)/shard_map/ppermute | solution.py:40
  105.6 7.0 %collective-permute-start.26 = (f32[2,16,1024]{2,1,0:T(8,128)S(1)}, f32[2,16,1024]{2,1,0:T(8,128)S(1)}, u32[]{:S(2)}, u32[]{:S(2)}) collective-permute-start(f32[2,16,1024]{2,1,0:T(8,128)S(1)} %get-tuple-element.70), channel_id=1, source_target_pairs={{0,32},{1,33},{2,34},{3,35},{4,36},{5,37},{6,38},{7,39},{8,40},{9,... | collective-permute-start | bytes 393224 | tf_op jit(solution)/shard_map/ppermute | solution.py:40
  108.2 5.0 %collective-permute-start.27 = (f32[2,16,1024]{2,1,0:T(8,128)S(1)}, f32[2,16,1024]{2,1,0:T(8,128)S(1)}, u32[]{:S(2)}, u32[]{:S(2)}) collective-permute-start(f32[2,16,1024]{2,1,0:T(8,128)S(1)} %get-tuple-element.71), channel_id=1, source_target_pairs={{0,48},{1,49},{2,50},{3,51},{4,52},{5,53},{6,54},{7,55},{8,56},{9,... | collective-permute-start | bytes 393224 | tf_op jit(solution)/shard_map/ppermute | solution.py:40
  (3 other events, 7.3 us)

commit v4 on v3

--- a/solution.py
+++ b/solution.py
@@ -30,6 +30,7 @@
 ACROSS = links(lambda x, y, z, core: (x ^ 2, y, z, core))
 BESIDE = links(lambda x, y, z, core: (x ^ 1, y, z, core))
 CORNER = links(lambda x, y, z, core: (3 - x, y, z, core))
+BESIDE_FAR = links(lambda x, y, z, core: (x ^ 1, y + 2, z, core))
 ALONG_Y = [None] + [links(lambda x, y, z, core, step=step: (x, y + step, z, core)) for step in (1, 2, 3)]
 
 RELATIVE_Z = (2, 1, 3, 0)
@@ -87,12 +88,13 @@
 
 
 def widen_far(blocks, owner):
-    def body(blocks, owner, out, read, sems):
-        copies = [
-            pltpu.make_async_copy(blocks.at[block_of(owner, FAR + i, False)], read.at[i], sems.at[i]) for i in range(2)
-        ]
-        for copy in copies:
-            copy.start()
+    def body(blocks, owner, out, own, read, sems):
+        copies = []
+        for keep, to in ((False, read), (True, own)):
+            for i in range(2):
+                source = blocks.at[block_of(owner, FAR + i, keep)]
+                copies.append(pltpu.make_async_copy(source, to.at[i], sems.at[len(copies)]))
+                copies[-1].start()
         for i in range(2):
             copies[i].wait()
 
@@ -100,24 +102,26 @@
                 out[i, :, columns] = read[i, :, columns].astype(F32)
 
             by_tiles(8192, 1024, cast)
+        for copy in copies[2:]:
+            copy.wait()
 
     return call(
         "widen_far",
         body,
         [(blocks, HBM), (owner, SMEM)],
-        [((2, 32, 8192), F32, VMEM)],
-        [pltpu.VMEM((2, 32, 8192), BF16), pltpu.SemaphoreType.DMA((2,))],
-        limit=50,
-    )[0]
-
-
-def widen_rest(blocks, owner, far):
-    def body(blocks, owner, far, out, own, read, sems):
-        copies = [
-            pltpu.make_async_copy(blocks.at[block_of(owner, UP + i, False)], read.at[i], sems.at[i]) for i in range(6)
-        ] + [pltpu.make_async_copy(blocks.at[block_of(owner, i, True)], own.at[i], sems.at[6 + i]) for i in range(8)]
-        for copy in copies:
-            copy.start()
+        [((2, 32, 8192), F32, VMEM), ((2, 32, 8192), BF16, VMEM)],
+        [pltpu.VMEM((2, 32, 8192), BF16), pltpu.SemaphoreType.DMA((4,))],
+        limit=48,
+    )
+
+
+def widen_rest(blocks, owner, after):
+    def body(blocks, owner, after, out, read, sems):
+        copies = []
+        for i in range(6):
+            source = blocks.at[block_of(owner, UP + i, False)]
+            copies.append(pltpu.make_async_copy(source, read.at[i], sems.at[i]))
+            copies[-1].start()
         for i in range(6):
             copies[i].wait()
 
@@ -125,17 +129,34 @@
                 out[i, :, columns] = read[i, :, columns].astype(F32)
 
             by_tiles(8192, 1024, cast)
-        for copy in copies[6:]:
+
+    return call(
+        "widen_rest",
+        body,
+        [(blocks, HBM), (owner, SMEM), (after, VMEM)],
+        [((6, 32, 8192), F32, VMEM)],
+        [pltpu.VMEM((6, 32, 8192), BF16), pltpu.SemaphoreType.DMA((6,))],
+        limit=42,
+    )[0]
+
+
+def own_rest(blocks, owner, after):
+    def body(blocks, owner, after, own, sems):
+        copies = []
+        for i in range(6):
+            source = blocks.at[block_of(owner, UP + i, True)]
+            copies.append(pltpu.make_async_copy(source, own.at[i], sems.at[i]))
+            copies[-1].start()
+        for copy in copies:
             copy.wait()
 
     return call(
-        "widen_rest",
-        body,
-        [(blocks, HBM), (owner, SMEM), (far, VMEM)],
-        [((6, 32, 8192), F32, VMEM), ((8, 32, 8192), BF16, VMEM)],
-        [pltpu.VMEM((6, 32, 8192), BF16), pltpu.SemaphoreType.DMA((14,))],
-        limit=40,
-    )
+        "own_rest",
+        body,
+        [(blocks, HBM), (owner, SMEM), (after, VMEM)],
+        [((6, 32, 8192), BF16, VMEM)],
+        [pltpu.SemaphoreType.DMA((6,))],
+    )[0]
 
 
 def pair_far(own, far, rest):
@@ -144,8 +165,8 @@
 
             def add(columns):
                 later = pl.ds(columns.start + 4096, columns.size)
-                up[j, :, columns] = own[FAR + j, :, columns].astype(F32) + far[j, :, columns]
-                down[j, :, columns] = own[FAR + j, :, later].astype(F32) + far[j, :, later]
+                up[j, :, columns] = own[j, :, columns].astype(F32) + far[j, :, columns]
+                down[j, :, columns] = own[j, :, later].astype(F32) + far[j, :, later]
 
             by_tiles(4096, 512, add)
 
@@ -165,7 +186,7 @@
         rows = pl.ds(16 * c, 16)
 
         def pair(slot, columns):
-            return own[slot, rows, columns].astype(F32) + rest[slot - 2, rows, columns]
+            return own[slot - 2, rows, columns].astype(F32) + rest[slot - 2, rows, columns]
 
         for j in range(2):
 
@@ -197,9 +218,9 @@
 
             def add(columns):
                 later = pl.ds(columns.start + 4096, columns.size)
-                both = own[HERE + j, rows, columns].astype(F32) + rest[HERE - 2 + j, rows, columns]
+                both = own[HERE - 2 + j, rows, columns].astype(F32) + rest[HERE - 2 + j, rows, columns]
                 out[:, columns] = both + below[0, j, :, columns] + above[1, j, :, columns]
-                both = own[HERE + j, rows, later].astype(F32) + rest[HERE - 2 + j, rows, later]
+                both = own[HERE - 2 + j, rows, later].astype(F32) + rest[HERE - 2 + j, rows, later]
                 out[:, later] = both + below[1, j, :, columns] + above[0, j, :, columns]
 
             by_tiles(4096, 512, add)
@@ -222,8 +243,9 @@
     )
 
 
-def for_holders(holder, mine, near, beside, corner, after):
-    def body(holder, mine, near, beside, corner, after, *outs):
+def for_holders(holder, mine, beside, corner, near, after=()):
+    def body(holder, mine, beside, corner, near, *refs):
+        outs = refs[len(after) :]
         for s in range(4):
             outs[s][0] = mine[:, pl.ds(column_of(holder, 0, s), 1024)] + near[s]
             outs[s][1] = beside[s] + corner[s]
@@ -231,7 +253,7 @@
     return call(
         "for_holders",
         body,
-        [(holder, SMEM)] + [(array, VMEM) for array in (mine, near, beside, corner, after)],
+        [(holder, SMEM)] + [(array, VMEM) for array in (mine, beside, corner, near, *after)],
         [((2, 16, 1024), F32, VMEM)] * 4,
     )
 
@@ -253,9 +275,29 @@
     return call(
         name,
         body,
-        [(holder, SMEM)] + [(old, VMEM) for old in states] + [(array, VMEM) for array in after],
+        [(holder, SMEM)] + [(old, VMEM) for old in states] + after,
         [((len(steps), 3, 32, 1024), F32, VMEM) for steps in asked],
     )
+
+
+def old_two(holder, weight, first, second, beside, after):
+    def body(holder, weight, first, second, beside, after, out):
+        start = column_of(holder, 0, 2)
+
+        def copy(columns):
+            source = pl.ds(pl.multiple_of(start + columns.start, 128), columns.size)
+            for k, old in enumerate((weight, first, second)):
+                out[0, k, :, columns] = old[0, :, source]
+                out[1, k, :, columns] = beside[1, k, :, columns]
+
+        by_tiles(1024, 256, copy)
+
+    return call(
+        "old_two",
+        body,
+        [(holder, SMEM)] + [(array, VMEM) for array in (weight, first, second, beside, after)],
+        [((2, 3, 32, 1024), F32, VMEM)],
+    )[0]
 
 
 def other_side(olds, after):
@@ -263,11 +305,11 @@
 
     def body(*refs):
         out = refs[count + len(after)]
-        for i in range(count):
+        for i, old in enumerate(olds):
 
             def copy(columns):
                 for k in range(3):
-                    out[i, k, :, columns] = refs[i][1, k, :, columns]
+                    out[i, k, :, columns] = refs[i][old.shape[0] - 1, k, :, columns]
 
             by_tiles(1024, 256, copy)
 
@@ -281,13 +323,14 @@
 
 def advance(weight, first, second, grad):
     first_new = 0.9 * first + 0.1 * grad
-    second_new = 0.95 * second + 0.05 * grad * grad
-    step = first_new / (1.0 - 0.9**10) / (jnp.sqrt(second_new / (1.0 - 0.95**10)) + 1e-08)
-    return weight - 0.01 * (step + 0.1 * weight), first_new, second_new
-
-
-def update(holder, weight, first, second, mine, across):
-    def body(holder, weight, first, second, mine_0, mine_1, all_0, near_1, far_1, *refs):
+    second_new = 0.95 * second + 0.05 * (grad * grad)
+    root = jnp.sqrt(second_new * (1.0 / (1.0 - 0.95**10))) + 1e-08
+    step = (first_new * (0.01 / (1.0 - 0.9**10))) * pl.reciprocal(root, approx=True)
+    return (1.0 - 0.01 * 0.1) * weight - step, first_new, second_new
+
+
+def update(holder, weight, first, second, mine, across, after):
+    def body(holder, after, weight, first, second, mine_0, mine_1, all_0, near_1, far_1, *refs):
         outs, made, sems = refs[:3], refs[3], refs[4]
         writes = []
         for c, mine in enumerate((mine_0, mine_1)):
@@ -308,7 +351,7 @@
     return call(
         "update",
         body,
-        [(holder, SMEM)] + [(array, VMEM) for array in (weight, first, second, *mine, *across)],
+        [(holder, SMEM)] + [(array, VMEM) for array in (after, weight, first, second, *mine, *across)],
         [((1, 32, 8192), F32, HBM)] * 3,
         [pltpu.VMEM((3, 32, 8192), F32), pltpu.SemaphoreType.DMA((6,))],
     )
@@ -325,7 +368,7 @@
             places[a][s] = (known[0] if known else len(arrays) - 1, part)
 
     def body(code, *refs):
-        olds, ins, (out, total, sem) = refs[: len(arrays)], refs[len(arrays) :], (refs[-4], *refs[-2:])
+        olds, ins, (out, total, sems) = refs[: len(arrays)], refs[len(arrays) :], (refs[-4], *refs[-2:])
         _, _, _, side, y = position()
         ranks = [[lax.rem(side + a, 2) * 4 + lax.rem(y + 4 - s, 4) for s in range(4)] for a in range(2)]
         scales = [[[code[j, ranks[a][s]] for s in range(4)] for a in range(2)] for j in range(4)]
@@ -334,6 +377,7 @@
             array, part = places[a][s]
             return olds[array][part, k, pl.ds(16 * c + row, 8), columns]
 
+        copies = []
         for row in range(0, 16, 8):
 
             def one(columns):
@@ -352,9 +396,11 @@
                         total[j, k, rows, columns] = sums[j][k]
 
             by_tiles(1024, 256, one)
-        copy = pltpu.make_async_copy(total, out.at[:, :, pl.ds(16 * c, 16)], sem)
-        copy.start()
-        copy.wait()
+            there = out.at[:, :, pl.ds(16 * c + row, 8)]
+            copies.append(pltpu.make_async_copy(total.at[:, :, pl.ds(row, 8)], there, sems.at[row // 8]))
+            copies[-1].start()
+        for copy in copies:
+            copy.wait()
         refs[-3][...] = jnp.zeros((8, 128), F32)
 
     return call(
@@ -362,7 +408,7 @@
         body,
         [(code, SMEM)] + [(array, VMEM) for array in (*arrays, *grads)] + ([] if into is None else [(into, HBM)]),
         [((4, 3, 32, 1024), F32, HBM), ((8, 128), F32, VMEM)],
-        [pltpu.VMEM((4, 3, 16, 1024), F32), pltpu.SemaphoreType.DMA],
+        [pltpu.VMEM((4, 3, 16, 1024), F32), pltpu.SemaphoreType.DMA((2,))],
         aliases=None if into is None else {1 + len(arrays) + len(grads): 0},
     )
 
@@ -371,45 +417,44 @@
     blocks = grad_part.reshape(16, 32, 8192)
     states = (weight, moment_one, moment_two)
 
-    far = widen_far(blocks, owner)
-    rest, own = widen_rest(blocks, owner, far)
+    far, own = widen_far(blocks, owner)
+    rest = widen_rest(blocks, owner, far)
     go_up, go_down, rest = pair_far(own, send(far, TO_CORE), rest)
     rest = send(rest, TO_CORE)
     far_below, far_above = send(go_up, UP_Z), send(go_down, DOWN_Z)
 
-    one, three = old_parts("old_odd", holder, states, [[(0, 1), (1, 1)], [(0, 3), (1, 3)]], (go_up,))
-    one, three = send(one, ALONG_Y[1]), send(three, ALONG_Y[3])
-    zero, beside = old_parts("old_here", holder, states, [[(0, 0)], [(1, 0)]], (rest,))
-    beside = send(beside, BESIDE)
-
     held = send(holder, ACROSS)
-    odd = other_side([one, three], [(beside, VMEM), (held, SMEM)])
-    (two,) = old_parts("old_two", holder, states, [[(0, 2), (1, 2)]], (odd,))
+    asked = [[(0, 0)], [(1, 0), (1, 2)]]
+    zero, beside = old_parts("old_here", holder, states, asked, [(go_up, VMEM), (held, SMEM)])
+    (one,) = old_parts("old_one", holder, states, [[(0, 1), (1, 1)]], [(beside, VMEM)])
+    (three,) = old_parts("old_three", holder, states, [[(0, 3), (1, 3)]], [(rest, VMEM)])
+    own = own_rest(blocks, owner, three)
+    beside, one, three = send(beside, BESIDE), send(one, ALONG_Y[1]), send(three, ALONG_Y[3])
+
+    go_up, go_down = onward(own, rest, far_below, far_above, 0, (beside,))
+    along_z = [(send(go_up, UP_Z), send(go_down, DOWN_Z))]
+    odd = other_side([one, three], [(go_up, VMEM)])
+    two = old_two(holder, *states, beside, odd)
     after = (two,)
     odd, two = send(odd, BESIDE), send(two, ALONG_Y[2])
-
-    go_up, go_down = onward(own, rest, far_below, far_above, 0, after)
-    along_z = [(send(go_up, UP_Z), send(go_down, DOWN_Z))]
-    even = other_side([two], [(odd, VMEM), (go_up, VMEM)])
-    after = (even,)
-    even = send(even, BESIDE)
     go_up, go_down = onward(own, rest, far_below, far_above, 1, after)
     along_z.append((send(go_up, UP_Z), send(go_down, DOWN_Z)))
-    old = [[(zero, 0), (one, 0), (two, 0), (three, 0)], [(beside, 0), (odd, 0), (even, 0), (odd, 1)]]
-
-    mine, across, parity = [], [], None
+    old = [[(zero, 0), (one, 0), (two, 0), (three, 0)], [(beside, 0), (odd, 0), (two, 1), (odd, 1)]]
+
+    mine, across, parity, after = [], [], None, (two,)
     for c in range(2):
-        ours, near, to_beside, to_corner = gathered_z(own, rest, (holder, held), *along_z[c], c, after)
+        before = (odd,) if c == 0 else (sums[1],)
+        ours, near, to_beside, corner = gathered_z(own, rest, (holder, held), *along_z[c], c, before)
         mine.append(ours)
-        across.append(send(near, ACROSS))
-        done = even if c == 0 else done
-        sums = for_holders(holder, ours, across[c], send(to_beside, BESIDE), send(to_corner, CORNER), done)
-        after = (sums[1],)
+        to_beside, to_corner, near = send(to_beside, BESIDE), send(corner, CORNER), send(near, ACROSS)
+        across.append(near)
+        sums = for_holders(holder, ours, to_beside, to_corner, near, after)
         grads = [sums[0]] + [send(sums[s], ALONG_Y[s]) for s in (1, 2, 3)]
-        parity, done = encode(code, old, grads, c, parity)
-    across.append(send(to_corner, ACROSS))
-
-    new = update(holder, *states, mine, across)
+        parity, mark = encode(code, old, grads, c, parity)
+        after = (mark,)
+    across.append(send(corner, ACROSS))
+
+    new = update(holder, *states, mine, across, sums[1])
     return (*new, parity)
 
 

time: 116 us -> 127 us (1.095)
  waiting for transfers between devices: 47.8 us -> 64.5 us
  starting transfers between devices: 46.4 us -> 40.6 us
    ppermute x28 -> x27, waiting for transfers between devices: 47.8 us -> 64.5 us  [send(): return lax.ppermute(array, AXES, pairs)]
    ppermute x28 -> x27, starting transfers between devices: 46.4 us -> 40.6 us  [send(): return lax.ppermute(array, AXES, pairs)]
    pallas_call x17 -> x18, Pallas kernels: 20.6 us -> 20.1 us  [call(): pl.pallas_call(body, out_shape=[jax.ShapeDtypeStruct(shape, kind) for sha...]
  transfers between devices with their start and end apart: 28 -> 27, of which waited for: 13 -> 13; matrix products, arithmetic and copies ran while one was open for 0% -> 0% of each run, Pallas kernels for 13% -> 12%
where the time goes in v4:
time: 127 us
  waiting for transfers between devices  64.5 us (51%)
  starting transfers between devices  40.6 us (32%)
  Pallas kernels  20.1 us (16%)
    ppermute x27, waiting for transfers between devices, send(): return lax.ppermute(array, AXES, pairs)  64.5 us
    ppermute x27, starting transfers between devices, send(): return lax.ppermute(array, AXES, pairs)  40.6 us
    pallas_call x18, Pallas kernels, call(): pl.pallas_call(body, out_shape=[jax.ShapeDtypeStruct(shape, kind) for sha...  20.1 us
  transfers between devices with their start and end apart: 27, of which 13 were waited for; matrix products, arithmetic and copies ran while one was open for 0% of the time, Pallas kernels for 12%

profile of v4, /device:TPU:0, one launch (start us, length us, event | category | flops | bytes accessed | tf_op | source)
XLA Modules:
  0.0 126.8 jit_solution(11320502638203999148)
XLA Ops:
  1.3 2.1 %widen_far.1 = (f32[2,32,8192]{2,1,0:T(8,128)S(1)}, bf16[2,32,8192]{2,1,0:T(8,128)(2,1)S(1)}) custom-call(bf16[16,32,8192]{2,1,0:T(8,128)(2,1)} %bitcast.1, s32[1,16]{1,0:T(1,128)S(1)} %copy-done.5), custom_call_target="tpu_custom_call" | custom-call | tf_op jit(solution)/shard_map/widen_far/pallas_call | solution.py:45
  3.5 2.6 %widen_rest.1.rest = f32[6,32,8192]{2,1,0:T(8,128)S(1)} custom-call(bf16[16,32,8192]{2,1,0:T(8,128)(2,1)} %bitcast.2, s32[1,16]{1,0:T(1,128)S(1)} %copy-done.5, f32[2,32,8192]{2,1,0:T(8,128)S(1)} %get-tuple-element.38.after), custom_call_target="tpu_custom_call" | custom-call | tf_op jit(solution)/shard_map/widen_rest/pallas_call | solution.py:45
  6.1 1.6 %collective-permute-done.far = f32[2,32,8192]{2,1,0:T(8,128)S(1)} collective-permute-done((f32[2,32,8192]{2,1,0:T(8,128)S(1)}, f32[2,32,8192]{2,1,0:T(8,128)S(1)}, u32[]{:S(2)}, u32[]{:S(2)}) %collective-permute-start) | collective-permute-done | bytes 2097184 | tf_op jit(solution)/shard_map/ppermute | solution.py:41
  8.2 4.1 %collective-permute-start.4 = (f32[2,32,4096]{2,1,0:T(8,128)S(1)}, f32[2,32,4096]{2,1,0:T(8,128)S(1)}, u32[]{:S(2)}, u32[]{:S(2)}) collective-permute-start(f32[2,32,4096]{2,1,0:T(8,128)S(1)} %get-tuple-element.41), channel_id=1, source_target_pairs={{0,12},{1,13},{2,14},{3,15},{4,0},{5,1},{6,2},{7,3},{8,4},{9,5},{1... | collective-permute-start | bytes 3145736 | tf_op jit(solution)/shard_map/ppermute | solution.py:41
  12.3 3.0 %collective-permute-start.2 = (s32[1,8]{1,0:T(1,128)S(1)}, s32[1,8]{1,0:T(1,128)S(1)}, u32[]{:S(2)}, u32[]{:S(2)}) collective-permute-start(s32[1,8]{1,0:T(1,128)S(1)} %copy-done.3), channel_id=1, source_target_pairs={{0,2},{1,3},{2,0},{3,1},{4,6},{5,7},{6,4},{7,5},{8,10},{9,11},{10,... | collective-permute-start | bytes 104 | tf_op jit(solution)/shard_map/ppermute | solution.py:41
  15.3 2.0 %collective-permute-done.2.refs_1_.other_held = s32[1,8]{1,0:T(1,128)S(1)} collective-permute-done((s32[1,8]{1,0:T(1,128)S(1)}, s32[1,8]{1,0:T(1,128)S(1)}, u32[]{:S(2)}, u32[]{:S(2)}) %collective-permute-start.2) | collective-permute-done | bytes 64 | tf_op jit(solution)/shard_map/ppermute | solution.py:41
  18.1 1.6 %collective-permute-start.5 = (f32[2,3,32,1024]{3,2,1,0:T(8,128)S(1)}, f32[2,3,32,1024]{3,2,1,0:T(8,128)S(1)}, u32[]{:S(2)}, u32[]{:S(2)}) collective-permute-start(f32[2,3,32,1024]{3,2,1,0:T(8,128)S(1)} %get-tuple-element.42.refs_0_), channel_id=1, source_target_pairs={{0,64},{1,65},{2,66},{3,67},{4,68},{5,69},{6,70},{7,71},{8,72},{9,... | collective-permute-start | bytes 2359304 | tf_op jit(solution)/shard_map/ppermute | solution.py:41
  20.3 1.6 %collective-permute-start.6 = (f32[2,3,32,1024]{3,2,1,0:T(8,128)S(1)}, f32[2,3,32,1024]{3,2,1,0:T(8,128)S(1)}, u32[]{:S(2)}, u32[]{:S(2)}) collective-permute-start(f32[2,3,32,1024]{3,2,1,0:T(8,128)S(1)} %old_one.1), channel_id=1, source_target_pairs={{0,16},{1,17},{2,18},{3,19},{4,20},{5,21},{6,22},{7,23},{8,24},{9,... | collective-permute-start | bytes 2359304 | tf_op jit(solution)/shard_map/ppermute | solution.py:41
  22.6 1.7 %collective-permute-start.7 = (f32[2,3,32,1024]{3,2,1,0:T(8,128)S(1)}, f32[2,3,32,1024]{3,2,1,0:T(8,128)S(1)}, u32[]{:S(2)}, u32[]{:S(2)}) collective-permute-start(f32[2,3,32,1024]{3,2,1,0:T(8,128)S(1)} %old_three.1.after), channel_id=1, source_target_pairs={{0,48},{1,49},{2,50},{3,51},{4,52},{5,53},{6,54},{7,55},{8,56},{9,... | collective-permute-start | bytes 2359304 | tf_op jit(solution)/shard_map/ppermute | solution.py:41
  25.3 11.2 %collective-permute-done.5.refs_0_.beside.refs_4_ = f32[2,3,32,1024]{3,2,1,0:T(8,128)S(1)} collective-permute-done((f32[2,3,32,1024]{3,2,1,0:T(8,128)S(1)}, f32[2,3,32,1024]{3,2,1,0:T(8,128)S(1)}, u32[]{:S(2)}, u32[]{:S(2)}) %collective-permute-start.5) | collective-permute-done | bytes 786464 | tf_op jit(solution)/shard_map/ppermute | solution.py:41
  36.6 2.1 %collective-permute-done.3.below = f32[2,32,4096]{2,1,0:T(8,128)S(1)} collective-permute-done((f32[2,32,4096]{2,1,0:T(8,128)S(1)}, f32[2,32,4096]{2,1,0:T(8,128)S(1)}, u32[]{:S(2)}, u32[]{:S(2)}) %collective-permute-start.3) | collective-permute-done | bytes 1048608 | tf_op jit(solution)/shard_map/ppermute | solution.py:41
  41.2 1.6 %collective-permute-start.12 = (f32[2,3,32,1024]{3,2,1,0:T(8,128)S(1)}, f32[2,3,32,1024]{3,2,1,0:T(8,128)S(1)}, u32[]{:S(2)}, u32[]{:S(2)}) collective-permute-start(f32[2,3,32,1024]{3,2,1,0:T(8,128)S(1)} %other_side.1.after), channel_id=1, source_target_pairs={{0,64},{1,65},{2,66},{3,67},{4,68},{5,69},{6,70},{7,71},{8,72},{9,... | collective-permute-start | bytes 2359304 | tf_op jit(solution)/shard_map/ppermute | solution.py:41
  43.4 3.3 %collective-permute-start.16 = (f32[2,3,32,1024]{3,2,1,0:T(8,128)S(1)}, f32[2,3,32,1024]{3,2,1,0:T(8,128)S(1)}, u32[]{:S(2)}, u32[]{:S(2)}) collective-permute-start(f32[2,3,32,1024]{3,2,1,0:T(8,128)S(1)} %old_two.1.refs_0_), channel_id=1, source_target_pairs={{0,32},{1,33},{2,34},{3,35},{4,36},{5,37},{6,38},{7,39},{8,40},{9,... | collective-permute-start | bytes 2359304 | tf_op jit(solution)/shard_map/ppermute | solution.py:41
  47.0 16.3 %collective-permute-done.11.above = f32[2,2,16,4096]{3,2,1,0:T(8,128)S(1)} collective-permute-done((f32[2,2,16,4096]{3,2,1,0:T(8,128)S(1)}, f32[2,2,16,4096]{3,2,1,0:T(8,128)S(1)}, u32[]{:S(2)}, u32[]{:S(2)}) %collective-permute-start.11) | collective-permute-done | bytes 1048608 | tf_op jit(solution)/shard_map/ppermute | solution.py:41
  63.4 1.8 %collective-permute-start.9 = (f32[2,2,16,4096]{3,2,1,0:T(8,128)S(1)}, f32[2,2,16,4096]{3,2,1,0:T(8,128)S(1)}, u32[]{:S(2)}, u32[]{:S(2)}) collective-permute-start(f32[2,2,16,4096]{3,2,1,0:T(8,128)S(1)} %get-tuple-element.45), channel_id=1, source_target_pairs={{0,12},{1,13},{2,14},{3,15},{4,0},{5,1},{6,2},{7,3},{8,4},{9,5},{1... | collective-permute-start | bytes 3145736 | tf_op jit(solution)/shard_map/ppermute | solution.py:41
  65.2 2.1 %collective-permute-done.10.below = f32[2,2,16,4096]{3,2,1,0:T(8,128)S(1)} collective-permute-done((f32[2,2,16,4096]{3,2,1,0:T(8,128)S(1)}, f32[2,2,16,4096]{3,2,1,0:T(8,128)S(1)}, u32[]{:S(2)}, u32[]{:S(2)}) %collective-permute-start.10) | collective-permute-done | bytes 1048608 | tf_op jit(solution)/shard_map/ppermute | solution.py:41
  68.2 3.4 %collective-permute-start.15 = (f32[8,16,1024]{2,1,0:T(8,128)S(1)}, f32[8,16,1024]{2,1,0:T(8,128)S(1)}, u32[]{:S(2)}, u32[]{:S(2)}) collective-permute-start(f32[8,16,1024]{2,1,0:T(8,128)S(1)} %get-tuple-element.50), channel_id=1, source_target_pairs={{0,2},{1,3},{2,0},{3,1},{4,6},{5,7},{6,4},{7,5},{8,10},{9,11},{10,... | collective-permute-start | bytes 1572872 | tf_op jit(solution)/shard_map/ppermute | solution.py:41
  72.7 12.4 %collective-permute-done.13.beside = f32[4,16,1024]{2,1,0:T(8,128)S(1)} collective-permute-done((f32[4,16,1024]{2,1,0:T(8,128)S(1)}, f32[4,16,1024]{2,1,0:T(8,128)S(1)}, u32[]{:S(2)}, u32[]{:S(2)}) %collective-permute-start.13) | collective-permute-done | bytes 262176 | tf_op jit(solution)/shard_map/ppermute | solution.py:41
  85.7 3.3 %collective-permute-start.21 = (f32[2,16,1024]{2,1,0:T(8,128)S(1)}, f32[2,16,1024]{2,1,0:T(8,128)S(1)}, u32[]{:S(2)}, u32[]{:S(2)}) collective-permute-start(f32[2,16,1024]{2,1,0:T(8,128)S(1)} %get-tuple-element.58), channel_id=1, source_target_pairs={{0,32},{1,33},{2,34},{3,35},{4,36},{5,37},{6,38},{7,39},{8,40},{9,... | collective-permute-start | bytes 393224 | tf_op jit(solution)/shard_map/ppermute | solution.py:41
  89.9 1.2 collective-permute-start.17
  91.1 3.0 %collective-permute-start.19 = (f32[4,16,1024]{2,1,0:T(8,128)S(1)}, f32[4,16,1024]{2,1,0:T(8,128)S(1)}, u32[]{:S(2)}, u32[]{:S(2)}) collective-permute-start(f32[4,16,1024]{2,1,0:T(8,128)S(1)} %get-tuple-element.55), channel_id=1, source_target_pairs={{0,2},{1,3},{2,0},{3,1},{4,6},{5,7},{6,4},{7,5},{8,10},{9,11},{10,... | collective-permute-start | bytes 786440 | tf_op jit(solution)/shard_map/ppermute | solution.py:41
  94.7 1.4 %collective-permute-start.22 = (f32[2,16,1024]{2,1,0:T(8,128)S(1)}, f32[2,16,1024]{2,1,0:T(8,128)S(1)}, u32[]{:S(2)}, u32[]{:S(2)}) collective-permute-start(f32[2,16,1024]{2,1,0:T(8,128)S(1)} %get-tuple-element.59), channel_id=1, source_target_pairs={{0,48},{1,49},{2,50},{3,51},{4,52},{5,53},{6,54},{7,55},{8,56},{9,... | collective-permute-start | bytes 393224 | tf_op jit(solution)/shard_map/ppermute | solution.py:41
  96.7 2.9 %collective-permute-done.22.refs_9_ = f32[2,16,1024]{2,1,0:T(8,128)S(1)} collective-permute-done((f32[2,16,1024]{2,1,0:T(8,128)S(1)}, f32[2,16,1024]{2,1,0:T(8,128)S(1)}, u32[]{:S(2)}, u32[]{:S(2)}) %collective-permute-start.22) | collective-permute-done | bytes 131104 | tf_op jit(solution)/shard_map/ppermute | solution.py:41
  99.6 1.4 %collective-permute-start.23 = (f32[4,16,1024]{2,1,0:T(8,128)S(1)}, f32[4,16,1024]{2,1,0:T(8,128)S(1)}, u32[]{:S(2)}, u32[]{:S(2)}) collective-permute-start(f32[4,16,1024]{2,1,0:T(8,128)S(1)} %get-tuple-element.54), channel_id=1, source_target_pairs={{0,2},{1,3},{2,0},{3,1},{4,6},{5,7},{6,4},{7,5},{8,10},{9,11},{10,... | collective-permute-start | bytes 786440 | tf_op jit(solution)/shard_map/ppermute | solution.py:41
  101.0 1.2 collective-permute-done.20.refs_7_
  102.3 2.3 %encode_0.1 = (f32[4,3,32,1024]{3,2,1,0:T(8,128)}, f32[8,128]{1,0:T(8,128)S(1)}) custom-call(f32[4,8]{1,0:T(4,128)S(1)} %copy-done.4, f32[1,3,32,1024]{3,2,1,0:T(8,128)S(1)} %get-tuple-element.56.refs_0_, f32[2,3,32,1024]{3,2,1,0:T(8,128)S(1)} %collective-permute-done.6.refs_0_.refs_1_, f32[2,3,32,1024]{3,2,1,0:T(8,128)S(1)} %collective-permute-done.16.refs_0_.refs_2_, ...), custom_call_target="tpu_custom_call" | custom-call | tf_op jit(solution)/shard_map/encode_0/pallas_call | solution.py:45
  104.6 2.4 %collective-permute-done.19.near.near_1 = f32[4,16,1024]{2,1,0:T(8,128)S(1)} collective-permute-done((f32[4,16,1024]{2,1,0:T(8,128)S(1)}, f32[4,16,1024]{2,1,0:T(8,128)S(1)}, u32[]{:S(2)}, u32[]{:S(2)}) %collective-permute-start.19) | collective-permute-done | bytes 262176 | tf_op jit(solution)/shard_map/ppermute | solution.py:41
  107.0 6.7 %collective-permute-done.18.corner = f32[4,16,1024]{2,1,0:T(8,128)S(1)} collective-permute-done((f32[4,16,1024]{2,1,0:T(8,128)S(1)}, f32[4,16,1024]{2,1,0:T(8,128)S(1)}, u32[]{:S(2)}, u32[]{:S(2)}) %collective-permute-start.18) | collective-permute-done | bytes 262176 | tf_op jit(solution)/shard_map/ppermute | solution.py:41
  114.7 3.0 %collective-permute-start.26 = (f32[2,16,1024]{2,1,0:T(8,128)S(1)}, f32[2,16,1024]{2,1,0:T(8,128)S(1)}, u32[]{:S(2)}, u32[]{:S(2)}) collective-permute-start(f32[2,16,1024]{2,1,0:T(8,128)S(1)} %get-tuple-element.67), channel_id=1, source_target_pairs={{0,48},{1,49},{2,50},{3,51},{4,52},{5,53},{6,54},{7,55},{8,56},{9,... | collective-permute-start | bytes 393224 | tf_op jit(solution)/shard_map/ppermute | solution.py:41
  117.7 2.7 %update.1 = (f32[1,32,8192]{2,1,0:T(8,128)}, f32[1,32,8192]{2,1,0:T(8,128)}, f32[1,32,8192]{2,1,0:T(8,128)}) custom-call(s32[1,8]{1,0:T(1,128)S(1)} %copy-done.3, f32[2,16,1024]{2,1,0:T(8,128)S(1)} %get-tuple-element.61.after, f32[1,32,8192]{2,1,0:T(8,128)S(1)} %copy-done, f32[1,32,8192]{2,1,0:T(8,128)S(1)} %copy-done.1, f32[1,32,8192]{2,1,0:T(8,128)S(1)} %copy-done.2, ...), custom_call_target="tpu_custom_call" | custom-call | tf_op jit(solution)/shard_map/update/pallas_call | solution.py:45
  121.2 2.7 %collective-permute-done.24.refs_7_ = f32[2,16,1024]{2,1,0:T(8,128)S(1)} collective-permute-done((f32[2,16,1024]{2,1,0:T(8,128)S(1)}, f32[2,16,1024]{2,1,0:T(8,128)S(1)}, u32[]{:S(2)}, u32[]{:S(2)}) %collective-permute-start.24) | collective-permute-done | bytes 131104 | tf_op jit(solution)/shard_map/ppermute | solution.py:41
  123.9 2.9 %encode_1.1 = (f32[4,3,32,1024]{3,2,1,0:T(8,128)}, f32[8,128]{1,0:T(8,128)}) custom-call(f32[4,8]{1,0:T(4,128)S(1)} %copy-done.4, f32[1,3,32,1024]{3,2,1,0:T(8,128)S(1)} %get-tuple-element.56.refs_0_, f32[2,3,32,1024]{3,2,1,0:T(8,128)S(1)} %collective-permute-done.6.refs_0_.refs_1_, ...), custom_call_target="tpu_custom_call", output_to_operand_aliasing={{0}: (11, {})} | custom-call | tf_op jit(solution)/shard_map/encode_1/pallas_call | solution.py:45
  (59 shorter events, 14.4 us)
Async XLA Ops:
  3.4 4.2 %collective-permute-start = (f32[2,32,8192]{2,1,0:T(8,128)S(1)}, f32[2,32,8192]{2,1,0:T(8,128)S(1)}, u32[]{:S(2)}, u32[]{:S(2)}) collective-permute-start(f32[2,32,8192]{2,1,0:T(8,128)S(1)} %get-tuple-element.38.after), channel_id=1, source_target_pairs={{0,1},{1,0},{2,3},{3,2},{4,5},{5,4},{6,7},{7,6},{8,9},{9,8},{10,11... | collective-permute-start | bytes 6291464 | tf_op jit(solution)/shard_map/ppermute | solution.py:41
  7.7 9.7 %copy-start = (f32[1,32,8192]{2,1,0:T(8,128)S(1)}, f32[1,32,8192]{2,1,0:T(8,128)}, u32[]{:S(2)}) copy-start(f32[1,32,8192]{2,1,0:T(8,128)} %weight.9) | copy-start | bytes 3145732
  7.7 9.7 %copy-start.1 = (f32[1,32,8192]{2,1,0:T(8,128)S(1)}, f32[1,32,8192]{2,1,0:T(8,128)}, u32[]{:S(2)}) copy-start(f32[1,32,8192]{2,1,0:T(8,128)} %first.9) | copy-start | bytes 3145732
  7.7 9.7 %copy-start.2 = (f32[1,32,8192]{2,1,0:T(8,128)S(1)}, f32[1,32,8192]{2,1,0:T(8,128)}, u32[]{:S(2)}) copy-start(f32[1,32,8192]{2,1,0:T(8,128)} %second.9) | copy-start | bytes 3145732
  8.0 14.0 %collective-permute-start.1 = (f32[6,32,8192]{2,1,0:T(8,128)S(1)}, f32[6,32,8192]{2,1,0:T(8,128)S(1)}, u32[]{:S(2)}, u32[]{:S(2)}) collective-permute-start(f32[6,32,8192]{2,1,0:T(8,128)S(1)} %get-tuple-element.39), channel_id=1, source_target_pairs={{0,1},{1,0},{2,3},{3,2},{4,5},{5,4},{6,7},{7,6},{8,9},{9,8},{10,11... | collective-permute-start | bytes 18874376 | tf_op jit(solution)/shard_map/ppermute | solution.py:41
  8.2 28.4 %collective-permute-start.4 = (f32[2,32,4096]{2,1,0:T(8,128)S(1)}, f32[2,32,4096]{2,1,0:T(8,128)S(1)}, u32[]{:S(2)}, u32[]{:S(2)}) collective-permute-start(f32[2,32,4096]{2,1,0:T(8,128)S(1)} %get-tuple-element.41), channel_id=1, source_target_pairs={{0,12},{1,13},{2,14},{3,15},{4,0},{5,1},{6,2},{7,3},{8,4},{9,5},{1... | collective-permute-start | bytes 3145736 | tf_op jit(solution)/shard_map/ppermute | solution.py:41
  12.3 26.4 %collective-permute-start.3 = (f32[2,32,4096]{2,1,0:T(8,128)S(1)}, f32[2,32,4096]{2,1,0:T(8,128)S(1)}, u32[]{:S(2)}, u32[]{:S(2)}) collective-permute-start(f32[2,32,4096]{2,1,0:T(8,128)S(1)} %get-tuple-element.40.refs_0_), channel_id=1, source_target_pairs={{0,4},{1,5},{2,6},{3,7},{4,8},{5,9},{6,10},{7,11},{8,12},{9,13},{1... | collective-permute-start | bytes 3145736 | tf_op jit(solution)/shard_map/ppermute | solution.py:41
  12.3 5.0 %collective-permute-start.2 = (s32[1,8]{1,0:T(1,128)S(1)}, s32[1,8]{1,0:T(1,128)S(1)}, u32[]{:S(2)}, u32[]{:S(2)}) collective-permute-start(s32[1,8]{1,0:T(1,128)S(1)} %copy-done.3), channel_id=1, source_target_pairs={{0,2},{1,3},{2,0},{3,1},{4,6},{5,7},{6,4},{7,5},{8,10},{9,11},{10,... | collective-permute-start | bytes 104 | tf_op jit(solution)/shard_map/ppermute | solution.py:41
  17.4 7.0 %slice-start = ((s8[8388608]{0:T(1024)(128)(4,1)}), s8[4194304]{0:T(1024)(128)(4,1)S(1)}, s32[]{:S(2)}) async-start(s8[8388608]{0:T(1024)(128)(4,1)} %bitcast.3), calls=%async_computation | async-start | bytes 8388608
  18.1 18.5 %collective-permute-start.5 = (f32[2,3,32,1024]{3,2,1,0:T(8,128)S(1)}, f32[2,3,32,1024]{3,2,1,0:T(8,128)S(1)}, u32[]{:S(2)}, u32[]{:S(2)}) collective-permute-start(f32[2,3,32,1024]{3,2,1,0:T(8,128)S(1)} %get-tuple-element.42.refs_0_), channel_id=1, source_target_pairs={{0,64},{1,65},{2,66},{3,67},{4,68},{5,69},{6,70},{7,71},{8,72},{9,... | collective-permute-start | bytes 2359304 | tf_op jit(solution)/shard_map/ppermute | solution.py:41
  20.3 20.7 %collective-permute-start.6 = (f32[2,3,32,1024]{3,2,1,0:T(8,128)S(1)}, f32[2,3,32,1024]{3,2,1,0:T(8,128)S(1)}, u32[]{:S(2)}, u32[]{:S(2)}) collective-permute-start(f32[2,3,32,1024]{3,2,1,0:T(8,128)S(1)} %old_one.1), channel_id=1, source_target_pairs={{0,16},{1,17},{2,18},{3,19},{4,20},{5,21},{6,22},{7,23},{8,24},{9,... | collective-permute-start | bytes 2359304 | tf_op jit(solution)/shard_map/ppermute | solution.py:41
  22.6 18.4 %collective-permute-start.7 = (f32[2,3,32,1024]{3,2,1,0:T(8,128)S(1)}, f32[2,3,32,1024]{3,2,1,0:T(8,128)S(1)}, u32[]{:S(2)}, u32[]{:S(2)}) collective-permute-start(f32[2,3,32,1024]{3,2,1,0:T(8,128)S(1)} %old_three.1.after), channel_id=1, source_target_pairs={{0,48},{1,49},{2,50},{3,51},{4,52},{5,53},{6,54},{7,55},{8,56},{9,... | collective-permute-start | bytes 2359304 | tf_op jit(solution)/shard_map/ppermute | solution.py:41
  39.0 24.4 %collective-permute-start.11 = (f32[2,2,16,4096]{3,2,1,0:T(8,128)S(1)}, f32[2,2,16,4096]{3,2,1,0:T(8,128)S(1)}, u32[]{:S(2)}, u32[]{:S(2)}) collective-permute-start(f32[2,2,16,4096]{3,2,1,0:T(8,128)S(1)} %get-tuple-element.46), channel_id=1, source_target_pairs={{0,12},{1,13},{2,14},{3,15},{4,0},{5,1},{6,2},{7,3},{8,4},{9,5},{1... | collective-permute-start | bytes 3145736 | tf_op jit(solution)/shard_map/ppermute | solution.py:41
  39.9 27.3 %collective-permute-start.10 = (f32[2,2,16,4096]{3,2,1,0:T(8,128)S(1)}, f32[2,2,16,4096]{3,2,1,0:T(8,128)S(1)}, u32[]{:S(2)}, u32[]{:S(2)}) collective-permute-start(f32[2,2,16,4096]{3,2,1,0:T(8,128)S(1)} %get-tuple-element.43.refs_2_), channel_id=1, source_target_pairs={{0,4},{1,5},{2,6},{3,7},{4,8},{5,9},{6,10},{7,11},{8,12},{9,13},{1... | collective-permute-start | bytes 3145736 | tf_op jit(solution)/shard_map/ppermute | solution.py:41
  41.2 26.1 %collective-permute-start.12 = (f32[2,3,32,1024]{3,2,1,0:T(8,128)S(1)}, f32[2,3,32,1024]{3,2,1,0:T(8,128)S(1)}, u32[]{:S(2)}, u32[]{:S(2)}) collective-permute-start(f32[2,3,32,1024]{3,2,1,0:T(8,128)S(1)} %other_side.1.after), channel_id=1, source_target_pairs={{0,64},{1,65},{2,66},{3,67},{4,68},{5,69},{6,70},{7,71},{8,72},{9,... | collective-permute-start | bytes 2359304 | tf_op jit(solution)/shard_map/ppermute | solution.py:41
  43.4 28.5 %collective-permute-start.16 = (f32[2,3,32,1024]{3,2,1,0:T(8,128)S(1)}, f32[2,3,32,1024]{3,2,1,0:T(8,128)S(1)}, u32[]{:S(2)}, u32[]{:S(2)}) collective-permute-start(f32[2,3,32,1024]{3,2,1,0:T(8,128)S(1)} %old_two.1.refs_0_), channel_id=1, source_target_pairs={{0,32},{1,33},{2,34},{3,35},{4,36},{5,37},{6,38},{7,39},{8,40},{9,... | collective-permute-start | bytes 2359304 | tf_op jit(solution)/shard_map/ppermute | solution.py:41
  47.0 42.0 %collective-permute-start.8 = (f32[2,2,16,4096]{3,2,1,0:T(8,128)S(1)}, f32[2,2,16,4096]{3,2,1,0:T(8,128)S(1)}, u32[]{:S(2)}, u32[]{:S(2)}) collective-permute-start(f32[2,2,16,4096]{3,2,1,0:T(8,128)S(1)} %get-tuple-element.44), channel_id=1, source_target_pairs={{0,4},{1,5},{2,6},{3,7},{4,8},{5,9},{6,10},{7,11},{8,12},{9,13},{1... | collective-permute-start | bytes 3145736 | tf_op jit(solution)/shard_map/ppermute | solution.py:41
  63.4 25.6 %collective-permute-start.9 = (f32[2,2,16,4096]{3,2,1,0:T(8,128)S(1)}, f32[2,2,16,4096]{3,2,1,0:T(8,128)S(1)}, u32[]{:S(2)}, u32[]{:S(2)}) collective-permute-start(f32[2,2,16,4096]{3,2,1,0:T(8,128)S(1)} %get-tuple-element.45), channel_id=1, source_target_pairs={{0,12},{1,13},{2,14},{3,15},{4,0},{5,1},{6,2},{7,3},{8,4},{9,5},{1... | collective-permute-start | bytes 3145736 | tf_op jit(solution)/shard_map/ppermute | solution.py:41
  68.2 16.9 %collective-permute-start.15 = (f32[8,16,1024]{2,1,0:T(8,128)S(1)}, f32[8,16,1024]{2,1,0:T(8,128)S(1)}, u32[]{:S(2)}, u32[]{:S(2)}) collective-permute-start(f32[8,16,1024]{2,1,0:T(8,128)S(1)} %get-tuple-element.50), channel_id=1, source_target_pairs={{0,2},{1,3},{2,0},{3,1},{4,6},{5,7},{6,4},{7,5},{8,10},{9,11},{10,... | collective-permute-start | bytes 1572872 | tf_op jit(solution)/shard_map/ppermute | solution.py:41
  71.5 13.5 %collective-permute-start.13 = (f32[4,16,1024]{2,1,0:T(8,128)S(1)}, f32[4,16,1024]{2,1,0:T(8,128)S(1)}, u32[]{:S(2)}, u32[]{:S(2)}) collective-permute-start(f32[4,16,1024]{2,1,0:T(8,128)S(1)} %get-tuple-element.48), channel_id=1, source_target_pairs={{0,64},{1,65},{2,66},{3,67},{4,68},{5,69},{6,70},{7,71},{8,72},{9,... | collective-permute-start | bytes 786440 | tf_op jit(solution)/shard_map/ppermute | solution.py:41
  71.8 13.2 %collective-permute-start.14 = (f32[4,16,1024]{2,1,0:T(8,128)S(1)}, f32[4,16,1024]{2,1,0:T(8,128)S(1)}, u32[]{:S(2)}, u32[]{:S(2)}) collective-permute-start(f32[4,16,1024]{2,1,0:T(8,128)S(1)} %get-tuple-element.49), channel_id=1, source_target_pairs={{0,66},{1,67},{2,64},{3,65},{4,70},{5,71},{6,68},{7,69},{8,74},{9,... | collective-permute-start | bytes 786440 | tf_op jit(solution)/shard_map/ppermute | solution.py:41
  85.7 10.4 %collective-permute-start.21 = (f32[2,16,1024]{2,1,0:T(8,128)S(1)}, f32[2,16,1024]{2,1,0:T(8,128)S(1)}, u32[]{:S(2)}, u32[]{:S(2)}) collective-permute-start(f32[2,16,1024]{2,1,0:T(8,128)S(1)} %get-tuple-element.58), channel_id=1, source_target_pairs={{0,32},{1,33},{2,34},{3,35},{4,36},{5,37},{6,38},{7,39},{8,40},{9,... | collective-permute-start | bytes 393224 | tf_op jit(solution)/shard_map/ppermute | solution.py:41
  89.0 13.3 %copy-start.4 = (f32[4,8]{1,0:T(4,128)S(1)}, f32[4,8]{1,0:T(4,128)}, u32[]{:S(2)}) copy-start(f32[4,8]{1,0:T(4,128)} %code.3) | copy-start | bytes 388
  89.9 14.7 %collective-permute-start.17 = (f32[4,16,1024]{2,1,0:T(8,128)S(1)}, f32[4,16,1024]{2,1,0:T(8,128)S(1)}, u32[]{:S(2)}, u32[]{:S(2)}) collective-permute-start(f32[4,16,1024]{2,1,0:T(8,128)S(1)} %get-tuple-element.53), channel_id=1, source_target_pairs={{0,64},{1,65},{2,66},{3,67},{4,68},{5,69},{6,70},{7,71},{8,72},{9,... | collective-permute-start | bytes 786440 | tf_op jit(solution)/shard_map/ppermute | solution.py:41
  91.1 15.9 %collective-permute-start.19 = (f32[4,16,1024]{2,1,0:T(8,128)S(1)}, f32[4,16,1024]{2,1,0:T(8,128)S(1)}, u32[]{:S(2)}, u32[]{:S(2)}) collective-permute-start(f32[4,16,1024]{2,1,0:T(8,128)S(1)} %get-tuple-element.55), channel_id=1, source_target_pairs={{0,2},{1,3},{2,0},{3,1},{4,6},{5,7},{6,4},{7,5},{8,10},{9,11},{10,... | collective-permute-start | bytes 786440 | tf_op jit(solution)/shard_map/ppermute | solution.py:41
  94.1 19.6 %collective-permute-start.18 = (f32[4,16,1024]{2,1,0:T(8,128)S(1)}, f32[4,16,1024]{2,1,0:T(8,128)S(1)}, u32[]{:S(2)}, u32[]{:S(2)}) collective-permute-start(f32[4,16,1024]{2,1,0:T(8,128)S(1)} %get-tuple-element.54), channel_id=1, source_target_pairs={{0,66},{1,67},{2,64},{3,65},{4,70},{5,71},{6,68},{7,69},{8,74},{9,... | collective-permute-start | bytes 786440 | tf_op jit(solution)/shard_map/ppermute | solution.py:41
  94.7 5.0 %collective-permute-start.22 = (f32[2,16,1024]{2,1,0:T(8,128)S(1)}, f32[2,16,1024]{2,1,0:T(8,128)S(1)}, u32[]{:S(2)}, u32[]{:S(2)}) collective-permute-start(f32[2,16,1024]{2,1,0:T(8,128)S(1)} %get-tuple-element.59), channel_id=1, source_target_pairs={{0,48},{1,49},{2,50},{3,51},{4,52},{5,53},{6,54},{7,55},{8,56},{9,... | collective-permute-start | bytes 393224 | tf_op jit(solution)/shard_map/ppermute | solution.py:41
  96.1 6.2 %collective-permute-start.20 = (f32[2,16,1024]{2,1,0:T(8,128)S(1)}, f32[2,16,1024]{2,1,0:T(8,128)S(1)}, u32[]{:S(2)}, u32[]{:S(2)}) collective-permute-start(f32[2,16,1024]{2,1,0:T(8,128)S(1)} %get-tuple-element.51.refs_0_), channel_id=1, source_target_pairs={{0,16},{1,17},{2,18},{3,19},{4,20},{5,21},{6,22},{7,23},{8,24},{9,... | collective-permute-start | bytes 393224 | tf_op jit(solution)/shard_map/ppermute | solution.py:41
  99.6 18.1 %collective-permute-start.23 = (f32[4,16,1024]{2,1,0:T(8,128)S(1)}, f32[4,16,1024]{2,1,0:T(8,128)S(1)}, u32[]{:S(2)}, u32[]{:S(2)}) collective-permute-start(f32[4,16,1024]{2,1,0:T(8,128)S(1)} %get-tuple-element.54), channel_id=1, source_target_pairs={{0,2},{1,3},{2,0},{3,1},{4,6},{5,7},{6,4},{7,5},{8,10},{9,11},{10,... | collective-permute-start | bytes 786440 | tf_op jit(solution)/shard_map/ppermute | solution.py:41
  114.3 6.9 %collective-permute-start.25 = (f32[2,16,1024]{2,1,0:T(8,128)S(1)}, f32[2,16,1024]{2,1,0:T(8,128)S(1)}, u32[]{:S(2)}, u32[]{:S(2)}) collective-permute-start(f32[2,16,1024]{2,1,0:T(8,128)S(1)} %get-tuple-element.66), channel_id=1, source_target_pairs={{0,32},{1,33},{2,34},{3,35},{4,36},{5,37},{6,38},{7,39},{8,40},{9,... | collective-permute-start | bytes 393224 | tf_op jit(solution)/shard_map/ppermute | solution.py:41
  114.7 6.5 %collective-permute-start.26 = (f32[2,16,1024]{2,1,0:T(8,128)S(1)}, f32[2,16,1024]{2,1,0:T(8,128)S(1)}, u32[]{:S(2)}, u32[]{:S(2)}) collective-permute-start(f32[2,16,1024]{2,1,0:T(8,128)S(1)} %get-tuple-element.67), channel_id=1, source_target_pairs={{0,48},{1,49},{2,50},{3,51},{4,52},{5,53},{6,54},{7,55},{8,56},{9,... | collective-permute-start | bytes 393224 | tf_op jit(solution)/shard_map/ppermute | solution.py:41
  117.7 6.2 %collective-permute-start.24 = (f32[2,16,1024]{2,1,0:T(8,128)S(1)}, f32[2,16,1024]{2,1,0:T(8,128)S(1)}, u32[]{:S(2)}, u32[]{:S(2)}) collective-permute-start(f32[2,16,1024]{2,1,0:T(8,128)S(1)} %get-tuple-element.61.after), channel_id=1, source_target_pairs={{0,16},{1,17},{2,18},{3,19},{4,20},{5,21},{6,22},{7,23},{8,24},{9,... | collective-permute-start | bytes 393224 | tf_op jit(solution)/shard_map/ppermute | solution.py:41
  (4 other events, 13.4 us)

commit v5 on v3

--- a/solution.py
+++ b/solution.py
@@ -281,9 +281,10 @@
 
 def advance(weight, first, second, grad):
     first_new = 0.9 * first + 0.1 * grad
-    second_new = 0.95 * second + 0.05 * grad * grad
-    step = first_new / (1.0 - 0.9**10) / (jnp.sqrt(second_new / (1.0 - 0.95**10)) + 1e-08)
-    return weight - 0.01 * (step + 0.1 * weight), first_new, second_new
+    second_new = 0.95 * second + 0.05 * (grad * grad)
+    root = jnp.sqrt(second_new * (1.0 / (1.0 - 0.95**10))) + 1e-08
+    step = (first_new * (0.01 / (1.0 - 0.9**10))) * pl.reciprocal(root, approx=True)
+    return (1.0 - 0.01 * 0.1) * weight - step, first_new, second_new
 
 
 def update(holder, weight, first, second, mine, across):
@@ -325,7 +326,7 @@
             places[a][s] = (known[0] if known else len(arrays) - 1, part)
 
     def body(code, *refs):
-        olds, ins, (out, total, sem) = refs[: len(arrays)], refs[len(arrays) :], (refs[-4], *refs[-2:])
+        olds, ins, (out, total, sems) = refs[: len(arrays)], refs[len(arrays) :], (refs[-4], *refs[-2:])
         _, _, _, side, y = position()
         ranks = [[lax.rem(side + a, 2) * 4 + lax.rem(y + 4 - s, 4) for s in range(4)] for a in range(2)]
         scales = [[[code[j, ranks[a][s]] for s in range(4)] for a in range(2)] for j in range(4)]
@@ -334,6 +335,7 @@
             array, part = places[a][s]
             return olds[array][part, k, pl.ds(16 * c + row, 8), columns]
 
+        copies = []
         for row in range(0, 16, 8):
 
             def one(columns):
@@ -351,10 +353,14 @@
                     for k in range(3):
                         total[j, k, rows, columns] = sums[j][k]
 
-            by_tiles(1024, 256, one)
-        copy = pltpu.make_async_copy(total, out.at[:, :, pl.ds(16 * c, 16)], sem)
-        copy.start()
-        copy.wait()
+            for lane in range(0, 1024, 256):
+                one(pl.ds(lane, 256))
+                there = out.at[:, :, pl.ds(16 * c + row, 8), pl.ds(lane, 256)]
+                made = total.at[:, :, pl.ds(row, 8), pl.ds(lane, 256)]
+                copies.append(pltpu.make_async_copy(made, there, sems.at[len(copies)]))
+                copies[-1].start()
+        for copy in copies:
+            copy.wait()
         refs[-3][...] = jnp.zeros((8, 128), F32)
 
     return call(
@@ -362,7 +368,7 @@
         body,
         [(code, SMEM)] + [(array, VMEM) for array in (*arrays, *grads)] + ([] if into is None else [(into, HBM)]),
         [((4, 3, 32, 1024), F32, HBM), ((8, 128), F32, VMEM)],
-        [pltpu.VMEM((4, 3, 16, 1024), F32), pltpu.SemaphoreType.DMA],
+        [pltpu.VMEM((4, 3, 16, 1024), F32), pltpu.SemaphoreType.DMA((8,))],
         aliases=None if into is None else {1 + len(arrays) + len(grads): 0},
     )
 
@@ -383,14 +389,14 @@
     beside = send(beside, BESIDE)
 
     held = send(holder, ACROSS)
-    odd = other_side([one, three], [(beside, VMEM), (held, SMEM)])
+    odd = other_side([one, three], [(beside, VMEM)])
     (two,) = old_parts("old_two", holder, states, [[(0, 2), (1, 2)]], (odd,))
     after = (two,)
     odd, two = send(odd, BESIDE), send(two, ALONG_Y[2])
 
     go_up, go_down = onward(own, rest, far_below, far_above, 0, after)
     along_z = [(send(go_up, UP_Z), send(go_down, DOWN_Z))]
-    even = other_side([two], [(odd, VMEM), (go_up, VMEM)])
+    even = other_side([two], [(odd, VMEM), (go_up, VMEM), (held, SMEM)])
     after = (even,)
     even = send(even, BESIDE)
     go_up, go_down = onward(own, rest, far_below, far_above, 1, after)

time: 116 us -> 116 us (level)
  starting transfers between devices: 46.4 us -> 41.9 us
  waiting for transfers between devices: 47.8 us -> 52.1 us
    ppermute x28, starting transfers between devices: 46.4 us -> 41.9 us  [send(): return lax.ppermute(array, AXES, pairs)]
    ppermute x28, waiting for transfers between devices: 47.8 us -> 52.1 us  [send(): return lax.ppermute(array, AXES, pairs)]
  transfers between devices with their start and end apart: 28 -> 28, of which waited for: 13 -> 9; matrix products, arithmetic and copies ran while one was open for 0% -> 0% of each run, Pallas kernels for 13% -> 13%
where the time goes in v5:
time: 116 us; the launch traced here: 115 us
  waiting for transfers between devices  52.1 us (45%)
  starting transfers between devices  41.9 us (36%)
  Pallas kernels  19.8 us (17%)
    ppermute x28, waiting for transfers between devices, send(): return lax.ppermute(array, AXES, pairs)  52.1 us
    ppermute x28, starting transfers between devices, send(): return lax.ppermute(array, AXES, pairs)  41.9 us
    pallas_call x17, Pallas kernels, call(): pl.pallas_call(body, out_shape=[jax.ShapeDtypeStruct(shape, kind) for sha...  19.8 us
  transfers between devices with their start and end apart: 28, of which 9 were waited for; matrix products, arithmetic and copies ran while one was open for 0% of the time, Pallas kernels for 13%

profile of v5, /device:TPU:0, one launch (start us, length us, event | category | flops | bytes accessed | tf_op | source)
XLA Modules:
  0.0 115.3 jit_solution(3944349812201684334)
XLA Ops:
  1.3 1.9 %widen_far.1.far = f32[2,32,8192]{2,1,0:T(8,128)S(1)} custom-call(bf16[16,32,8192]{2,1,0:T(8,128)(2,1)} %bitcast.1, s32[1,16]{1,0:T(1,128)S(1)} %copy-done.5), custom_call_target="tpu_custom_call" | custom-call | tf_op jit(solution)/shard_map/widen_far/pallas_call | solution.py:44
  3.3 3.8 %widen_rest.1 = (f32[6,32,8192]{2,1,0:T(8,128)S(1)}, bf16[8,32,8192]{2,1,0:T(8,128)(2,1)S(1)}) custom-call(bf16[16,32,8192]{2,1,0:T(8,128)(2,1)} %bitcast.2, s32[1,16]{1,0:T(1,128)S(1)} %copy-done.6, f32[2,32,8192]{2,1,0:T(8,128)S(1)} %widen_far.1.far), custom_call_target="tpu_custom_call" | custom-call | tf_op jit(solution)/shard_map/widen_rest/pallas_call | solution.py:44
  8.0 2.0 %collective-permute-start.3 = (f32[2,32,4096]{2,1,0:T(8,128)S(1)}, f32[2,32,4096]{2,1,0:T(8,128)S(1)}, u32[]{:S(2)}, u32[]{:S(2)}) collective-permute-start(f32[2,32,4096]{2,1,0:T(8,128)S(1)} %get-tuple-element.42.refs_0_), channel_id=1, source_target_pairs={{0,4},{1,5},{2,6},{3,7},{4,8},{5,9},{6,10},{7,11},{8,12},{9,13},{1... | collective-permute-start | bytes 3145736 | tf_op jit(solution)/shard_map/ppermute | solution.py:40
  10.0 2.1 %collective-permute-start.4 = (f32[2,32,4096]{2,1,0:T(8,128)S(1)}, f32[2,32,4096]{2,1,0:T(8,128)S(1)}, u32[]{:S(2)}, u32[]{:S(2)}) collective-permute-start(f32[2,32,4096]{2,1,0:T(8,128)S(1)} %get-tuple-element.43), channel_id=1, source_target_pairs={{0,12},{1,13},{2,14},{3,15},{4,0},{5,1},{6,2},{7,3},{8,4},{9,5},{1... | collective-permute-start | bytes 3145736 | tf_op jit(solution)/shard_map/ppermute | solution.py:40
  12.9 1.6 %collective-permute-start.5 = (f32[2,3,32,1024]{3,2,1,0:T(8,128)S(1)}, f32[2,3,32,1024]{3,2,1,0:T(8,128)S(1)}, u32[]{:S(2)}, u32[]{:S(2)}) collective-permute-start(f32[2,3,32,1024]{3,2,1,0:T(8,128)S(1)} %get-tuple-element.44), channel_id=1, source_target_pairs={{0,16},{1,17},{2,18},{3,19},{4,20},{5,21},{6,22},{7,23},{8,24},{9,... | collective-permute-start | bytes 2359304 | tf_op jit(solution)/shard_map/ppermute | solution.py:40
  14.5 1.7 %collective-permute-start.6 = (f32[2,3,32,1024]{3,2,1,0:T(8,128)S(1)}, f32[2,3,32,1024]{3,2,1,0:T(8,128)S(1)}, u32[]{:S(2)}, u32[]{:S(2)}) collective-permute-start(f32[2,3,32,1024]{3,2,1,0:T(8,128)S(1)} %get-tuple-element.45), channel_id=1, source_target_pairs={{0,48},{1,49},{2,50},{3,51},{4,52},{5,53},{6,54},{7,55},{8,56},{9,... | collective-permute-start | bytes 2359304 | tf_op jit(solution)/shard_map/ppermute | solution.py:40
  16.2 1.8 %collective-permute-done.1.refs_0_.rest = f32[6,32,8192]{2,1,0:T(8,128)S(1)} collective-permute-done((f32[6,32,8192]{2,1,0:T(8,128)S(1)}, f32[6,32,8192]{2,1,0:T(8,128)S(1)}, u32[]{:S(2)}, u32[]{:S(2)}) %collective-permute-start.1) | collective-permute-done | bytes 6291488 | tf_op jit(solution)/shard_map/ppermute | solution.py:40
  18.6 1.7 %collective-permute-start.7 = (f32[1,3,32,1024]{3,2,1,0:T(8,128)S(1)}, f32[1,3,32,1024]{3,2,1,0:T(8,128)S(1)}, u32[]{:S(2)}, u32[]{:S(2)}) collective-permute-start(f32[1,3,32,1024]{3,2,1,0:T(8,128)S(1)} %get-tuple-element.46), channel_id=1, source_target_pairs={{0,64},{1,65},{2,66},{3,67},{4,68},{5,69},{6,70},{7,71},{8,72},{9,... | collective-permute-start | bytes 1179656 | tf_op jit(solution)/shard_map/ppermute | solution.py:40
  20.2 13.4 %collective-permute-done.5.refs_0_.refs_1_ = f32[2,3,32,1024]{3,2,1,0:T(8,128)S(1)} collective-permute-done((f32[2,3,32,1024]{3,2,1,0:T(8,128)S(1)}, f32[2,3,32,1024]{3,2,1,0:T(8,128)S(1)}, u32[]{:S(2)}, u32[]{:S(2)}) %collective-permute-start.5) | collective-permute-done | bytes 786464 | tf_op jit(solution)/shard_map/ppermute | solution.py:40
  34.4 3.0 %collective-permute-start.10 = (f32[2,3,32,1024]{3,2,1,0:T(8,128)S(1)}, f32[2,3,32,1024]{3,2,1,0:T(8,128)S(1)}, u32[]{:S(2)}, u32[]{:S(2)}) collective-permute-start(f32[2,3,32,1024]{3,2,1,0:T(8,128)S(1)} %old_two.1.refs_0_), channel_id=1, source_target_pairs={{0,32},{1,33},{2,34},{3,35},{4,36},{5,37},{6,38},{7,39},{8,40},{9,... | collective-permute-start | bytes 2359304 | tf_op jit(solution)/shard_map/ppermute | solution.py:40
  37.4 1.5 %collective-permute-start.11 = (f32[2,3,32,1024]{3,2,1,0:T(8,128)S(1)}, f32[2,3,32,1024]{3,2,1,0:T(8,128)S(1)}, u32[]{:S(2)}, u32[]{:S(2)}) collective-permute-start(f32[2,3,32,1024]{3,2,1,0:T(8,128)S(1)} %other_side.2.refs_0_), channel_id=1, source_target_pairs={{0,64},{1,65},{2,66},{3,67},{4,68},{5,69},{6,70},{7,71},{8,72},{9,... | collective-permute-start | bytes 2359304 | tf_op jit(solution)/shard_map/ppermute | solution.py:40
  39.3 3.2 %collective-permute-start.9 = (f32[2,2,16,4096]{3,2,1,0:T(8,128)S(1)}, f32[2,2,16,4096]{3,2,1,0:T(8,128)S(1)}, u32[]{:S(2)}, u32[]{:S(2)}) collective-permute-start(f32[2,2,16,4096]{3,2,1,0:T(8,128)S(1)} %get-tuple-element.48), channel_id=1, source_target_pairs={{0,12},{1,13},{2,14},{3,15},{4,0},{5,1},{6,2},{7,3},{8,4},{9,5},{1... | collective-permute-start | bytes 3145736 | tf_op jit(solution)/shard_map/ppermute | solution.py:40
  42.6 2.7 %collective-permute-start.2 = (s32[1,8]{1,0:T(1,128)S(1)}, s32[1,8]{1,0:T(1,128)S(1)}, u32[]{:S(2)}, u32[]{:S(2)}) collective-permute-start(s32[1,8]{1,0:T(1,128)S(1)} %copy-done.3), channel_id=1, source_target_pairs={{0,2},{1,3},{2,0},{3,1},{4,6},{5,7},{6,4},{7,5},{8,10},{9,11},{10,... | collective-permute-start | bytes 104 | tf_op jit(solution)/shard_map/ppermute | solution.py:40
  45.3 12.3 %collective-permute-done.2.refs_3_.other_held = s32[1,8]{1,0:T(1,128)S(1)} collective-permute-done((s32[1,8]{1,0:T(1,128)S(1)}, s32[1,8]{1,0:T(1,128)S(1)}, u32[]{:S(2)}, u32[]{:S(2)}) %collective-permute-start.2) | collective-permute-done | bytes 64 | tf_op jit(solution)/shard_map/ppermute | solution.py:40
  58.6 3.2 %collective-permute-start.13 = (f32[2,2,16,4096]{3,2,1,0:T(8,128)S(1)}, f32[2,2,16,4096]{3,2,1,0:T(8,128)S(1)}, u32[]{:S(2)}, u32[]{:S(2)}) collective-permute-start(f32[2,2,16,4096]{3,2,1,0:T(8,128)S(1)} %get-tuple-element.51), channel_id=1, source_target_pairs={{0,12},{1,13},{2,14},{3,15},{4,0},{5,1},{6,2},{7,3},{8,4},{9,5},{1... | collective-permute-start | bytes 3145736 | tf_op jit(solution)/shard_map/ppermute | solution.py:40
  62.1 4.5 %collective-permute-done.8.below = f32[2,2,16,4096]{3,2,1,0:T(8,128)S(1)} collective-permute-done((f32[2,2,16,4096]{3,2,1,0:T(8,128)S(1)}, f32[2,2,16,4096]{3,2,1,0:T(8,128)S(1)}, u32[]{:S(2)}, u32[]{:S(2)}) %collective-permute-start.8) | collective-permute-done | bytes 1048608 | tf_op jit(solution)/shard_map/ppermute | solution.py:40
  66.6 0.9 gathered_z_0.1
  67.6 2.8 %collective-permute-start.14 = (f32[8,16,1024]{2,1,0:T(8,128)S(1)}, f32[8,16,1024]{2,1,0:T(8,128)S(1)}, u32[]{:S(2)}, u32[]{:S(2)}) collective-permute-start(f32[8,16,1024]{2,1,0:T(8,128)S(1)} %get-tuple-element.52), channel_id=1, source_target_pairs={{0,2},{1,3},{2,0},{3,1},{4,6},{5,7},{6,4},{7,5},{8,10},{9,11},{10,... | collective-permute-start | bytes 1572872 | tf_op jit(solution)/shard_map/ppermute | solution.py:40
  70.6 3.0 %collective-permute-done.17.after.refs_6_ = f32[1,3,32,1024]{3,2,1,0:T(8,128)S(1)} collective-permute-done((f32[1,3,32,1024]{3,2,1,0:T(8,128)S(1)}, f32[1,3,32,1024]{3,2,1,0:T(8,128)S(1)}, u32[]{:S(2)}, u32[]{:S(2)}) %collective-permute-start.17) | collective-permute-done | bytes 393248 | tf_op jit(solution)/shard_map/ppermute | solution.py:40
  74.1 12.4 %collective-permute-done.15.beside = f32[4,16,1024]{2,1,0:T(8,128)S(1)} collective-permute-done((f32[4,16,1024]{2,1,0:T(8,128)S(1)}, f32[4,16,1024]{2,1,0:T(8,128)S(1)}, u32[]{:S(2)}, u32[]{:S(2)}) %collective-permute-start.15) | collective-permute-done | bytes 262176 | tf_op jit(solution)/shard_map/ppermute | solution.py:40
  87.1 1.4 %collective-permute-start.22 = (f32[2,16,1024]{2,1,0:T(8,128)S(1)}, f32[2,16,1024]{2,1,0:T(8,128)S(1)}, u32[]{:S(2)}, u32[]{:S(2)}) collective-permute-start(f32[2,16,1024]{2,1,0:T(8,128)S(1)} %get-tuple-element.55.refs_0_), channel_id=1, source_target_pairs={{0,16},{1,17},{2,18},{3,19},{4,20},{5,21},{6,22},{7,23},{8,24},{9,... | collective-permute-start | bytes 393224 | tf_op jit(solution)/shard_map/ppermute | solution.py:40
  89.4 1.3 %collective-permute-start.18 = (f32[4,16,1024]{2,1,0:T(8,128)S(1)}, f32[4,16,1024]{2,1,0:T(8,128)S(1)}, u32[]{:S(2)}, u32[]{:S(2)}) collective-permute-start(f32[4,16,1024]{2,1,0:T(8,128)S(1)} %get-tuple-element.57), channel_id=1, source_target_pairs={{0,2},{1,3},{2,0},{3,1},{4,6},{5,7},{6,4},{7,5},{8,10},{9,11},{10,... | collective-permute-start | bytes 786440 | tf_op jit(solution)/shard_map/ppermute | solution.py:40
  91.3 2.3 %collective-permute-start.21 = (f32[4,16,1024]{2,1,0:T(8,128)S(1)}, f32[4,16,1024]{2,1,0:T(8,128)S(1)}, u32[]{:S(2)}, u32[]{:S(2)}) collective-permute-start(f32[4,16,1024]{2,1,0:T(8,128)S(1)} %get-tuple-element.58), channel_id=1, source_target_pairs={{0,66},{1,67},{2,64},{3,65},{4,70},{5,71},{6,68},{7,69},{8,74},{9,... | collective-permute-start | bytes 786440 | tf_op jit(solution)/shard_map/ppermute | solution.py:40
  93.6 1.9 %collective-permute-start.23 = (f32[2,16,1024]{2,1,0:T(8,128)S(1)}, f32[2,16,1024]{2,1,0:T(8,128)S(1)}, u32[]{:S(2)}, u32[]{:S(2)}) collective-permute-start(f32[2,16,1024]{2,1,0:T(8,128)S(1)} %get-tuple-element.65), channel_id=1, source_target_pairs={{0,32},{1,33},{2,34},{3,35},{4,36},{5,37},{6,38},{7,39},{8,40},{9,... | collective-permute-start | bytes 393224 | tf_op jit(solution)/shard_map/ppermute | solution.py:40
  96.4 3.7 %collective-permute-done.23.refs_9_ = f32[2,16,1024]{2,1,0:T(8,128)S(1)} collective-permute-done((f32[2,16,1024]{2,1,0:T(8,128)S(1)}, f32[2,16,1024]{2,1,0:T(8,128)S(1)}, u32[]{:S(2)}, u32[]{:S(2)}) %collective-permute-start.23) | collective-permute-done | bytes 131104 | tf_op jit(solution)/shard_map/ppermute | solution.py:40
  100.1 1.2 %collective-permute-start.19 = (f32[4,16,1024]{2,1,0:T(8,128)S(1)}, f32[4,16,1024]{2,1,0:T(8,128)S(1)}, u32[]{:S(2)}, u32[]{:S(2)}) collective-permute-start(f32[4,16,1024]{2,1,0:T(8,128)S(1)} %get-tuple-element.58), channel_id=1, source_target_pairs={{0,2},{1,3},{2,0},{3,1},{4,6},{5,7},{6,4},{7,5},{8,10},{9,11},{10,... | collective-permute-start | bytes 786440 | tf_op jit(solution)/shard_map/ppermute | solution.py:40
  101.3 2.1 %encode_0.1 = (f32[4,3,32,1024]{3,2,1,0:T(8,128)}, f32[8,128]{1,0:T(8,128)S(1)}) custom-call(f32[4,8]{1,0:T(4,128)S(1)} %copy-done.4, f32[1,3,32,1024]{3,2,1,0:T(8,128)S(1)} %get-tuple-element.62.refs_0_, f32[2,3,32,1024]{3,2,1,0:T(8,128)S(1)} %collective-permute-done.5.refs_0_.refs_1_, f32[2,3,32,1024]{3,2,1,0:T(8,128)S(1)} %collective-permute-done.10.refs_0_.refs_2_, ...), custom_call_target="tpu_custom_call" | custom-call | tf_op jit(solution)/shard_map/encode_0/pallas_call | solution.py:44
  104.0 1.5 %collective-permute-start.25 = (f32[2,16,1024]{2,1,0:T(8,128)S(1)}, f32[2,16,1024]{2,1,0:T(8,128)S(1)}, u32[]{:S(2)}, u32[]{:S(2)}) collective-permute-start(f32[2,16,1024]{2,1,0:T(8,128)S(1)} %get-tuple-element.69), channel_id=1, source_target_pairs={{0,16},{1,17},{2,18},{3,19},{4,20},{5,21},{6,22},{7,23},{8,24},{9,... | collective-permute-start | bytes 393224 | tf_op jit(solution)/shard_map/ppermute | solution.py:40
  105.5 2.2 %collective-permute-start.26 = (f32[2,16,1024]{2,1,0:T(8,128)S(1)}, f32[2,16,1024]{2,1,0:T(8,128)S(1)}, u32[]{:S(2)}, u32[]{:S(2)}) collective-permute-start(f32[2,16,1024]{2,1,0:T(8,128)S(1)} %get-tuple-element.70), channel_id=1, source_target_pairs={{0,32},{1,33},{2,34},{3,35},{4,36},{5,37},{6,38},{7,39},{8,40},{9,... | collective-permute-start | bytes 393224 | tf_op jit(solution)/shard_map/ppermute | solution.py:40
  107.7 1.7 %collective-permute-start.27 = (f32[2,16,1024]{2,1,0:T(8,128)S(1)}, f32[2,16,1024]{2,1,0:T(8,128)S(1)}, u32[]{:S(2)}, u32[]{:S(2)}) collective-permute-start(f32[2,16,1024]{2,1,0:T(8,128)S(1)} %get-tuple-element.71), channel_id=1, source_target_pairs={{0,48},{1,49},{2,50},{3,51},{4,52},{5,53},{6,54},{7,55},{8,56},{9,... | collective-permute-start | bytes 393224 | tf_op jit(solution)/shard_map/ppermute | solution.py:40
  109.4 2.7 %update.1 = (f32[1,32,8192]{2,1,0:T(8,128)}, f32[1,32,8192]{2,1,0:T(8,128)}, f32[1,32,8192]{2,1,0:T(8,128)}) custom-call(s32[1,8]{1,0:T(1,128)S(1)} %copy-done.3, f32[1,32,8192]{2,1,0:T(8,128)S(1)} %copy-done, f32[1,32,8192]{2,1,0:T(8,128)S(1)} %copy-done.1, f32[1,32,8192]{2,1,0:T(8,128)S(1)} %copy-done.2, f32[16,8192]{1,0:T(8,128)S(1)} %get-tuple-element.49.mine.mine_0, ...), custom_call_target="tpu_custom_call" | custom-call | tf_op jit(solution)/shard_map/update/pallas_call | solution.py:44
  112.7 2.6 %encode_1.1 = (f32[4,3,32,1024]{3,2,1,0:T(8,128)}, f32[8,128]{1,0:T(8,128)}) custom-call(f32[4,8]{1,0:T(4,128)S(1)} %copy-done.4, f32[1,3,32,1024]{3,2,1,0:T(8,128)S(1)} %get-tuple-element.62.refs_0_, f32[2,3,32,1024]{3,2,1,0:T(8,128)S(1)} %collective-permute-done.5.refs_0_.refs_1_, ...), custom_call_target="tpu_custom_call", output_to_operand_aliasing={{0}: (12, {})} | custom-call | tf_op jit(solution)/shard_map/encode_1/pallas_call | solution.py:44
  (55 shorter events, 10.4 us)
Async XLA Ops:
  3.2 4.2 %collective-permute-start = (f32[2,32,8192]{2,1,0:T(8,128)S(1)}, f32[2,32,8192]{2,1,0:T(8,128)S(1)}, u32[]{:S(2)}, u32[]{:S(2)}) collective-permute-start(f32[2,32,8192]{2,1,0:T(8,128)S(1)} %widen_far.1.far), channel_id=1, source_target_pairs={{0,1},{1,0},{2,3},{3,2},{4,5},{5,4},{6,7},{7,6},{8,9},{9,8},{10,11... | collective-permute-start | bytes 6291464 | tf_op jit(solution)/shard_map/ppermute | solution.py:40
  7.4 4.7 %copy-start.1 = (f32[1,32,8192]{2,1,0:T(8,128)S(1)}, f32[1,32,8192]{2,1,0:T(8,128)}, u32[]{:S(2)}) copy-start(f32[1,32,8192]{2,1,0:T(8,128)} %first.7) | copy-start | bytes 3145732
  7.4 4.7 %copy-start.2 = (f32[1,32,8192]{2,1,0:T(8,128)S(1)}, f32[1,32,8192]{2,1,0:T(8,128)}, u32[]{:S(2)}) copy-start(f32[1,32,8192]{2,1,0:T(8,128)} %second.7) | copy-start | bytes 3145732
  7.4 4.7 %copy-start.3 = (s32[1,8]{1,0:T(1,128)S(1)}, s32[1,8]{1,0:T(1,128)}, u32[]{:S(2)}) copy-start(s32[1,8]{1,0:T(1,128)} %holder.11) | copy-start | bytes 100
  7.7 10.2 %collective-permute-start.1 = (f32[6,32,8192]{2,1,0:T(8,128)S(1)}, f32[6,32,8192]{2,1,0:T(8,128)S(1)}, u32[]{:S(2)}, u32[]{:S(2)}) collective-permute-start(f32[6,32,8192]{2,1,0:T(8,128)S(1)} %get-tuple-element.41), channel_id=1, source_target_pairs={{0,1},{1,0},{2,3},{3,2},{4,5},{5,4},{6,7},{7,6},{8,9},{9,8},{10,11... | collective-permute-start | bytes 18874376 | tf_op jit(solution)/shard_map/ppermute | solution.py:40
  8.0 30.9 %collective-permute-start.3 = (f32[2,32,4096]{2,1,0:T(8,128)S(1)}, f32[2,32,4096]{2,1,0:T(8,128)S(1)}, u32[]{:S(2)}, u32[]{:S(2)}) collective-permute-start(f32[2,32,4096]{2,1,0:T(8,128)S(1)} %get-tuple-element.42.refs_0_), channel_id=1, source_target_pairs={{0,4},{1,5},{2,6},{3,7},{4,8},{5,9},{6,10},{7,11},{8,12},{9,13},{1... | collective-permute-start | bytes 3145736 | tf_op jit(solution)/shard_map/ppermute | solution.py:40
  10.0 28.9 %collective-permute-start.4 = (f32[2,32,4096]{2,1,0:T(8,128)S(1)}, f32[2,32,4096]{2,1,0:T(8,128)S(1)}, u32[]{:S(2)}, u32[]{:S(2)}) collective-permute-start(f32[2,32,4096]{2,1,0:T(8,128)S(1)} %get-tuple-element.43), channel_id=1, source_target_pairs={{0,12},{1,13},{2,14},{3,15},{4,0},{5,1},{6,2},{7,3},{8,4},{9,5},{1... | collective-permute-start | bytes 3145736 | tf_op jit(solution)/shard_map/ppermute | solution.py:40
  12.9 20.8 %collective-permute-start.5 = (f32[2,3,32,1024]{3,2,1,0:T(8,128)S(1)}, f32[2,3,32,1024]{3,2,1,0:T(8,128)S(1)}, u32[]{:S(2)}, u32[]{:S(2)}) collective-permute-start(f32[2,3,32,1024]{3,2,1,0:T(8,128)S(1)} %get-tuple-element.44), channel_id=1, source_target_pairs={{0,16},{1,17},{2,18},{3,19},{4,20},{5,21},{6,22},{7,23},{8,24},{9,... | collective-permute-start | bytes 2359304 | tf_op jit(solution)/shard_map/ppermute | solution.py:40
  14.5 19.2 %collective-permute-start.6 = (f32[2,3,32,1024]{3,2,1,0:T(8,128)S(1)}, f32[2,3,32,1024]{3,2,1,0:T(8,128)S(1)}, u32[]{:S(2)}, u32[]{:S(2)}) collective-permute-start(f32[2,3,32,1024]{3,2,1,0:T(8,128)S(1)} %get-tuple-element.45), channel_id=1, source_target_pairs={{0,48},{1,49},{2,50},{3,51},{4,52},{5,53},{6,54},{7,55},{8,56},{9,... | collective-permute-start | bytes 2359304 | tf_op jit(solution)/shard_map/ppermute | solution.py:40
  18.6 15.1 %collective-permute-start.7 = (f32[1,3,32,1024]{3,2,1,0:T(8,128)S(1)}, f32[1,3,32,1024]{3,2,1,0:T(8,128)S(1)}, u32[]{:S(2)}, u32[]{:S(2)}) collective-permute-start(f32[1,3,32,1024]{3,2,1,0:T(8,128)S(1)} %get-tuple-element.46), channel_id=1, source_target_pairs={{0,64},{1,65},{2,66},{3,67},{4,68},{5,69},{6,70},{7,71},{8,72},{9,... | collective-permute-start | bytes 1179656 | tf_op jit(solution)/shard_map/ppermute | solution.py:40
  34.4 23.2 %collective-permute-start.10 = (f32[2,3,32,1024]{3,2,1,0:T(8,128)S(1)}, f32[2,3,32,1024]{3,2,1,0:T(8,128)S(1)}, u32[]{:S(2)}, u32[]{:S(2)}) collective-permute-start(f32[2,3,32,1024]{3,2,1,0:T(8,128)S(1)} %old_two.1.refs_0_), channel_id=1, source_target_pairs={{0,32},{1,33},{2,34},{3,35},{4,36},{5,37},{6,38},{7,39},{8,40},{9,... | collective-permute-start | bytes 2359304 | tf_op jit(solution)/shard_map/ppermute | solution.py:40
  37.4 20.2 %collective-permute-start.11 = (f32[2,3,32,1024]{3,2,1,0:T(8,128)S(1)}, f32[2,3,32,1024]{3,2,1,0:T(8,128)S(1)}, u32[]{:S(2)}, u32[]{:S(2)}) collective-permute-start(f32[2,3,32,1024]{3,2,1,0:T(8,128)S(1)} %other_side.2.refs_0_), channel_id=1, source_target_pairs={{0,64},{1,65},{2,66},{3,67},{4,68},{5,69},{6,70},{7,71},{8,72},{9,... | collective-permute-start | bytes 2359304 | tf_op jit(solution)/shard_map/ppermute | solution.py:40
  39.2 27.4 %collective-permute-start.8 = (f32[2,2,16,4096]{3,2,1,0:T(8,128)S(1)}, f32[2,2,16,4096]{3,2,1,0:T(8,128)S(1)}, u32[]{:S(2)}, u32[]{:S(2)}) collective-permute-start(f32[2,2,16,4096]{3,2,1,0:T(8,128)S(1)} %get-tuple-element.47.refs_2_), channel_id=1, source_target_pairs={{0,4},{1,5},{2,6},{3,7},{4,8},{5,9},{6,10},{7,11},{8,12},{9,13},{1... | collective-permute-start | bytes 3145736 | tf_op jit(solution)/shard_map/ppermute | solution.py:40
  39.3 27.3 %collective-permute-start.9 = (f32[2,2,16,4096]{3,2,1,0:T(8,128)S(1)}, f32[2,2,16,4096]{3,2,1,0:T(8,128)S(1)}, u32[]{:S(2)}, u32[]{:S(2)}) collective-permute-start(f32[2,2,16,4096]{3,2,1,0:T(8,128)S(1)} %get-tuple-element.48), channel_id=1, source_target_pairs={{0,12},{1,13},{2,14},{3,15},{4,0},{5,1},{6,2},{7,3},{8,4},{9,5},{1... | collective-permute-start | bytes 3145736 | tf_op jit(solution)/shard_map/ppermute | solution.py:40
  42.6 15.0 %collective-permute-start.2 = (s32[1,8]{1,0:T(1,128)S(1)}, s32[1,8]{1,0:T(1,128)S(1)}, u32[]{:S(2)}, u32[]{:S(2)}) collective-permute-start(s32[1,8]{1,0:T(1,128)S(1)} %copy-done.3), channel_id=1, source_target_pairs={{0,2},{1,3},{2,0},{3,1},{4,6},{5,7},{6,4},{7,5},{8,10},{9,11},{10,... | collective-permute-start | bytes 104 | tf_op jit(solution)/shard_map/ppermute | solution.py:40
  58.5 30.0 %collective-permute-start.12 = (f32[2,2,16,4096]{3,2,1,0:T(8,128)S(1)}, f32[2,2,16,4096]{3,2,1,0:T(8,128)S(1)}, u32[]{:S(2)}, u32[]{:S(2)}) collective-permute-start(f32[2,2,16,4096]{3,2,1,0:T(8,128)S(1)} %get-tuple-element.50), channel_id=1, source_target_pairs={{0,4},{1,5},{2,6},{3,7},{4,8},{5,9},{6,10},{7,11},{8,12},{9,13},{1... | collective-permute-start | bytes 3145736 | tf_op jit(solution)/shard_map/ppermute | solution.py:40
  58.6 29.9 %collective-permute-start.13 = (f32[2,2,16,4096]{3,2,1,0:T(8,128)S(1)}, f32[2,2,16,4096]{3,2,1,0:T(8,128)S(1)}, u32[]{:S(2)}, u32[]{:S(2)}) collective-permute-start(f32[2,2,16,4096]{3,2,1,0:T(8,128)S(1)} %get-tuple-element.51), channel_id=1, source_target_pairs={{0,12},{1,13},{2,14},{3,15},{4,0},{5,1},{6,2},{7,3},{8,4},{9,5},{1... | collective-permute-start | bytes 3145736 | tf_op jit(solution)/shard_map/ppermute | solution.py:40
  61.9 11.8 %collective-permute-start.17 = (f32[1,3,32,1024]{3,2,1,0:T(8,128)S(1)}, f32[1,3,32,1024]{3,2,1,0:T(8,128)S(1)}, u32[]{:S(2)}, u32[]{:S(2)}) collective-permute-start(f32[1,3,32,1024]{3,2,1,0:T(8,128)S(1)} %other_side.3.refs_0_), channel_id=1, source_target_pairs={{0,64},{1,65},{2,66},{3,67},{4,68},{5,69},{6,70},{7,71},{8,72},{9,... | collective-permute-start | bytes 1179656 | tf_op jit(solution)/shard_map/ppermute | solution.py:40
  67.6 18.9 %collective-permute-start.14 = (f32[8,16,1024]{2,1,0:T(8,128)S(1)}, f32[8,16,1024]{2,1,0:T(8,128)S(1)}, u32[]{:S(2)}, u32[]{:S(2)}) collective-permute-start(f32[8,16,1024]{2,1,0:T(8,128)S(1)} %get-tuple-element.52), channel_id=1, source_target_pairs={{0,2},{1,3},{2,0},{3,1},{4,6},{5,7},{6,4},{7,5},{8,10},{9,11},{10,... | collective-permute-start | bytes 1572872 | tf_op jit(solution)/shard_map/ppermute | solution.py:40
  70.4 16.1 %collective-permute-start.15 = (f32[4,16,1024]{2,1,0:T(8,128)S(1)}, f32[4,16,1024]{2,1,0:T(8,128)S(1)}, u32[]{:S(2)}, u32[]{:S(2)}) collective-permute-start(f32[4,16,1024]{2,1,0:T(8,128)S(1)} %get-tuple-element.53), channel_id=1, source_target_pairs={{0,64},{1,65},{2,66},{3,67},{4,68},{5,69},{6,70},{7,71},{8,72},{9,... | collective-permute-start | bytes 786440 | tf_op jit(solution)/shard_map/ppermute | solution.py:40
  73.6 12.9 %collective-permute-start.16 = (f32[4,16,1024]{2,1,0:T(8,128)S(1)}, f32[4,16,1024]{2,1,0:T(8,128)S(1)}, u32[]{:S(2)}, u32[]{:S(2)}) collective-permute-start(f32[4,16,1024]{2,1,0:T(8,128)S(1)} %get-tuple-element.54), channel_id=1, source_target_pairs={{0,66},{1,67},{2,64},{3,65},{4,70},{5,71},{6,68},{7,69},{8,74},{9,... | collective-permute-start | bytes 786440 | tf_op jit(solution)/shard_map/ppermute | solution.py:40
  87.1 14.1 %copy-start.4 = (f32[4,8]{1,0:T(4,128)S(1)}, f32[4,8]{1,0:T(4,128)}, u32[]{:S(2)}) copy-start(f32[4,8]{1,0:T(4,128)} %code.3) | copy-start | bytes 388
  87.1 8.3 %collective-permute-start.22 = (f32[2,16,1024]{2,1,0:T(8,128)S(1)}, f32[2,16,1024]{2,1,0:T(8,128)S(1)}, u32[]{:S(2)}, u32[]{:S(2)}) collective-permute-start(f32[2,16,1024]{2,1,0:T(8,128)S(1)} %get-tuple-element.55.refs_0_), channel_id=1, source_target_pairs={{0,16},{1,17},{2,18},{3,19},{4,20},{5,21},{6,22},{7,23},{8,24},{9,... | collective-permute-start | bytes 393224 | tf_op jit(solution)/shard_map/ppermute | solution.py:40
  89.4 13.9 %collective-permute-start.18 = (f32[4,16,1024]{2,1,0:T(8,128)S(1)}, f32[4,16,1024]{2,1,0:T(8,128)S(1)}, u32[]{:S(2)}, u32[]{:S(2)}) collective-permute-start(f32[4,16,1024]{2,1,0:T(8,128)S(1)} %get-tuple-element.57), channel_id=1, source_target_pairs={{0,2},{1,3},{2,0},{3,1},{4,6},{5,7},{6,4},{7,5},{8,10},{9,11},{10,... | collective-permute-start | bytes 786440 | tf_op jit(solution)/shard_map/ppermute | solution.py:40
  90.7 12.7 %collective-permute-start.20 = (f32[4,16,1024]{2,1,0:T(8,128)S(1)}, f32[4,16,1024]{2,1,0:T(8,128)S(1)}, u32[]{:S(2)}, u32[]{:S(2)}) collective-permute-start(f32[4,16,1024]{2,1,0:T(8,128)S(1)} %get-tuple-element.63), channel_id=1, source_target_pairs={{0,64},{1,65},{2,66},{3,67},{4,68},{5,69},{6,70},{7,71},{8,72},{9,... | collective-permute-start | bytes 786440 | tf_op jit(solution)/shard_map/ppermute | solution.py:40
  91.3 12.1 %collective-permute-start.21 = (f32[4,16,1024]{2,1,0:T(8,128)S(1)}, f32[4,16,1024]{2,1,0:T(8,128)S(1)}, u32[]{:S(2)}, u32[]{:S(2)}) collective-permute-start(f32[4,16,1024]{2,1,0:T(8,128)S(1)} %get-tuple-element.58), channel_id=1, source_target_pairs={{0,66},{1,67},{2,64},{3,65},{4,70},{5,71},{6,68},{7,69},{8,74},{9,... | collective-permute-start | bytes 786440 | tf_op jit(solution)/shard_map/ppermute | solution.py:40
  93.6 6.5 %collective-permute-start.23 = (f32[2,16,1024]{2,1,0:T(8,128)S(1)}, f32[2,16,1024]{2,1,0:T(8,128)S(1)}, u32[]{:S(2)}, u32[]{:S(2)}) collective-permute-start(f32[2,16,1024]{2,1,0:T(8,128)S(1)} %get-tuple-element.65), channel_id=1, source_target_pairs={{0,32},{1,33},{2,34},{3,35},{4,36},{5,37},{6,38},{7,39},{8,40},{9,... | collective-permute-start | bytes 393224 | tf_op jit(solution)/shard_map/ppermute | solution.py:40
  95.5 5.8 %collective-permute-start.24 = (f32[2,16,1024]{2,1,0:T(8,128)S(1)}, f32[2,16,1024]{2,1,0:T(8,128)S(1)}, u32[]{:S(2)}, u32[]{:S(2)}) collective-permute-start(f32[2,16,1024]{2,1,0:T(8,128)S(1)} %get-tuple-element.66), channel_id=1, source_target_pairs={{0,48},{1,49},{2,50},{3,51},{4,52},{5,53},{6,54},{7,55},{8,56},{9,... | collective-permute-start | bytes 393224 | tf_op jit(solution)/shard_map/ppermute | solution.py:40
  100.1 9.3 %collective-permute-start.19 = (f32[4,16,1024]{2,1,0:T(8,128)S(1)}, f32[4,16,1024]{2,1,0:T(8,128)S(1)}, u32[]{:S(2)}, u32[]{:S(2)}) collective-permute-start(f32[4,16,1024]{2,1,0:T(8,128)S(1)} %get-tuple-element.58), channel_id=1, source_target_pairs={{0,2},{1,3},{2,0},{3,1},{4,6},{5,7},{6,4},{7,5},{8,10},{9,11},{10,... | collective-permute-start | bytes 786440 | tf_op jit(solution)/shard_map/ppermute | solution.py:40
  104.0 8.1 %collective-permute-start.25 = (f32[2,16,1024]{2,1,0:T(8,128)S(1)}, f32[2,16,1024]{2,1,0:T(8,128)S(1)}, u32[]{:S(2)}, u32[]{:S(2)}) collective-permute-start(f32[2,16,1024]{2,1,0:T(8,128)S(1)} %get-tuple-element.69), channel_id=1, source_target_pairs={{0,16},{1,17},{2,18},{3,19},{4,20},{5,21},{6,22},{7,23},{8,24},{9,... | collective-permute-start | bytes 393224 | tf_op jit(solution)/shard_map/ppermute | solution.py:40
  105.5 6.5 %collective-permute-start.26 = (f32[2,16,1024]{2,1,0:T(8,128)S(1)}, f32[2,16,1024]{2,1,0:T(8,128)S(1)}, u32[]{:S(2)}, u32[]{:S(2)}) collective-permute-start(f32[2,16,1024]{2,1,0:T(8,128)S(1)} %get-tuple-element.70), channel_id=1, source_target_pairs={{0,32},{1,33},{2,34},{3,35},{4,36},{5,37},{6,38},{7,39},{8,40},{9,... | collective-permute-start | bytes 393224 | tf_op jit(solution)/shard_map/ppermute | solution.py:40
  107.7 5.0 %collective-permute-start.27 = (f32[2,16,1024]{2,1,0:T(8,128)S(1)}, f32[2,16,1024]{2,1,0:T(8,128)S(1)}, u32[]{:S(2)}, u32[]{:S(2)}) collective-permute-start(f32[2,16,1024]{2,1,0:T(8,128)S(1)} %get-tuple-element.71), channel_id=1, source_target_pairs={{0,48},{1,49},{2,50},{3,51},{4,52},{5,53},{6,54},{7,55},{8,56},{9,... | collective-permute-start | bytes 393224 | tf_op jit(solution)/shard_map/ppermute | solution.py:40
  (3 other events, 7.3 us)

commit v6 on v5

--- a/solution.py
+++ b/solution.py
@@ -315,7 +315,34 @@
     )
 
 
-def encode(code, old, grads, c, into=None):
+def encode_here(code, old, grad, c):
+    def body(code, old_0, old_1, grad, total):
+        _, _, _, side, y = position()
+        scales = [[code[j, lax.rem(side + a, 2) * 4 + y] for a in range(2)] for j in range(4)]
+        for row in range(0, 16, 8):
+
+            def one(columns):
+                rows = pl.ds(row, 8)
+                states = []
+                for a, source in enumerate((old_0, old_1)):
+                    was = [source[old[a][1], k, pl.ds(16 * c + row, 8), columns] for k in range(3)]
+                    states.append(advance(*was, grad[a, rows, columns]))
+                for j in range(4):
+                    for k in range(3):
+                        total[j, k, rows, columns] = scales[j][0] * states[0][k] + scales[j][1] * states[1][k]
+
+            by_tiles(1024, 256, one)
+
+    return call(
+        "encode_here",
+        body,
+        [(code, SMEM), (old[0][0], VMEM), (old[1][0], VMEM), (grad, VMEM)],
+        [((4, 3, 16, 1024), F32, VMEM)],
+    )[0]
+
+
+def encode(code, old, grads, c, into=None, begun=None):
+    given = [*grads] if begun is None else [*grads, begun]
     arrays, places = [], [[None] * 4, [None] * 4]
     for a in range(2):
         for s in range(4):
@@ -341,7 +368,9 @@
             def one(columns):
                 rows = pl.ds(row, 8)
                 sums = [[None] * 3 for _ in range(4)]
-                for s in range(4):
+                if begun is not None:
+                    sums = [[ins[4][j, k, rows, columns] for k in range(3)] for j in range(4)]
+                for s in range(0 if begun is None else 1, 4):
                     for a in range(2):
                         was = [state(s, a, k, row, columns) for k in range(3)]
                         states = advance(*was, ins[s][a, rows, columns])
@@ -366,10 +395,10 @@
     return call(
         f"encode_{c}",
         body,
-        [(code, SMEM)] + [(array, VMEM) for array in (*arrays, *grads)] + ([] if into is None else [(into, HBM)]),
+        [(code, SMEM)] + [(array, VMEM) for array in (*arrays, *given)] + ([] if into is None else [(into, HBM)]),
         [((4, 3, 32, 1024), F32, HBM), ((8, 128), F32, VMEM)],
         [pltpu.VMEM((4, 3, 16, 1024), F32), pltpu.SemaphoreType.DMA((8,))],
-        aliases=None if into is None else {1 + len(arrays) + len(grads): 0},
+        aliases=None if into is None else {1 + len(arrays) + len(given): 0},
     )
 
 
@@ -412,7 +441,8 @@
         sums = for_holders(holder, ours, across[c], send(to_beside, BESIDE), send(to_corner, CORNER), done)
         after = (sums[1],)
         grads = [sums[0]] + [send(sums[s], ALONG_Y[s]) for s in (1, 2, 3)]
-        parity, done = encode(code, old, grads, c, parity)
+        begun = encode_here(code, [old[0][0], old[1][0]], sums[0], c) if c else None
+        parity, done = encode(code, old, grads, c, parity, begun)
     across.append(send(to_corner, ACROSS))
 
     new = update(holder, *states, mine, across)

time: 116 us -> 116 us (level)
    pallas_call x17 -> x18, Pallas kernels: 19.8 us -> 20.4 us  [call(): pl.pallas_call(body, out_shape=[jax.ShapeDtypeStruct(shape, kind) for sha...]
  transfers between devices with their start and end apart: 28 -> 28, of which waited for: 9 -> 8; matrix products, arithmetic and copies ran while one was open for 0% -> 0% of each run, Pallas kernels for 13% -> 14%
where the time goes in v6:
time: 116 us; the launch traced here: 115 us
  waiting for transfers between devices  51.6 us (44%)
  starting transfers between devices  41.9 us (36%)
  Pallas kernels  20.4 us (18%)
    ppermute x28, waiting for transfers between devices, send(): return lax.ppermute(array, AXES, pairs)  51.6 us
    ppermute x28, starting transfers between devices, send(): return lax.ppermute(array, AXES, pairs)  41.9 us
    pallas_call x18, Pallas kernels, call(): pl.pallas_call(body, out_shape=[jax.ShapeDtypeStruct(shape, kind) for sha...  20.4 us
  transfers between devices with their start and end apart: 28, of which 8 were waited for; matrix products, arithmetic and copies ran while one was open for 0% of the time, Pallas kernels for 14%

profile of v6, /device:TPU:0, one launch (start us, length us, event | category | flops | bytes accessed | tf_op | source)
XLA Modules:
  0.0 115.4 jit_solution(16392367128264088461)
XLA Ops:
  1.3 1.9 %widen_far.1.far = f32[2,32,8192]{2,1,0:T(8,128)S(1)} custom-call(bf16[16,32,8192]{2,1,0:T(8,128)(2,1)} %bitcast.1, s32[1,16]{1,0:T(1,128)S(1)} %copy-done.5), custom_call_target="tpu_custom_call" | custom-call | tf_op jit(solution)/shard_map/widen_far/pallas_call | solution.py:44
  3.3 3.8 %widen_rest.1 = (f32[6,32,8192]{2,1,0:T(8,128)S(1)}, bf16[8,32,8192]{2,1,0:T(8,128)(2,1)S(1)}) custom-call(bf16[16,32,8192]{2,1,0:T(8,128)(2,1)} %bitcast.2, s32[1,16]{1,0:T(1,128)S(1)} %copy-done.6, f32[2,32,8192]{2,1,0:T(8,128)S(1)} %widen_far.1.far), custom_call_target="tpu_custom_call" | custom-call | tf_op jit(solution)/shard_map/widen_rest/pallas_call | solution.py:44
  8.0 2.0 %collective-permute-start.3 = (f32[2,32,4096]{2,1,0:T(8,128)S(1)}, f32[2,32,4096]{2,1,0:T(8,128)S(1)}, u32[]{:S(2)}, u32[]{:S(2)}) collective-permute-start(f32[2,32,4096]{2,1,0:T(8,128)S(1)} %get-tuple-element.42.refs_0_), channel_id=1, source_target_pairs={{0,4},{1,5},{2,6},{3,7},{4,8},{5,9},{6,10},{7,11},{8,12},{9,13},{1... | collective-permute-start | bytes 3145736 | tf_op jit(solution)/shard_map/ppermute | solution.py:40
  10.0 2.1 %collective-permute-start.4 = (f32[2,32,4096]{2,1,0:T(8,128)S(1)}, f32[2,32,4096]{2,1,0:T(8,128)S(1)}, u32[]{:S(2)}, u32[]{:S(2)}) collective-permute-start(f32[2,32,4096]{2,1,0:T(8,128)S(1)} %get-tuple-element.43), channel_id=1, source_target_pairs={{0,12},{1,13},{2,14},{3,15},{4,0},{5,1},{6,2},{7,3},{8,4},{9,5},{1... | collective-permute-start | bytes 3145736 | tf_op jit(solution)/shard_map/ppermute | solution.py:40
  12.9 1.6 %collective-permute-start.5 = (f32[2,3,32,1024]{3,2,1,0:T(8,128)S(1)}, f32[2,3,32,1024]{3,2,1,0:T(8,128)S(1)}, u32[]{:S(2)}, u32[]{:S(2)}) collective-permute-start(f32[2,3,32,1024]{3,2,1,0:T(8,128)S(1)} %get-tuple-element.44), channel_id=1, source_target_pairs={{0,16},{1,17},{2,18},{3,19},{4,20},{5,21},{6,22},{7,23},{8,24},{9,... | collective-permute-start | bytes 2359304 | tf_op jit(solution)/shard_map/ppermute | solution.py:40
  14.5 1.7 %collective-permute-start.6 = (f32[2,3,32,1024]{3,2,1,0:T(8,128)S(1)}, f32[2,3,32,1024]{3,2,1,0:T(8,128)S(1)}, u32[]{:S(2)}, u32[]{:S(2)}) collective-permute-start(f32[2,3,32,1024]{3,2,1,0:T(8,128)S(1)} %get-tuple-element.45), channel_id=1, source_target_pairs={{0,48},{1,49},{2,50},{3,51},{4,52},{5,53},{6,54},{7,55},{8,56},{9,... | collective-permute-start | bytes 2359304 | tf_op jit(solution)/shard_map/ppermute | solution.py:40
  16.2 1.8 %collective-permute-done.1.refs_0_.rest = f32[6,32,8192]{2,1,0:T(8,128)S(1)} collective-permute-done((f32[6,32,8192]{2,1,0:T(8,128)S(1)}, f32[6,32,8192]{2,1,0:T(8,128)S(1)}, u32[]{:S(2)}, u32[]{:S(2)}) %collective-permute-start.1) | collective-permute-done | bytes 6291488 | tf_op jit(solution)/shard_map/ppermute | solution.py:40
  18.6 1.7 %collective-permute-start.7 = (f32[1,3,32,1024]{3,2,1,0:T(8,128)S(1)}, f32[1,3,32,1024]{3,2,1,0:T(8,128)S(1)}, u32[]{:S(2)}, u32[]{:S(2)}) collective-permute-start(f32[1,3,32,1024]{3,2,1,0:T(8,128)S(1)} %get-tuple-element.46), channel_id=1, source_target_pairs={{0,64},{1,65},{2,66},{3,67},{4,68},{5,69},{6,70},{7,71},{8,72},{9,... | collective-permute-start | bytes 1179656 | tf_op jit(solution)/shard_map/ppermute | solution.py:40
  20.2 13.4 %collective-permute-done.5.refs_0_.refs_1_ = f32[2,3,32,1024]{3,2,1,0:T(8,128)S(1)} collective-permute-done((f32[2,3,32,1024]{3,2,1,0:T(8,128)S(1)}, f32[2,3,32,1024]{3,2,1,0:T(8,128)S(1)}, u32[]{:S(2)}, u32[]{:S(2)}) %collective-permute-start.5) | collective-permute-done | bytes 786464 | tf_op jit(solution)/shard_map/ppermute | solution.py:40
  34.4 3.0 %collective-permute-start.10 = (f32[2,3,32,1024]{3,2,1,0:T(8,128)S(1)}, f32[2,3,32,1024]{3,2,1,0:T(8,128)S(1)}, u32[]{:S(2)}, u32[]{:S(2)}) collective-permute-start(f32[2,3,32,1024]{3,2,1,0:T(8,128)S(1)} %old_two.1.refs_0_), channel_id=1, source_target_pairs={{0,32},{1,33},{2,34},{3,35},{4,36},{5,37},{6,38},{7,39},{8,40},{9,... | collective-permute-start | bytes 2359304 | tf_op jit(solution)/shard_map/ppermute | solution.py:40
  37.4 1.5 %collective-permute-start.11 = (f32[2,3,32,1024]{3,2,1,0:T(8,128)S(1)}, f32[2,3,32,1024]{3,2,1,0:T(8,128)S(1)}, u32[]{:S(2)}, u32[]{:S(2)}) collective-permute-start(f32[2,3,32,1024]{3,2,1,0:T(8,128)S(1)} %other_side.2.refs_0_), channel_id=1, source_target_pairs={{0,64},{1,65},{2,66},{3,67},{4,68},{5,69},{6,70},{7,71},{8,72},{9,... | collective-permute-start | bytes 2359304 | tf_op jit(solution)/shard_map/ppermute | solution.py:40
  39.3 3.2 %collective-permute-start.9 = (f32[2,2,16,4096]{3,2,1,0:T(8,128)S(1)}, f32[2,2,16,4096]{3,2,1,0:T(8,128)S(1)}, u32[]{:S(2)}, u32[]{:S(2)}) collective-permute-start(f32[2,2,16,4096]{3,2,1,0:T(8,128)S(1)} %get-tuple-element.48), channel_id=1, source_target_pairs={{0,12},{1,13},{2,14},{3,15},{4,0},{5,1},{6,2},{7,3},{8,4},{9,5},{1... | collective-permute-start | bytes 3145736 | tf_op jit(solution)/shard_map/ppermute | solution.py:40
  42.6 2.7 %collective-permute-start.2 = (s32[1,8]{1,0:T(1,128)S(1)}, s32[1,8]{1,0:T(1,128)S(1)}, u32[]{:S(2)}, u32[]{:S(2)}) collective-permute-start(s32[1,8]{1,0:T(1,128)S(1)} %copy-done.3), channel_id=1, source_target_pairs={{0,2},{1,3},{2,0},{3,1},{4,6},{5,7},{6,4},{7,5},{8,10},{9,11},{10,... | collective-permute-start | bytes 104 | tf_op jit(solution)/shard_map/ppermute | solution.py:40
  45.3 12.3 %collective-permute-done.2.refs_3_.other_held = s32[1,8]{1,0:T(1,128)S(1)} collective-permute-done((s32[1,8]{1,0:T(1,128)S(1)}, s32[1,8]{1,0:T(1,128)S(1)}, u32[]{:S(2)}, u32[]{:S(2)}) %collective-permute-start.2) | collective-permute-done | bytes 64 | tf_op jit(solution)/shard_map/ppermute | solution.py:40
  58.6 3.2 %collective-permute-start.13 = (f32[2,2,16,4096]{3,2,1,0:T(8,128)S(1)}, f32[2,2,16,4096]{3,2,1,0:T(8,128)S(1)}, u32[]{:S(2)}, u32[]{:S(2)}) collective-permute-start(f32[2,2,16,4096]{3,2,1,0:T(8,128)S(1)} %get-tuple-element.51), channel_id=1, source_target_pairs={{0,12},{1,13},{2,14},{3,15},{4,0},{5,1},{6,2},{7,3},{8,4},{9,5},{1... | collective-permute-start | bytes 3145736 | tf_op jit(solution)/shard_map/ppermute | solution.py:40
  62.1 4.5 %collective-permute-done.8.below = f32[2,2,16,4096]{3,2,1,0:T(8,128)S(1)} collective-permute-done((f32[2,2,16,4096]{3,2,1,0:T(8,128)S(1)}, f32[2,2,16,4096]{3,2,1,0:T(8,128)S(1)}, u32[]{:S(2)}, u32[]{:S(2)}) %collective-permute-start.8) | collective-permute-done | bytes 1048608 | tf_op jit(solution)/shard_map/ppermute | solution.py:40
  67.6 2.8 %collective-permute-start.14 = (f32[8,16,1024]{2,1,0:T(8,128)S(1)}, f32[8,16,1024]{2,1,0:T(8,128)S(1)}, u32[]{:S(2)}, u32[]{:S(2)}) collective-permute-start(f32[8,16,1024]{2,1,0:T(8,128)S(1)} %get-tuple-element.52), channel_id=1, source_target_pairs={{0,2},{1,3},{2,0},{3,1},{4,6},{5,7},{6,4},{7,5},{8,10},{9,11},{10,... | collective-permute-start | bytes 1572872 | tf_op jit(solution)/shard_map/ppermute | solution.py:40
  70.6 3.0 %collective-permute-done.17.after.refs_6_ = f32[1,3,32,1024]{3,2,1,0:T(8,128)S(1)} collective-permute-done((f32[1,3,32,1024]{3,2,1,0:T(8,128)S(1)}, f32[1,3,32,1024]{3,2,1,0:T(8,128)S(1)}, u32[]{:S(2)}, u32[]{:S(2)}) %collective-permute-start.17) | collective-permute-done | bytes 393248 | tf_op jit(solution)/shard_map/ppermute | solution.py:40
  74.1 12.4 %collective-permute-done.15.beside = f32[4,16,1024]{2,1,0:T(8,128)S(1)} collective-permute-done((f32[4,16,1024]{2,1,0:T(8,128)S(1)}, f32[4,16,1024]{2,1,0:T(8,128)S(1)}, u32[]{:S(2)}, u32[]{:S(2)}) %collective-permute-start.15) | collective-permute-done | bytes 262176 | tf_op jit(solution)/shard_map/ppermute | solution.py:40
  87.1 1.4 %collective-permute-start.22 = (f32[2,16,1024]{2,1,0:T(8,128)S(1)}, f32[2,16,1024]{2,1,0:T(8,128)S(1)}, u32[]{:S(2)}, u32[]{:S(2)}) collective-permute-start(f32[2,16,1024]{2,1,0:T(8,128)S(1)} %get-tuple-element.55.refs_0_), channel_id=1, source_target_pairs={{0,16},{1,17},{2,18},{3,19},{4,20},{5,21},{6,22},{7,23},{8,24},{9,... | collective-permute-start | bytes 393224 | tf_op jit(solution)/shard_map/ppermute | solution.py:40
  88.5 0.9 gathered_z_1.1
  89.5 1.3 %collective-permute-start.18 = (f32[4,16,1024]{2,1,0:T(8,128)S(1)}, f32[4,16,1024]{2,1,0:T(8,128)S(1)}, u32[]{:S(2)}, u32[]{:S(2)}) collective-permute-start(f32[4,16,1024]{2,1,0:T(8,128)S(1)} %get-tuple-element.57), channel_id=1, source_target_pairs={{0,2},{1,3},{2,0},{3,1},{4,6},{5,7},{6,4},{7,5},{8,10},{9,11},{10,... | collective-permute-start | bytes 786440 | tf_op jit(solution)/shard_map/ppermute | solution.py:40
  91.3 2.3 %collective-permute-start.21 = (f32[4,16,1024]{2,1,0:T(8,128)S(1)}, f32[4,16,1024]{2,1,0:T(8,128)S(1)}, u32[]{:S(2)}, u32[]{:S(2)}) collective-permute-start(f32[4,16,1024]{2,1,0:T(8,128)S(1)} %get-tuple-element.58), channel_id=1, source_target_pairs={{0,66},{1,67},{2,64},{3,65},{4,70},{5,71},{6,68},{7,69},{8,74},{9,... | collective-permute-start | bytes 786440 | tf_op jit(solution)/shard_map/ppermute | solution.py:40
  93.6 1.9 %collective-permute-start.23 = (f32[2,16,1024]{2,1,0:T(8,128)S(1)}, f32[2,16,1024]{2,1,0:T(8,128)S(1)}, u32[]{:S(2)}, u32[]{:S(2)}) collective-permute-start(f32[2,16,1024]{2,1,0:T(8,128)S(1)} %get-tuple-element.65), channel_id=1, source_target_pairs={{0,32},{1,33},{2,34},{3,35},{4,36},{5,37},{6,38},{7,39},{8,40},{9,... | collective-permute-start | bytes 393224 | tf_op jit(solution)/shard_map/ppermute | solution.py:40
  96.4 3.7 %collective-permute-done.23.refs_9_ = f32[2,16,1024]{2,1,0:T(8,128)S(1)} collective-permute-done((f32[2,16,1024]{2,1,0:T(8,128)S(1)}, f32[2,16,1024]{2,1,0:T(8,128)S(1)}, u32[]{:S(2)}, u32[]{:S(2)}) %collective-permute-start.23) | collective-permute-done | bytes 131104 | tf_op jit(solution)/shard_map/ppermute | solution.py:40
  100.1 1.2 %collective-permute-start.19 = (f32[4,16,1024]{2,1,0:T(8,128)S(1)}, f32[4,16,1024]{2,1,0:T(8,128)S(1)}, u32[]{:S(2)}, u32[]{:S(2)}) collective-permute-start(f32[4,16,1024]{2,1,0:T(8,128)S(1)} %get-tuple-element.58), channel_id=1, source_target_pairs={{0,2},{1,3},{2,0},{3,1},{4,6},{5,7},{6,4},{7,5},{8,10},{9,11},{10,... | collective-permute-start | bytes 786440 | tf_op jit(solution)/shard_map/ppermute | solution.py:40
  101.3 2.1 %encode_0.1 = (f32[4,3,32,1024]{3,2,1,0:T(8,128)}, f32[8,128]{1,0:T(8,128)S(1)}) custom-call(f32[4,8]{1,0:T(4,128)S(1)} %copy-done.4, f32[1,3,32,1024]{3,2,1,0:T(8,128)S(1)} %get-tuple-element.62.refs_0_.old_0, f32[2,3,32,1024]{3,2,1,0:T(8,128)S(1)} %collective-permute-done.5.refs_0_.refs_1_, f32[2,3,32,1024]{3,2,1,0:T(8,128)S(1)} %collective-permute-done.10.refs_0_.refs_2_, ...), custom_call_target="tpu_custom_call" | custom-call | tf_op jit(solution)/shard_map/encode_0/pallas_call | solution.py:44
  104.0 1.6 %collective-permute-start.25 = (f32[2,16,1024]{2,1,0:T(8,128)S(1)}, f32[2,16,1024]{2,1,0:T(8,128)S(1)}, u32[]{:S(2)}, u32[]{:S(2)}) collective-permute-start(f32[2,16,1024]{2,1,0:T(8,128)S(1)} %get-tuple-element.69), channel_id=1, source_target_pairs={{0,16},{1,17},{2,18},{3,19},{4,20},{5,21},{6,22},{7,23},{8,24},{9,... | collective-permute-start | bytes 393224 | tf_op jit(solution)/shard_map/ppermute | solution.py:40
  105.6 2.1 %collective-permute-start.26 = (f32[2,16,1024]{2,1,0:T(8,128)S(1)}, f32[2,16,1024]{2,1,0:T(8,128)S(1)}, u32[]{:S(2)}, u32[]{:S(2)}) collective-permute-start(f32[2,16,1024]{2,1,0:T(8,128)S(1)} %get-tuple-element.70), channel_id=1, source_target_pairs={{0,32},{1,33},{2,34},{3,35},{4,36},{5,37},{6,38},{7,39},{8,40},{9,... | collective-permute-start | bytes 393224 | tf_op jit(solution)/shard_map/ppermute | solution.py:40
  107.7 1.7 %collective-permute-start.27 = (f32[2,16,1024]{2,1,0:T(8,128)S(1)}, f32[2,16,1024]{2,1,0:T(8,128)S(1)}, u32[]{:S(2)}, u32[]{:S(2)}) collective-permute-start(f32[2,16,1024]{2,1,0:T(8,128)S(1)} %get-tuple-element.71), channel_id=1, source_target_pairs={{0,48},{1,49},{2,50},{3,51},{4,52},{5,53},{6,54},{7,55},{8,56},{9,... | collective-permute-start | bytes 393224 | tf_op jit(solution)/shard_map/ppermute | solution.py:40
  109.4 2.7 %update.1 = (f32[1,32,8192]{2,1,0:T(8,128)}, f32[1,32,8192]{2,1,0:T(8,128)}, f32[1,32,8192]{2,1,0:T(8,128)}) custom-call(s32[1,8]{1,0:T(1,128)S(1)} %copy-done.3, f32[1,32,8192]{2,1,0:T(8,128)S(1)} %copy-done, f32[1,32,8192]{2,1,0:T(8,128)S(1)} %copy-done.1, f32[1,32,8192]{2,1,0:T(8,128)S(1)} %copy-done.2, f32[16,8192]{1,0:T(8,128)S(1)} %get-tuple-element.49.mine.mine_0, ...), custom_call_target="tpu_custom_call" | custom-call | tf_op jit(solution)/shard_map/update/pallas_call | solution.py:44
  112.9 2.5 %encode_1.1 = (f32[4,3,32,1024]{3,2,1,0:T(8,128)}, f32[8,128]{1,0:T(8,128)}) custom-call(f32[4,8]{1,0:T(4,128)S(1)} %copy-done.4, f32[1,3,32,1024]{3,2,1,0:T(8,128)S(1)} %get-tuple-element.62.refs_0_.old_0, f32[2,3,32,1024]{3,2,1,0:T(8,128)S(1)} %collective-permute-done.5.refs_0_.refs_1_, ...), custom_call_target="tpu_custom_call", output_to_operand_aliasing={{0}: (13, {})} | custom-call | tf_op jit(solution)/shard_map/encode_1/pallas_call | solution.py:44
  (56 shorter events, 10.7 us)
Async XLA Ops:
  3.2 4.2 %collective-permute-start = (f32[2,32,8192]{2,1,0:T(8,128)S(1)}, f32[2,32,8192]{2,1,0:T(8,128)S(1)}, u32[]{:S(2)}, u32[]{:S(2)}) collective-permute-start(f32[2,32,8192]{2,1,0:T(8,128)S(1)} %widen_far.1.far), channel_id=1, source_target_pairs={{0,1},{1,0},{2,3},{3,2},{4,5},{5,4},{6,7},{7,6},{8,9},{9,8},{10,11... | collective-permute-start | bytes 6291464 | tf_op jit(solution)/shard_map/ppermute | solution.py:40
  7.4 4.7 %copy-start.1 = (f32[1,32,8192]{2,1,0:T(8,128)S(1)}, f32[1,32,8192]{2,1,0:T(8,128)}, u32[]{:S(2)}) copy-start(f32[1,32,8192]{2,1,0:T(8,128)} %first.7) | copy-start | bytes 3145732
  7.4 4.7 %copy-start.2 = (f32[1,32,8192]{2,1,0:T(8,128)S(1)}, f32[1,32,8192]{2,1,0:T(8,128)}, u32[]{:S(2)}) copy-start(f32[1,32,8192]{2,1,0:T(8,128)} %second.7) | copy-start | bytes 3145732
  7.4 4.7 %copy-start.3 = (s32[1,8]{1,0:T(1,128)S(1)}, s32[1,8]{1,0:T(1,128)}, u32[]{:S(2)}) copy-start(s32[1,8]{1,0:T(1,128)} %holder.11) | copy-start | bytes 100
  7.7 10.2 %collective-permute-start.1 = (f32[6,32,8192]{2,1,0:T(8,128)S(1)}, f32[6,32,8192]{2,1,0:T(8,128)S(1)}, u32[]{:S(2)}, u32[]{:S(2)}) collective-permute-start(f32[6,32,8192]{2,1,0:T(8,128)S(1)} %get-tuple-element.41), channel_id=1, source_target_pairs={{0,1},{1,0},{2,3},{3,2},{4,5},{5,4},{6,7},{7,6},{8,9},{9,8},{10,11... | collective-permute-start | bytes 18874376 | tf_op jit(solution)/shard_map/ppermute | solution.py:40
  8.0 30.9 %collective-permute-start.3 = (f32[2,32,4096]{2,1,0:T(8,128)S(1)}, f32[2,32,4096]{2,1,0:T(8,128)S(1)}, u32[]{:S(2)}, u32[]{:S(2)}) collective-permute-start(f32[2,32,4096]{2,1,0:T(8,128)S(1)} %get-tuple-element.42.refs_0_), channel_id=1, source_target_pairs={{0,4},{1,5},{2,6},{3,7},{4,8},{5,9},{6,10},{7,11},{8,12},{9,13},{1... | collective-permute-start | bytes 3145736 | tf_op jit(solution)/shard_map/ppermute | solution.py:40
  10.0 28.9 %collective-permute-start.4 = (f32[2,32,4096]{2,1,0:T(8,128)S(1)}, f32[2,32,4096]{2,1,0:T(8,128)S(1)}, u32[]{:S(2)}, u32[]{:S(2)}) collective-permute-start(f32[2,32,4096]{2,1,0:T(8,128)S(1)} %get-tuple-element.43), channel_id=1, source_target_pairs={{0,12},{1,13},{2,14},{3,15},{4,0},{5,1},{6,2},{7,3},{8,4},{9,5},{1... | collective-permute-start | bytes 3145736 | tf_op jit(solution)/shard_map/ppermute | solution.py:40
  12.9 20.8 %collective-permute-start.5 = (f32[2,3,32,1024]{3,2,1,0:T(8,128)S(1)}, f32[2,3,32,1024]{3,2,1,0:T(8,128)S(1)}, u32[]{:S(2)}, u32[]{:S(2)}) collective-permute-start(f32[2,3,32,1024]{3,2,1,0:T(8,128)S(1)} %get-tuple-element.44), channel_id=1, source_target_pairs={{0,16},{1,17},{2,18},{3,19},{4,20},{5,21},{6,22},{7,23},{8,24},{9,... | collective-permute-start | bytes 2359304 | tf_op jit(solution)/shard_map/ppermute | solution.py:40
  14.5 19.2 %collective-permute-start.6 = (f32[2,3,32,1024]{3,2,1,0:T(8,128)S(1)}, f32[2,3,32,1024]{3,2,1,0:T(8,128)S(1)}, u32[]{:S(2)}, u32[]{:S(2)}) collective-permute-start(f32[2,3,32,1024]{3,2,1,0:T(8,128)S(1)} %get-tuple-element.45), channel_id=1, source_target_pairs={{0,48},{1,49},{2,50},{3,51},{4,52},{5,53},{6,54},{7,55},{8,56},{9,... | collective-permute-start | bytes 2359304 | tf_op jit(solution)/shard_map/ppermute | solution.py:40
  18.6 15.1 %collective-permute-start.7 = (f32[1,3,32,1024]{3,2,1,0:T(8,128)S(1)}, f32[1,3,32,1024]{3,2,1,0:T(8,128)S(1)}, u32[]{:S(2)}, u32[]{:S(2)}) collective-permute-start(f32[1,3,32,1024]{3,2,1,0:T(8,128)S(1)} %get-tuple-element.46), channel_id=1, source_target_pairs={{0,64},{1,65},{2,66},{3,67},{4,68},{5,69},{6,70},{7,71},{8,72},{9,... | collective-permute-start | bytes 1179656 | tf_op jit(solution)/shard_map/ppermute | solution.py:40
  34.4 23.2 %collective-permute-start.10 = (f32[2,3,32,1024]{3,2,1,0:T(8,128)S(1)}, f32[2,3,32,1024]{3,2,1,0:T(8,128)S(1)}, u32[]{:S(2)}, u32[]{:S(2)}) collective-permute-start(f32[2,3,32,1024]{3,2,1,0:T(8,128)S(1)} %old_two.1.refs_0_), channel_id=1, source_target_pairs={{0,32},{1,33},{2,34},{3,35},{4,36},{5,37},{6,38},{7,39},{8,40},{9,... | collective-permute-start | bytes 2359304 | tf_op jit(solution)/shard_map/ppermute | solution.py:40
  37.4 20.2 %collective-permute-start.11 = (f32[2,3,32,1024]{3,2,1,0:T(8,128)S(1)}, f32[2,3,32,1024]{3,2,1,0:T(8,128)S(1)}, u32[]{:S(2)}, u32[]{:S(2)}) collective-permute-start(f32[2,3,32,1024]{3,2,1,0:T(8,128)S(1)} %other_side.2.refs_0_), channel_id=1, source_target_pairs={{0,64},{1,65},{2,66},{3,67},{4,68},{5,69},{6,70},{7,71},{8,72},{9,... | collective-permute-start | bytes 2359304 | tf_op jit(solution)/shard_map/ppermute | solution.py:40
  39.2 27.4 %collective-permute-start.8 = (f32[2,2,16,4096]{3,2,1,0:T(8,128)S(1)}, f32[2,2,16,4096]{3,2,1,0:T(8,128)S(1)}, u32[]{:S(2)}, u32[]{:S(2)}) collective-permute-start(f32[2,2,16,4096]{3,2,1,0:T(8,128)S(1)} %get-tuple-element.47.refs_2_), channel_id=1, source_target_pairs={{0,4},{1,5},{2,6},{3,7},{4,8},{5,9},{6,10},{7,11},{8,12},{9,13},{1... | collective-permute-start | bytes 3145736 | tf_op jit(solution)/shard_map/ppermute | solution.py:40
  39.3 27.3 %collective-permute-start.9 = (f32[2,2,16,4096]{3,2,1,0:T(8,128)S(1)}, f32[2,2,16,4096]{3,2,1,0:T(8,128)S(1)}, u32[]{:S(2)}, u32[]{:S(2)}) collective-permute-start(f32[2,2,16,4096]{3,2,1,0:T(8,128)S(1)} %get-tuple-element.48), channel_id=1, source_target_pairs={{0,12},{1,13},{2,14},{3,15},{4,0},{5,1},{6,2},{7,3},{8,4},{9,5},{1... | collective-permute-start | bytes 3145736 | tf_op jit(solution)/shard_map/ppermute | solution.py:40
  42.6 15.0 %collective-permute-start.2 = (s32[1,8]{1,0:T(1,128)S(1)}, s32[1,8]{1,0:T(1,128)S(1)}, u32[]{:S(2)}, u32[]{:S(2)}) collective-permute-start(s32[1,8]{1,0:T(1,128)S(1)} %copy-done.3), channel_id=1, source_target_pairs={{0,2},{1,3},{2,0},{3,1},{4,6},{5,7},{6,4},{7,5},{8,10},{9,11},{10,... | collective-permute-start | bytes 104 | tf_op jit(solution)/shard_map/ppermute | solution.py:40
  58.5 30.0 %collective-permute-start.12 = (f32[2,2,16,4096]{3,2,1,0:T(8,128)S(1)}, f32[2,2,16,4096]{3,2,1,0:T(8,128)S(1)}, u32[]{:S(2)}, u32[]{:S(2)}) collective-permute-start(f32[2,2,16,4096]{3,2,1,0:T(8,128)S(1)} %get-tuple-element.50), channel_id=1, source_target_pairs={{0,4},{1,5},{2,6},{3,7},{4,8},{5,9},{6,10},{7,11},{8,12},{9,13},{1... | collective-permute-start | bytes 3145736 | tf_op jit(solution)/shard_map/ppermute | solution.py:40
  58.6 29.9 %collective-permute-start.13 = (f32[2,2,16,4096]{3,2,1,0:T(8,128)S(1)}, f32[2,2,16,4096]{3,2,1,0:T(8,128)S(1)}, u32[]{:S(2)}, u32[]{:S(2)}) collective-permute-start(f32[2,2,16,4096]{3,2,1,0:T(8,128)S(1)} %get-tuple-element.51), channel_id=1, source_target_pairs={{0,12},{1,13},{2,14},{3,15},{4,0},{5,1},{6,2},{7,3},{8,4},{9,5},{1... | collective-permute-start | bytes 3145736 | tf_op jit(solution)/shard_map/ppermute | solution.py:40
  61.9 11.8 %collective-permute-start.17 = (f32[1,3,32,1024]{3,2,1,0:T(8,128)S(1)}, f32[1,3,32,1024]{3,2,1,0:T(8,128)S(1)}, u32[]{:S(2)}, u32[]{:S(2)}) collective-permute-start(f32[1,3,32,1024]{3,2,1,0:T(8,128)S(1)} %other_side.3.refs_0_), channel_id=1, source_target_pairs={{0,64},{1,65},{2,66},{3,67},{4,68},{5,69},{6,70},{7,71},{8,72},{9,... | collective-permute-start | bytes 1179656 | tf_op jit(solution)/shard_map/ppermute | solution.py:40
  67.6 19.0 %collective-permute-start.14 = (f32[8,16,1024]{2,1,0:T(8,128)S(1)}, f32[8,16,1024]{2,1,0:T(8,128)S(1)}, u32[]{:S(2)}, u32[]{:S(2)}) collective-permute-start(f32[8,16,1024]{2,1,0:T(8,128)S(1)} %get-tuple-element.52), channel_id=1, source_target_pairs={{0,2},{1,3},{2,0},{3,1},{4,6},{5,7},{6,4},{7,5},{8,10},{9,11},{10,... | collective-permute-start | bytes 1572872 | tf_op jit(solution)/shard_map/ppermute | solution.py:40
  70.4 16.1 %collective-permute-start.15 = (f32[4,16,1024]{2,1,0:T(8,128)S(1)}, f32[4,16,1024]{2,1,0:T(8,128)S(1)}, u32[]{:S(2)}, u32[]{:S(2)}) collective-permute-start(f32[4,16,1024]{2,1,0:T(8,128)S(1)} %get-tuple-element.53), channel_id=1, source_target_pairs={{0,64},{1,65},{2,66},{3,67},{4,68},{5,69},{6,70},{7,71},{8,72},{9,... | collective-permute-start | bytes 786440 | tf_op jit(solution)/shard_map/ppermute | solution.py:40
  73.6 12.9 %collective-permute-start.16 = (f32[4,16,1024]{2,1,0:T(8,128)S(1)}, f32[4,16,1024]{2,1,0:T(8,128)S(1)}, u32[]{:S(2)}, u32[]{:S(2)}) collective-permute-start(f32[4,16,1024]{2,1,0:T(8,128)S(1)} %get-tuple-element.54), channel_id=1, source_target_pairs={{0,66},{1,67},{2,64},{3,65},{4,70},{5,71},{6,68},{7,69},{8,74},{9,... | collective-permute-start | bytes 786440 | tf_op jit(solution)/shard_map/ppermute | solution.py:40
  87.1 14.1 %copy-start.4 = (f32[4,8]{1,0:T(4,128)S(1)}, f32[4,8]{1,0:T(4,128)}, u32[]{:S(2)}) copy-start(f32[4,8]{1,0:T(4,128)} %code.5) | copy-start | bytes 388
  87.1 8.3 %collective-permute-start.22 = (f32[2,16,1024]{2,1,0:T(8,128)S(1)}, f32[2,16,1024]{2,1,0:T(8,128)S(1)}, u32[]{:S(2)}, u32[]{:S(2)}) collective-permute-start(f32[2,16,1024]{2,1,0:T(8,128)S(1)} %get-tuple-element.55.refs_0_), channel_id=1, source_target_pairs={{0,16},{1,17},{2,18},{3,19},{4,20},{5,21},{6,22},{7,23},{8,24},{9,... | collective-permute-start | bytes 393224 | tf_op jit(solution)/shard_map/ppermute | solution.py:40
  89.5 13.9 %collective-permute-start.18 = (f32[4,16,1024]{2,1,0:T(8,128)S(1)}, f32[4,16,1024]{2,1,0:T(8,128)S(1)}, u32[]{:S(2)}, u32[]{:S(2)}) collective-permute-start(f32[4,16,1024]{2,1,0:T(8,128)S(1)} %get-tuple-element.57), channel_id=1, source_target_pairs={{0,2},{1,3},{2,0},{3,1},{4,6},{5,7},{6,4},{7,5},{8,10},{9,11},{10,... | collective-permute-start | bytes 786440 | tf_op jit(solution)/shard_map/ppermute | solution.py:40
  90.7 12.7 %collective-permute-start.20 = (f32[4,16,1024]{2,1,0:T(8,128)S(1)}, f32[4,16,1024]{2,1,0:T(8,128)S(1)}, u32[]{:S(2)}, u32[]{:S(2)}) collective-permute-start(f32[4,16,1024]{2,1,0:T(8,128)S(1)} %get-tuple-element.63), channel_id=1, source_target_pairs={{0,64},{1,65},{2,66},{3,67},{4,68},{5,69},{6,70},{7,71},{8,72},{9,... | collective-permute-start | bytes 786440 | tf_op jit(solution)/shard_map/ppermute | solution.py:40
  91.3 12.1 %collective-permute-start.21 = (f32[4,16,1024]{2,1,0:T(8,128)S(1)}, f32[4,16,1024]{2,1,0:T(8,128)S(1)}, u32[]{:S(2)}, u32[]{:S(2)}) collective-permute-start(f32[4,16,1024]{2,1,0:T(8,128)S(1)} %get-tuple-element.58), channel_id=1, source_target_pairs={{0,66},{1,67},{2,64},{3,65},{4,70},{5,71},{6,68},{7,69},{8,74},{9,... | collective-permute-start | bytes 786440 | tf_op jit(solution)/shard_map/ppermute | solution.py:40
  93.6 6.5 %collective-permute-start.23 = (f32[2,16,1024]{2,1,0:T(8,128)S(1)}, f32[2,16,1024]{2,1,0:T(8,128)S(1)}, u32[]{:S(2)}, u32[]{:S(2)}) collective-permute-start(f32[2,16,1024]{2,1,0:T(8,128)S(1)} %get-tuple-element.65), channel_id=1, source_target_pairs={{0,32},{1,33},{2,34},{3,35},{4,36},{5,37},{6,38},{7,39},{8,40},{9,... | collective-permute-start | bytes 393224 | tf_op jit(solution)/shard_map/ppermute | solution.py:40
  95.5 5.8 %collective-permute-start.24 = (f32[2,16,1024]{2,1,0:T(8,128)S(1)}, f32[2,16,1024]{2,1,0:T(8,128)S(1)}, u32[]{:S(2)}, u32[]{:S(2)}) collective-permute-start(f32[2,16,1024]{2,1,0:T(8,128)S(1)} %get-tuple-element.66), channel_id=1, source_target_pairs={{0,48},{1,49},{2,50},{3,51},{4,52},{5,53},{6,54},{7,55},{8,56},{9,... | collective-permute-start | bytes 393224 | tf_op jit(solution)/shard_map/ppermute | solution.py:40
  100.1 9.3 %collective-permute-start.19 = (f32[4,16,1024]{2,1,0:T(8,128)S(1)}, f32[4,16,1024]{2,1,0:T(8,128)S(1)}, u32[]{:S(2)}, u32[]{:S(2)}) collective-permute-start(f32[4,16,1024]{2,1,0:T(8,128)S(1)} %get-tuple-element.58), channel_id=1, source_target_pairs={{0,2},{1,3},{2,0},{3,1},{4,6},{5,7},{6,4},{7,5},{8,10},{9,11},{10,... | collective-permute-start | bytes 786440 | tf_op jit(solution)/shard_map/ppermute | solution.py:40
  104.0 8.9 %collective-permute-start.25 = (f32[2,16,1024]{2,1,0:T(8,128)S(1)}, f32[2,16,1024]{2,1,0:T(8,128)S(1)}, u32[]{:S(2)}, u32[]{:S(2)}) collective-permute-start(f32[2,16,1024]{2,1,0:T(8,128)S(1)} %get-tuple-element.69), channel_id=1, source_target_pairs={{0,16},{1,17},{2,18},{3,19},{4,20},{5,21},{6,22},{7,23},{8,24},{9,... | collective-permute-start | bytes 393224 | tf_op jit(solution)/shard_map/ppermute | solution.py:40
  105.6 7.3 %collective-permute-start.26 = (f32[2,16,1024]{2,1,0:T(8,128)S(1)}, f32[2,16,1024]{2,1,0:T(8,128)S(1)}, u32[]{:S(2)}, u32[]{:S(2)}) collective-permute-start(f32[2,16,1024]{2,1,0:T(8,128)S(1)} %get-tuple-element.70), channel_id=1, source_target_pairs={{0,32},{1,33},{2,34},{3,35},{4,36},{5,37},{6,38},{7,39},{8,40},{9,... | collective-permute-start | bytes 393224 | tf_op jit(solution)/shard_map/ppermute | solution.py:40
  107.7 5.2 %collective-permute-start.27 = (f32[2,16,1024]{2,1,0:T(8,128)S(1)}, f32[2,16,1024]{2,1,0:T(8,128)S(1)}, u32[]{:S(2)}, u32[]{:S(2)}) collective-permute-start(f32[2,16,1024]{2,1,0:T(8,128)S(1)} %get-tuple-element.71), channel_id=1, source_target_pairs={{0,48},{1,49},{2,50},{3,51},{4,52},{5,53},{6,54},{7,55},{8,56},{9,... | collective-permute-start | bytes 393224 | tf_op jit(solution)/shard_map/ppermute | solution.py:40
  (3 other events, 7.3 us)
